TPU v7x, 512 devices: a whole 4x8x8 slice. The times are simulated.
512 devices in a mesh: tr: 16 (over z, core), tc: 32 (over x, y).
Axes of the slice: x: 4, y: 8, z: 8, core: 2. Of those that a mesh axis runs over, the one named last changes fastest.
Arguments:
- cov_tiles: float32 [16384, 16384], P('tr', 'tc'), may hold values from -3 to 9, as said below
- block_order: int32 [32], replicated, may hold values from 0 to 31, as said below
- stations: int32 [1, 256], P(None, 'tc'), may hold values from 0 to 31
- obs_values: float32 [1, 256, 512], P(None, 'tc'), may hold values from -0.25 to 0.25
- obs_error: float32 [1, 256], P(None, 'tc'), may hold values from 0.5 to 4
Outputs:
- cov_updated: float32 [16384, 16384], P('tr', 'tc')
Inputs may be any that keep to these rules, and one draw needn't show every extreme that they name: `block_order`: a permutation of 0 to 31. `cov_tiles`: the matrix that the live tiles describe, completed by symmetry, is positive definite with diagonal tiles symmetric; tiles that are not live are zero.
All inputs are finite; a program needn't handle non-finite values.
Results may differ from a plain program's by a relative error of at most 0.0001.
Values sent between devices are 32-bit elements; how exact they have to be, the bound alone decides.
No kernel may reach another device: no remote copies, remote signals or barrier semaphores. Data moves between devices by JAX's collectives and lax.ppermute only.
A program may use at most 64 MiB of HBM per device.

v0:
```python
import jax
import jax.numpy as jnp
from jax import lax
from jax.sharding import Mesh
from jax.sharding import PartitionSpec as P

TR = ("tr_0", "tr_1")


precise = lax.Precision.HIGHEST


def laid_out(pieces, dim):
    pieces = jnp.moveaxis(pieces, 0, dim)
    lengths = pieces.shape
    return pieces.reshape(*lengths[:dim], lengths[dim] * lengths[dim + 1], *lengths[dim + 2 :])


def from_everyone(array, axis):
    length = lax.axis_size(axis)
    return lax.all_to_all(
        jnp.broadcast_to(array[None], (length, *array.shape)), axis, 0, 0, tiled=True
    )


def collect(array, axis, dim):
    return laid_out(from_everyone(array, axis), dim)


def in_blocks(array, dim, length):
    before, after = (array.shape[:dim], array.shape[dim + 1 :])
    return jnp.moveaxis(array.reshape(*before, length, -1, *after), dim, 0)


def sum_at_owner(array, axis, dim):
    length = lax.axis_size(axis)
    pieces = lax.all_to_all(in_blocks(array, dim, length), axis, 0, 0, tiled=True)
    return jnp.sum(pieces, axis=0)


def sum_by_axis(array, axes, dim):
    far, near = axes
    own = sum_at_owner(in_blocks(array, dim, lax.axis_size(far)), near, dim + 1)
    return jnp.sum(lax.all_to_all(own, far, 0, 0, tiled=True), axis=0)


def padded_to(lines, length):
    spare = -lines.shape[0] % length
    if not spare:
        return lines
    return jnp.concatenate([lines, jnp.zeros((spare, *lines.shape[1:]), lines.dtype)])


def gather_axes(array, axes, dim):
    far, near = axes
    leading = from_everyone(array, far)
    pieces = jnp.swapaxes(from_everyone(leading, near), 0, 1)
    return laid_out(pieces.reshape(-1, *array.shape), dim)


def total_of(array, axes):
    own = sum_by_axis(padded_to(array, lax.axis_size(axes[0]) * lax.axis_size(axes[1])), axes, 0)
    whole = gather_axes(own, axes, 0)
    return whole[: len(array)].reshape(array.shape)


def in_one(arrays, axis):
    ravelled, at, finished = (jnp.concatenate([a.reshape(-1) for a in arrays]), 0, [])
    subtotal = total_of(ravelled, axis)
    for a in arrays:
        finished.append(subtotal[at : at + a.size].reshape(a.shape))
        at += a.size
    return tuple(finished)


def nested_sum(array, axes):
    lines = array.reshape(-1, array.shape[-1])
    own = sum_at_owner(padded_to(lines, lax.axis_size(axes)), axes, 0)
    whole = collect(own, axes, 0)
    return whole[: len(lines)].reshape(array.shape)


def broadcast(array, axis, root):
    return lax.dynamic_index_in_dim(lax.all_gather(array, axis), root, 0, keepdims=False)


def plain_product(former, latter):
    return jnp.dot(former, latter, precision=precise, preferred_element_type=jnp.float32)


def transposed_product(former, latter):
    return lax.dot_general(
        former,
        latter,
        (((0,), (0,)), ((), ())),
        precision=precise,
        preferred_element_type=jnp.float32,
    )


def paired_product(former, latter):
    return lax.dot_general(
        former,
        latter,
        (((1,), (1,)), ((), ())),
        precision=precise,
        preferred_element_type=jnp.float32,
    )


def tile_spread(blockwise, tile_size):
    row_count, col_count = blockwise.shape
    return jnp.broadcast_to(
        blockwise[:, None, :, None], (row_count, tile_size, col_count, tile_size)
    ).reshape(row_count * tile_size, col_count * tile_size)


def design_block(order_part, station_codes, values):
    select = (station_codes[None, :] == order_part[:, None]).astype(jnp.float32)
    return (select[:, None, :] * values.T[None, :, :]).reshape(
        order_part.shape[0] * values.shape[1], values.shape[0]
    )


def body(cov_tiles, block_order, stations, obs_values, obs_error):
    row_rows, col_rows = cov_tiles.shape
    tile_size = obs_values.shape[2]
    row_blocks = row_rows // tile_size
    col_blocks = col_rows // tile_size
    column_ratio = lax.axis_size("tc") // lax.axis_size(TR)
    row_index = lax.axis_index(TR)
    col_index = lax.axis_index("tc")
    values, station_codes, errors = (
        collect(obs_values, "tc", 1),
        collect(stations, "tc", 1),
        collect(obs_error, "tc", 1),
    )
    row_order = lax.dynamic_slice_in_dim(block_order, row_index * row_blocks, row_blocks)
    col_order = lax.dynamic_slice_in_dim(block_order, col_index * col_blocks, col_blocks)
    row_places = row_index * row_blocks + jnp.arange(row_blocks, dtype=jnp.int32)
    col_places = col_index * col_blocks + jnp.arange(col_blocks, dtype=jnp.int32)
    below_mask = (row_order[:, None] > col_order[None, :]).astype(jnp.float32)
    on_diagonal = (row_places[:, None] == col_places[None, :]).astype(jnp.float32)
    below_full = tile_spread(below_mask, tile_size)
    keep_full = tile_spread(below_mask + on_diagonal, tile_size)
    owner_flag = (col_index // column_ratio == row_index).astype(jnp.float32)
    offset = col_index % column_ratio * col_rows
    root_row = col_index // column_ratio
    current = cov_tiles
    strict_part = cov_tiles * below_full
    design_rows = design_block(row_order, station_codes[0], values[0])
    design_cols = design_block(col_order, station_codes[0], values[0])
    row_part = plain_product(current, design_cols)
    col_part = transposed_product(strict_part, design_rows)
    gram_part = transposed_product(design_rows, row_part) + transposed_product(
        design_cols, col_part
    )
    col_sum, gram_column = in_one((col_part, gram_part), ("tr_0", "tr_1"))
    placed = lax.dynamic_update_slice_in_dim(
        jnp.zeros_like(row_part), col_sum * owner_flag, offset, 0
    )
    cross_share = sum_at_owner(row_part + placed, "tc", 0)
    gram_total = nested_sum(gram_column, "tc")
    innovation = gram_total + jnp.diag(errors[0])
    factor = jnp.linalg.cholesky(innovation)
    scaled_share = lax.linalg.triangular_solve(
        factor, cross_share, left_side=False, lower=True, transpose_a=True
    )
    scaled = collect(scaled_share, "tc", 0)
    column_slice = lax.dynamic_slice_in_dim(scaled, offset, col_rows, 0)
    scaled_cols = broadcast(column_slice, TR, root_row)
    current = (current - paired_product(scaled, scaled_cols)) * keep_full
    return current


def solution(mesh):
    split = Mesh(mesh.devices.reshape(8, 2, mesh.shape["tc"]), ("tr_0", "tr_1", "tc"))
    return jax.shard_map(
        body,
        mesh=split,
        in_specs=(P(TR, "tc"), P(), P(None, "tc"), P(None, "tc", None), P(None, "tc")),
        out_specs=P(TR, "tc"),
        check_vma=False,
    )
```

profile of v0, /device:TPU:1, one launch (start us, length us, event | category | flops | bytes accessed | tf_op | source)
XLA Modules:
  0.0 358.9 jit_solution(9395875998569801380)
XLA Ops:
  7.2 18.9 %all_to_all.60 = s32[32,1,8]{2,1,0:T(1,128)S(1)} all-to-all(s32[32,1,8]{2,1,0:T(1,128)S(1)} %broadcast_in_dim.57), channel_id=1, replica_groups=mesh['tr_0'=8,'tr_1'=2,'tc'=32] {'tc'}, dimensions={0} | all-to-all | bytes 2048 | tf_op jit(solution)/shard_map/all_to_all | solution.py:21
  26.1 1.7 broadcast_in_dim.105
  27.9 3.9 %all-to-all-start.1 = ((f32[32,1,8,512]{3,2,1,0:T(8,128)}), f32[32,1,8,512]{3,2,1,0:T(8,128)S(1)}, u32[]{:S(2)}, u32[]{:S(2)}) async-start(f32[32,1,8,512]{3,2,1,0:T(8,128)} %broadcast_in_dim.105), calls=%async_computation.1 | async-start | bytes 1048576 | tf_op jit(solution)/shard_map/all_to_all | solution.py:21
  36.6 8.2 %all-to-all-done.1 = f32[32,1,8,512]{3,2,1,0:T(8,128)S(1)} async-done(((f32[32,1,8,512]{3,2,1,0:T(8,128)}), f32[32,1,8,512]{3,2,1,0:T(8,128)S(1)}, u32[]{:S(2)}, u32[]{:S(2)}) %all-to-all-start.1) | async-done | bytes 524320 | tf_op jit(solution)/shard_map/all_to_all | solution.py:21
  45.0 3.6 %fusion = f32[512,256]{1,0:T(8,128)S(1)} fusion(f32[1024,256]{1,0:T(8,128)S(1)} %bitcast.80, f32[1024,512]{1,0:T(8,128)S(1)} %copy-done, f32[1024]{0:T(1024)S(1)} %bitcast.94), kind=kOutput, calls=%fused_computation.3 | convolution fusion | flops 1611137024 | bytes 3674112 | tf_op jit(solution)/shard_map/dot_general | solution.py:92
  48.9 3.0 fusion.8
  51.9 1.9 fusion.25
  55.5 2.5 reshape_reshape.2
  59.6 9.9 %all_to_all.61 = f32[2,8,12288]{2,1,0:T(8,128)} all-to-all(f32[2,8,12288]{2,1,0:T(8,128)S(1)} %copy.33), channel_id=1, replica_groups=mesh['tr_0'=8,'tr_1'=2,'tc'=32] {'tr_1'}, dimensions={0} | all-to-all | bytes 1572864 | tf_op jit(solution)/shard_map/all_to_all | solution.py:37
  71.0 23.7 %all_to_all.62 = f32[8,1,12288]{2,1,0:T(1,128)S(1)} all-to-all(f32[8,1,12288]{2,1,0:T(1,128)S(1)} %all_to_all.40), channel_id=1, replica_groups=mesh['tr_0'=8,'tr_1'=2,'tc'=32] {'tr_0'}, dimensions={0} | all-to-all | bytes 786432 | tf_op jit(solution)/shard_map/all_to_all | solution.py:44
  96.7 14.8 %all_to_all.63 = f32[8,1,12288]{2,1,0:T(1,128)S(1)} all-to-all(f32[8,1,12288]{2,1,0:T(1,128)S(1)} %broadcast_in_dim.109), channel_id=1, replica_groups=mesh['tr_0'=8,'tr_1'=2,'tc'=32] {'tr_0'}, dimensions={0} | all-to-all | bytes 786432 | tf_op jit(solution)/shard_map/all_to_all | solution.py:21
  111.8 7.2 %all_to_all.64 = f32[2,8,12288]{2,1,0:T(8,128)S(1)} all-to-all(f32[2,8,12288]{2,1,0:T(8,128)S(1)} %broadcast_in_dim.111), channel_id=1, replica_groups=mesh['tr_0'=8,'tr_1'=2,'tc'=32] {'tr_1'}, dimensions={0} | all-to-all | bytes 1572864 | tf_op jit(solution)/shard_map/all_to_all | solution.py:21
  120.5 2.7 slice.56
  124.1 14.5 %all_to_all.65 = f32[32,8,256]{2,1,0:T(8,128)S(1)} all-to-all(f32[32,8,256]{2,1,0:T(8,128)S(1)} %slice.70), channel_id=1, replica_groups=mesh['tr_0'=8,'tr_1'=2,'tc'=32] {'tc'}, dimensions={0} | all-to-all | bytes 524288 | tf_op jit(solution)/shard_map/all_to_all | solution.py:37
  139.2 6.7 %all-to-all-start.9 = ((f32[32,1,8]{2,1,0:T(1,128)}), f32[32,1,8]{2,1,0:T(1,128)S(1)}, u32[]{:S(2)}, u32[]{:S(2)}) async-start(f32[32,1,8]{2,1,0:T(1,128)} %broadcast_in_dim.114), calls=%async_computation.9 | async-start | bytes 32768 | tf_op jit(solution)/shard_map/all_to_all | solution.py:21
  146.0 8.5 %all-to-all-done.9 = f32[32,1,8]{2,1,0:T(1,128)S(1)} async-done(((f32[32,1,8]{2,1,0:T(1,128)}), f32[32,1,8]{2,1,0:T(1,128)S(1)}, u32[]{:S(2)}, u32[]{:S(2)}) %all-to-all-start.9) | async-done | bytes 1056 | tf_op jit(solution)/shard_map/all_to_all | solution.py:21
  155.3 3.9 %all-to-all-start.8 = ((f32[32,8,256]{2,1,0:T(8,128)}), f32[32,8,256]{2,1,0:T(8,128)S(1)}, u32[]{:S(2)}, u32[]{:S(2)}) async-start(f32[32,8,256]{2,1,0:T(8,128)} %broadcast_in_dim.112), calls=%async_computation.8 | async-start | bytes 524288 | tf_op jit(solution)/shard_map/all_to_all | solution.py:21
  161.5 2.7 slice.54
  164.2 1.9 slice.69
  166.0 2.1 copy.46
  168.1 1.9 fusion.5
  170.0 2.5 copy.36
  172.6 9.2 %all-to-all-start.6 = ((f32[32,32,256]{2,1,0:T(8,128)}), f32[32,32,256]{2,1,0:T(8,128)S(1)}, u32[]{:S(2)}, u32[]{:S(2)}) async-start(f32[32,32,256]{2,1,0:T(8,128)} %bitcast.11), calls=%async_computation.6 | async-start | bytes 2097152 | tf_op jit(solution)/shard_map/all_to_all | solution.py:37
  183.7 1.8 copy.39
  187.2 11.7 %cholesky.49 = f32[128,128]{1,0:T(8,128)S(1)} custom-call(f32[128,128]{1,0:T(8,128)S(1)} %cholesky.115), custom_call_target="Cholesky" | custom-call | tf_op jit(solution)/shard_map/jit(cholesky)/cholesky | solution.py:165
  198.9 9.8 %custom-call.14 = f32[1,128,128]{1,2,0:T(8,128)S(1)} custom-call(f32[1,128,128]{2,1,0:T(8,128)S(1)} %get-tuple-element.43), custom_call_target="InvertDiagBlocksLowerTriangular" | custom-call | tf_op jit(solution)/shard_map/jit(cholesky)/cholesky | solution.py:165
  211.1 11.7 %cholesky.103 = f32[128,128]{1,0:T(8,128)S(1)} custom-call(f32[128,128]{1,0:T(8,128)S(1)} %convolution_subtract_fusion), custom_call_target="Cholesky" | custom-call | tf_op jit(solution)/shard_map/jit(cholesky)/cholesky | solution.py:165
  228.6 5.7 %while.1 = (s32[]{:T(128)}, f32[256,256]{0,1:T(8,128)S(1)}, s32[2,2]{1,0:T(2,128)S(1)}, f32[2,128,128]{2,1,0:T(8,128)}, s32[]{:T(128)}) while((s32[]{:T(128)}, f32[256,256]{0,1:T(8,128)S(1)}, s32[2,2]{1,0:T(2,128)S(1)}, f32[2,128,128]{2,1,0:T(8,128)}, s32[]{:T(128)}) %tuple.27), condition=%wide.while_cond, body=%wide.while_body.sunk | while | flops 2 | bytes 393329 | solution.py:166
  234.3 21.1 %custom-call.15 = f32[2,128,128]{1,2,0:T(8,128)} custom-call(f32[2,128,128]{2,1,0:T(8,128)} %get-tuple-element.12), custom_call_target="InvertDiagBlocksLowerTriangular" | custom-call | tf_op jit(solution)/shard_map/triangular_solve | solution.py:166
  257.8 30.7 %all_to_all.66 = f32[32,32,256]{2,1,0:T(8,128)S(1)} all-to-all(f32[32,32,256]{2,1,0:T(8,128)S(1)} %broadcast_in_dim.118), channel_id=1, replica_groups=mesh['tr_0'=8,'tr_1'=2,'tc'=32] {'tc'}, dimensions={0} | all-to-all | bytes 2097152 | tf_op jit(solution)/shard_map/all_to_all | solution.py:21
  289.4 58.5 %all-gather.3.cloned.1.call-done = f32[8192,256]{1,0:T(8,128)} async-done(((f32[512,256]{1,0:T(8,128)}), f32[8192,256]{1,0:T(8,128)}) %all-gather.3.cloned.1.call-update) | async-done | bytes 8388624 | tf_op jit(solution)/shard_map/all_gather | solution.py:84
  347.9 4.2 %subtract_multiply_fusion = f32[1024,512]{1,0:T(8,128)} fusion(f32[1024,512]{1,0:T(8,128)S(1)} %copy-done, f32[1024,256]{1,0:T(8,128)S(1)} %bitcast.84, f32[1024]{0:T(1024)S(1)} %bitcast.95, f32[16,512,256]{2,1,0:T(8,128)} %bitcast.92, s32[]{:T(128)S(6)} %select_n.42), kind=kOutput, calls=%fused_computation.2 | convolution fusion | flops 1611661312 | bytes 5771268 | tf_op jit(solution)/shard_map/dot_general | solution.py:102
  (86 shorter events, 38.3 us)
Async XLA Ops:
  26.1 18.9 %copy-start = (f32[1024,512]{1,0:T(8,128)S(1)}, f32[1024,512]{1,0:T(8,128)}, u32[]{:S(2)}) copy-start(f32[1024,512]{1,0:T(8,128)} %param.5) | copy-start | bytes 6291460
  27.9 16.9 %all-to-all-start.1 = ((f32[32,1,8,512]{3,2,1,0:T(8,128)}), f32[32,1,8,512]{3,2,1,0:T(8,128)S(1)}, u32[]{:S(2)}, u32[]{:S(2)}) async-start(f32[32,1,8,512]{3,2,1,0:T(8,128)} %broadcast_in_dim.105), calls=%async_computation.1 | async-start | bytes 1048576 | tf_op jit(solution)/shard_map/all_to_all | solution.py:21
  44.7 3.9 %copy-start.1 = (f32[32,1,8,512]{3,2,1,0:T(8,128)}, f32[32,1,8,512]{3,2,1,0:T(8,128)S(1)}, u32[]{:S(2)}) copy-start(f32[32,1,8,512]{3,2,1,0:T(8,128)S(1)} %all-to-all-done.1) | copy-start | bytes 1572868
  51.9 1.9 copy-start.2
  119.0 19.6 %copy-start.5 = (f32[1,8]{1,0:T(1,128)S(1)}, f32[1,8]{1,0:T(1,128)}, u32[]{:S(2)}) copy-start(f32[1,8]{1,0:T(1,128)} %param.9) | copy-start | bytes 100
  139.2 15.3 %all-to-all-start.9 = ((f32[32,1,8]{2,1,0:T(1,128)}), f32[32,1,8]{2,1,0:T(1,128)S(1)}, u32[]{:S(2)}, u32[]{:S(2)}) async-start(f32[32,1,8]{2,1,0:T(1,128)} %broadcast_in_dim.114), calls=%async_computation.9 | async-start | bytes 32768 | tf_op jit(solution)/shard_map/all_to_all | solution.py:21
  155.3 17.3 %all-to-all-start.8 = ((f32[32,8,256]{2,1,0:T(8,128)}), f32[32,8,256]{2,1,0:T(8,128)S(1)}, u32[]{:S(2)}, u32[]{:S(2)}) async-start(f32[32,8,256]{2,1,0:T(8,128)} %broadcast_in_dim.112), calls=%async_computation.8 | async-start | bytes 524288 | tf_op jit(solution)/shard_map/all_to_all | solution.py:21
  172.6 9.3 %copy-start.3 = (f32[32,8,256]{2,1,0:T(8,128)}, f32[32,8,256]{2,1,0:T(8,128)S(1)}, u32[]{:S(2)}) copy-start(f32[32,8,256]{2,1,0:T(8,128)S(1)} %all-to-all-done.8) | copy-start | bytes 786436
  172.6 82.9 %all-to-all-start.6 = ((f32[32,32,256]{2,1,0:T(8,128)}), f32[32,32,256]{2,1,0:T(8,128)S(1)}, u32[]{:S(2)}, u32[]{:S(2)}) async-start(f32[32,32,256]{2,1,0:T(8,128)} %bitcast.11), calls=%async_computation.6 | async-start | bytes 2097152 | tf_op jit(solution)/shard_map/all_to_all | solution.py:37
  181.8 166.0 %all-gather.3.cloned.1.call-start = ((), (), s32[]{:S(2)}) async-start(), calls=%async_computation.11 | async-start | bytes 8912896 | tf_op jit(solution)/shard_map/all_gather | solution.py:84
  186.5 0.7 copy-start.4
Sparse Core Ops, SparseCore 0:
  289.5 58.3 all-gather.2
where the time goes:
time: 361 us; the launch traced here: 359 us
  blocking collectives  120 us (33%)
  waiting for transfers between devices  75.2 us (21%)
  other arithmetic  67.1 us (19%)
  local copies, waits for them, and re-layouts  40.2 us (11%)
  starting transfers between devices  23.7 us (7%)
  matrix products  17.6 us (5%)
  between operations  15.1 us (4%)
    all_to_all x4, blocking collectives, from_everyone(): lax.all_to_all(jnp.broadcast_to(array[None], (length, *array.shape)), axi...  71.6 us
    all_gather x1, waiting for transfers between devices, broadcast(): lax.all_gather(array, axis)  58.5 us
    another operation x7, other arithmetic, body(): factor = jnp.linalg.cholesky(innovation)  34.7 us
    all_to_all x2, blocking collectives, sum_at_owner(): lax.all_to_all(in_blocks(array, dim, length), axis, 0, 0, tiled=True)  24.4 us
    all_to_all x1, blocking collectives, sum_by_axis(): return jnp.sum(lax.all_to_all(own, far, 0, 0, tiled=True), axis=0)  23.7 us
    another operation x4, other arithmetic, body(): lax.linalg.triangular_solve(factor, cross_share, left_side=False, lower=T...  22.1 us
    all_to_all x3, waiting for transfers between devices, from_everyone(): lax.all_to_all(jnp.broadcast_to(array[None], (length, *array.shape)), axi...  16.7 us
    all_to_all x3, starting transfers between devices, from_everyone(): lax.all_to_all(jnp.broadcast_to(array[None], (length, *array.shape)), axi...  14.5 us
  transfers between devices with their start and end apart: 5, of which 3 were waited for; matrix products, arithmetic and copies ran while one was open for 25% of the time, Pallas kernels for 0%

commit v1 on v0

v1 whole, which is shorter than its diff:
```python
import jax
import jax.numpy as jnp
from jax import lax
from jax.sharding import Mesh
from jax.sharding import PartitionSpec as P

TR = ("z", "k")
TC = ("x", "yh", "yl")
NEAR = ("z", "k", "yl")
ALL = ("z", "k", "x", "yh", "yl")
SLOTS = 32
PAIR_SLOTS = 48
LANES = 128

precise = lax.Precision.HIGHEST


def dot(former, latter, dims=((1,), (0,))):
    return lax.dot_general(
        former, latter, (dims, ((), ())), precision=precise, preferred_element_type=jnp.float32
    )


def exchange(array, axes):
    return lax.all_to_all(array, axes, 0, 0, tiled=True)


def spread(array, axes):
    count = lax.axis_size(axes)
    return exchange(jnp.broadcast_to(array[None], (count, *array.shape)), axes)


def body(cov, order, stations, obs_values, obs_error):
    rows, tile = cov.shape
    nobs_own = obs_values.shape[1]
    tr_size, tc_size = lax.axis_size(TR), lax.axis_size(TC)
    nobs = nobs_own * tc_size
    share = tile // tc_size
    halves = share // 8
    row = lax.axis_index(TR)
    col = lax.axis_index(TC)
    blocks = order.shape[0]

    tail = jnp.stack([stations[0].astype(jnp.float32), obs_error[0]], axis=1)
    packed = jnp.concatenate(
        [obs_values[0], jnp.pad(tail, ((0, 0), (0, LANES - tail.shape[1])))], axis=1
    )
    everything = spread(packed, TC).reshape(nobs, tile + LANES)
    values = everything[:, :tile]
    station = everything[:, tile].astype(jnp.int32)
    errors = everything[:, tile + 1]

    numbers = jnp.arange(nobs, dtype=jnp.int32)
    position = jnp.sum(
        jnp.where(station[None, :] == order[:, None], jnp.arange(blocks, dtype=jnp.int32)[:, None], 0), axis=0
    )
    before = numbers[:, None] < numbers[None, :]
    rank = jnp.sum(((station[:, None] == station[None, :]) & before).astype(jnp.int32), axis=0)
    pair = position // 2
    pair_rank = jnp.sum(((pair[:, None] == pair[None, :]) & before).astype(jnp.int32), axis=0)
    rounds = 1 + jnp.maximum(jnp.max(rank) // SLOTS, jnp.max(pair_rank) // PAIR_SLOTS)

    lane = jnp.arange(LANES, dtype=jnp.int32)
    weighted = [values * (position == 2 * row + t).astype(jnp.float32)[:, None] for t in range(2)]

    def one_round(number, carry):
        cross_rows, gram_rows = carry
        slot = rank - number * SLOTS
        code = jnp.where((slot >= 0) & (slot < SLOTS), position * SLOTS + slot, -1)
        pair_slot = pair_rank - number * PAIR_SLOTS
        pair_code = jnp.where(
            (pair_slot >= 0) & (pair_slot < PAIR_SLOTS), pair * PAIR_SLOTS + pair_slot, -1
        )
        pick = (code[None, :] == (col * SLOTS + lane % SLOTS)[:, None]).astype(jnp.float32)
        column_weights = dot(pick, values)
        row_terms = dot(cov, column_weights, ((1,), (1,)))
        pair_pick = (pair_code[None, :] == (row * PAIR_SLOTS + lane % PAIR_SLOTS)[:, None]) & (
            lane < 2 * PAIR_SLOTS
        )[:, None]
        pair_weights = []
        for t in range(2):
            off_diagonal = (2 * row + t) != col
            chosen = pair_pick & (position == 2 * row + t)[None, :] & off_diagonal
            pair_weights.append(dot(chosen.astype(jnp.float32), values))
        column_terms = dot(cov[:tile], pair_weights[0], ((0,), (1,))) + dot(
            cov[tile:], pair_weights[1], ((0,), (1,))
        )
        gram_terms = dot(weighted[0], row_terms[:tile]) + dot(weighted[1], row_terms[tile:])
        shaped = row_terms.reshape(2, tc_size, halves, 8, LANES)
        first = sum(
            jnp.where(lane // SLOTS == t * halves + m, shaped[t, :, m], 0.0)
            for t in range(2)
            for m in range(halves)
        )
        shaped = column_terms.reshape(tc_size, halves, 8, LANES)
        second = sum(
            jnp.where(lane // PAIR_SLOTS == m, shaped[:, m], 0.0) for m in range(halves)
        )
        second = jnp.where(lane >= LANES - SLOTS, gram_terms.reshape(tc_size, 8, LANES), second)
        arrived = exchange(jnp.concatenate([first, second], axis=1), TC)

        slots = jnp.arange(tc_size * SLOTS, dtype=jnp.int32)
        place = (slots[:, None] == code[None, :]).astype(jnp.float32)
        first = arrived[:, :8].reshape(tc_size, 8, 2 * halves, SLOTS)
        first = first.transpose(2, 1, 0, 3).reshape(2 * share, tc_size * SLOTS)
        gram = arrived[:, 8:, LANES - SLOTS :].transpose(1, 0, 2).reshape(8, tc_size * SLOTS)
        placed = dot(jnp.concatenate([first, gram]), place)
        gram = placed[2 * share :].reshape(8, nobs // LANES, LANES).transpose(1, 0, 2)
        second = jnp.concatenate(
            [
                arrived[:, 8:].reshape(tr_size, 2, 8, LANES),
                jnp.broadcast_to(gram[None], (tr_size, *gram.shape)),
            ],
            axis=1,
        )
        arrived = exchange(second, TR)
        pair_slots = jnp.arange(tr_size * PAIR_SLOTS, dtype=jnp.int32)
        pair_place = (pair_slots[:, None] == pair_code[None, :]).astype(jnp.float32)
        second = arrived[:, :2, :, : halves * PAIR_SLOTS].reshape(tr_size, 2, 8, halves, PAIR_SLOTS)
        second = second.transpose(1, 3, 2, 0, 4).reshape(2 * share, tr_size * PAIR_SLOTS)
        gram = jnp.sum(arrived[:, 2:], axis=0).transpose(1, 0, 2).reshape(8, nobs)
        cross_rows = cross_rows + placed[: 2 * share] + dot(second, pair_place)
        return cross_rows, gram_rows + gram

    cross_rows, gram_rows = lax.fori_loop(
        0,
        rounds,
        one_round,
        (jnp.zeros((2 * share, nobs), jnp.float32), jnp.zeros((8, nobs), jnp.float32)),
    )

    moves = [
        (r * tc_size + c, (c // 2) * tc_size + 2 * r + c % 2)
        for r in range(tr_size)
        for c in range(tc_size)
    ]
    moved = lax.ppermute(cross_rows, ALL, moves)
    arrived = spread(jnp.concatenate([cross_rows, gram_rows]), TC)
    row_cross = arrived[:, : 2 * share].reshape(tc_size, 2, share, nobs)
    row_cross = row_cross.transpose(1, 0, 2, 3).reshape(rows, nobs)
    gram = arrived[:, 2 * share :].reshape(nobs, nobs)
    near = jnp.broadcast_to(moved.reshape(1, 2, share, nobs), (tr_size, 2, share, nobs))
    col_cross = exchange(near.reshape(2 * tr_size, share, nobs), NEAR).reshape(tile, nobs)

    both = gram + gram.T
    same = position[:, None] == position[None, :]
    innovation = jnp.where(same, 0.5 * both, both) + jnp.diag(errors)
    factor = jnp.linalg.cholesky(innovation)
    inverse = lax.linalg.triangular_solve(
        factor, jnp.eye(nobs, dtype=jnp.float32), left_side=True, lower=True
    )
    row_scaled = dot(row_cross, inverse, ((1,), (1,)))
    col_scaled = dot(col_cross, inverse, ((1,), (1,)))
    places = 2 * row + jnp.arange(2, dtype=jnp.int32)
    row_order = lax.dynamic_slice_in_dim(order, 2 * row, 2)
    col_order = lax.dynamic_slice_in_dim(order, col, 1)
    keep = ((row_order > col_order) | (places == col)).astype(jnp.float32)
    updated = cov - dot(row_scaled, col_scaled, ((1,), (1,)))
    return (updated.reshape(2, tile, tile) * keep[:, None, None]).reshape(rows, tile)


def solution(mesh):
    tr_size, tc_size = mesh.shape["tr"], mesh.shape["tc"]
    y_size = 8 if tc_size % 8 == 0 else tc_size
    split = Mesh(
        mesh.devices.reshape(tr_size // 2, 2, tc_size // y_size, y_size // 2, 2), ALL
    )
    return jax.shard_map(
        body,
        mesh=split,
        in_specs=(P(TR, TC), P(), P(None, TC), P(None, TC, None), P(None, TC)),
        out_specs=P(TR, TC),
        check_vma=False,
    )
```

time: 361 us -> 249 us (0.69)
  blocking collectives: 120 us -> 17.9 us
  waiting for transfers between devices: 75.2 us -> 54.9 us
  starting transfers between devices: 23.7 us -> 43.9 us
  local copies, waits for them, and re-layouts: 40.2 us -> 24.2 us
  other arithmetic: 67.1 us -> 78.9 us
  between operations: 15.1 us -> 6.27 us
    all_to_all x7 -> x1, blocking collectives: 120 us -> 17.9 us  [exchange(): return lax.all_to_all(array, axes, 0, 0, tiled=True)]
    all_gather x1 -> x0, waiting for transfers between devices: 58.5 us -> none  [broadcast(): lax.all_gather(array, axis)]
    ppermute x0 -> x1, waiting for transfers between devices: none -> 24.1 us  [body(): moved = lax.ppermute(cross_rows, ALL, moves)]
    all_to_all x4, starting transfers between devices: 23.7 us -> 39.8 us  [exchange(): return lax.all_to_all(array, axes, 0, 0, tiled=True)]
    all_to_all x4, waiting for transfers between devices: 16.7 us -> 30.8 us  [exchange(): return lax.all_to_all(array, axes, 0, 0, tiled=True)]
    slice x4, local copies, waits for them, and re-layouts: 8.23 us -> 1.24 us  [the longest x1 1.08 us: body(): errors = everything[:, tile + 1]]
    reshape x1 -> x8, local copies, waits for them, and re-layouts: 1.08 us -> 5.6 us  [the longest x2 2.5 us: body(): gram = arrived[:, 2 * share:].reshape(nobs, nobs)]
    ppermute x0 -> x1, starting transfers between devices: none -> 4.05 us  [body(): moved = lax.ppermute(cross_rows, ALL, moves)]
  transfers between devices with their start and end apart: 5 -> 5, of which waited for: 3 -> 4; matrix products, arithmetic and copies ran while one was open for 25% -> 34% of each run, Pallas kernels for 0% -> 0%
where the time goes in v1:
time: 249 us; the launch traced here: 247 us
  other arithmetic  78.9 us (32%)
  waiting for transfers between devices  54.9 us (22%)
  starting transfers between devices  43.9 us (18%)
  local copies, waits for them, and re-layouts  24.2 us (10%)
  matrix products  20.8 us (8%)
  blocking collectives  17.9 us (7%)
  between operations  6.27 us (3%)
    all_to_all x4, starting transfers between devices, exchange(): return lax.all_to_all(array, axes, 0, 0, tiled=True)  39.8 us
    another operation x7, other arithmetic, body(): factor = jnp.linalg.cholesky(innovation)  38.4 us
    all_to_all x4, waiting for transfers between devices, exchange(): return lax.all_to_all(array, axes, 0, 0, tiled=True)  30.8 us
    ppermute x1, waiting for transfers between devices, body(): moved = lax.ppermute(cross_rows, ALL, moves)  24.1 us
    another operation x3, other arithmetic, body(): lax.linalg.triangular_solve(factor, jnp.eye(nobs, dtype=jnp.float32), lef...  22.4 us
    all_to_all x1, blocking collectives, exchange(): return lax.all_to_all(array, axes, 0, 0, tiled=True)  17.9 us
    dot_general x13, matrix products, dot(): lax.dot_general(former, latter, (dims, ((), ())), precision=precise, pref...  14.9 us
    another operation x6, local copies, waits for them, and re-layouts  6.69 us
  transfers between devices with their start and end apart: 5, of which 4 were waited for; matrix products, arithmetic and copies ran while one was open for 34% of the time, Pallas kernels for 0%

profile of v1, /device:TPU:1, one launch (start us, length us, event | category | flops | bytes accessed | tf_op | source)
XLA Modules:
  0.0 247.1 jit_solution(17374287495022407571)
XLA Ops:
  3.0 10.5 %all-to-all-start.2 = ((f32[32,8,640]{2,1,0:T(8,128)}), f32[32,8,640]{2,1,0:T(8,128)S(1)}, u32[]{:S(2)}, u32[]{:S(2)}) async-start(f32[32,8,640]{2,1,0:T(8,128)} %broadcast_in_dim.183), calls=%async_computation.2 | async-start | bytes 1310720 | tf_op jit(solution)/shard_map/all_to_all | solution.py:25
  13.6 16.4 %all-to-all-done.2 = f32[32,8,640]{2,1,0:T(8,128)S(1)} async-done(((f32[32,8,640]{2,1,0:T(8,128)}), f32[32,8,640]{2,1,0:T(8,128)S(1)}, u32[]{:S(2)}, u32[]{:S(2)}) %all-to-all-start.2) | async-done | bytes 655392 | tf_op jit(solution)/shard_map/all_to_all | solution.py:25
  30.7 1.5 convert_reduce_fusion
  35.4 1.4 reduce_max.19
  41.3 63.7 %while.21 = (s32[]{:T(128)}, f32[32,256]{1,0:T(8,128)}, f32[8,256]{1,0:T(8,128)S(1)}, s32[]{:T(128)}, s32[256]{0:T(256)}, /*index=5*/s32[256]{0:T(256)S(1)}, s32...) while((s32[]{:T(128)}, f32[32,256]{1,0:T(8,128)}, ...), condition=%wide.region_7.8_spmd.clone.clone, body=%wide.region_5.7_spmd.clone.clone.sunk | while | flops 2820016896 | bytes 19294208 | solution.py:125
  47.0 2.3 convolution_bitcast_fusion.2
  50.3 1.7 fusion.146
  52.0 1.7 fusion.147
  55.7 17.9 %all_to_all.43 = f32[32,16,128]{2,1,0:T(8,128)S(1)} all-to-all(f32[32,16,128]{2,1,0:T(8,128)S(1)} %pad_maximum_fusion.9), channel_id=1, replica_groups=mesh['z'=8,'k'=2,'x'=4,'yh'=4,'yl'=2] {'x','yh','yl'}, dimensions={0} | all-to-all | bytes 524288 | tf_op jit(solution)/shard_map/while/body/all_to_all | solution.py:25
  75.2 1.3 reshape.319
  77.8 13.9 %all-to-all-start.1 = ((f32[16,4,8,128]{3,2,1,0:T(8,128)}), f32[16,4,8,128]{3,2,1,0:T(8,128)S(1)}, u32[]{:S(2)}, u32[]{:S(2)}) async-start(f32[16,4,8,128]{3,2,1,0:T(8,128)} %pad_maximum_fusion.10), calls=%async_computation.1 | async-start | bytes 524288 | tf_op jit(solution)/shard_map/while/body/all_to_all | solution.py:25
  91.7 11.7 %all-to-all-done.1 = f32[16,4,8,128]{3,2,1,0:T(8,128)S(1)} async-done(((f32[16,4,8,128]{3,2,1,0:T(8,128)}), f32[16,4,8,128]{3,2,1,0:T(8,128)S(1)}, u32[]{:S(2)}, u32[]{:S(2)}) %all-to-all-start.1) | async-done | bytes 262176 | tf_op jit(solution)/shard_map/while/body/all_to_all | solution.py:25
  107.0 4.3 %all-to-all-start.3 = ((f32[32,40,256]{2,1,0:T(8,128)}), f32[32,40,256]{2,1,0:T(8,128)S(1)}, u32[]{:S(2)}, u32[]{:S(2)}) async-start(f32[32,40,256]{2,1,0:T(8,128)} %broadcast_in_dim.186), calls=%async_computation.3 | async-start | bytes 2621440 | tf_op jit(solution)/shard_map/all_to_all | solution.py:25
  112.6 4.1 %collective-permute-start = (f32[32,256]{1,0:T(8,128)S(1)}, f32[32,256]{1,0:T(8,128)S(1)}, u32[]{:S(2)}, u32[]{:S(2)}) collective-permute-start(f32[32,256]{1,0:T(8,128)S(1)} %copy-done.6), channel_id=1, source_target_pairs={{0,0},{1,1},{2,32},{3,33},{4,64},{5,65},{6,96},{7,97},{8,128},{9,1... | collective-permute-start | bytes 98312 | tf_op jit(solution)/shard_map/ppermute | solution.py:137
  117.7 24.1 %collective-permute-done = f32[32,256]{1,0:T(8,128)S(1)} collective-permute-done((f32[32,256]{1,0:T(8,128)S(1)}, f32[32,256]{1,0:T(8,128)S(1)}, u32[]{:S(2)}, u32[]{:S(2)}) %collective-permute-start) | collective-permute-done | bytes 32800 | tf_op jit(solution)/shard_map/ppermute | solution.py:137
  141.8 2.7 %all-to-all-done.3 = f32[32,40,256]{2,1,0:T(8,128)S(1)} async-done(((f32[32,40,256]{2,1,0:T(8,128)}), f32[32,40,256]{2,1,0:T(8,128)S(1)}, u32[]{:S(2)}, u32[]{:S(2)}) %all-to-all-start.3) | async-done | bytes 1310752 | tf_op jit(solution)/shard_map/all_to_all | solution.py:25
  145.4 11.1 %all-to-all-start.4 = ((f32[32,16,256]{2,1,0:T(8,128)}), f32[32,16,256]{2,1,0:T(8,128)}, u32[]{:S(2)}, u32[]{:S(2)}) async-start(f32[32,16,256]{2,1,0:T(8,128)} %bitcast.218), calls=%async_computation.4 | async-start | bytes 1048576 | tf_op jit(solution)/shard_map/all_to_all | solution.py:25
  157.2 1.8 copy.58
  159.0 1.8 fusion.54
  160.8 1.8 copy.59
  165.0 12.5 %cholesky.49 = f32[128,128]{1,0:T(8,128)S(1)} custom-call(f32[128,128]{1,0:T(8,128)} %cholesky.115), custom_call_target="Cholesky" | custom-call | tf_op jit(solution)/shard_map/jit(cholesky)/cholesky | solution.py:148
  179.6 10.6 %custom-call.14 = f32[1,128,128]{1,2,0:T(8,128)S(1)} custom-call(f32[1,128,128]{2,1,0:T(8,128)} %get-tuple-element.676), custom_call_target="InvertDiagBlocksLowerTriangular" | custom-call | tf_op jit(solution)/shard_map/jit(cholesky)/cholesky | solution.py:148
  190.3 1.7 constant_dynamic-update-slice_fusion.1
  192.0 1.7 convolution_subtract_fusion.1
  193.7 12.5 %cholesky.103 = f32[128,128]{1,0:T(8,128)S(1)} custom-call(f32[128,128]{1,0:T(8,128)} %convolution_subtract_fusion.1), custom_call_target="Cholesky" | custom-call | tf_op jit(solution)/shard_map/jit(cholesky)/cholesky | solution.py:148
  208.9 1.7 select_select_fusion
  210.6 6.7 %while.20 = (s32[]{:T(128)}, f32[256,256]{1,0:T(8,128)}, s32[2,2]{1,0:T(2,128)S(1)}, f32[2,128,128]{2,1,0:T(8,128)}, s32[]{:T(128)}) while((s32[]{:T(128)}, f32[256,256]{1,0:T(8,128)}, s32[2,2]{1,0:T(2,128)S(1)}, f32[2,128,128]{2,1,0:T(8,128)}, s32[]{:T(128)}) %tuple.87), condition=%wide.while_cond, body=%wide.while_body.sunk | while | flops 2 | bytes 132205 | solution.py:149
  211.2 2.8 %bitcast_dynamic-update-slice_fusion.2 = f32[2,128,128]{2,1,0:T(8,128)} fusion(f32[2,128,128]{2,1,0:T(8,128)} %get-tuple-element.921, s32[]{:T(128)S(6)} %copy.95, f32[256,256]{1,0:T(8,128)} %get-tuple-element.924, s32[]{:T(128)} %bitcast.178, s32[]{:T(128)} %bitcast.179), kind=kLoop, calls=%fused_computation.3.clone.1 | loop fusion | bytes 132100 | tf_op jit(solution)/shard_map/triangular_solve
  214.6 2.7 %bitcast_dynamic-update-slice_fusion.2 = f32[2,128,128]{2,1,0:T(8,128)} fusion(f32[2,128,128]{2,1,0:T(8,128)} %get-tuple-element.921, s32[]{:T(128)S(6)} %copy.95, f32[256,256]{1,0:T(8,128)} %get-tuple-element.924, s32[]{:T(128)} %bitcast.178, s32[]{:T(128)} %bitcast.179), kind=kLoop, calls=%fused_computation.3.clone.1 | loop fusion | bytes 132100 | tf_op jit(solution)/shard_map/triangular_solve
  217.5 20.7 %custom-call.15 = f32[2,128,128]{1,2,0:T(8,128)S(1)} custom-call(f32[2,128,128]{2,1,0:T(8,128)} %get-tuple-element.500), custom_call_target="InvertDiagBlocksLowerTriangular" | custom-call | tf_op jit(solution)/shard_map/triangular_solve | solution.py:149
  241.2 1.7 fusion.58
  243.9 3.2 %subtract_multiply_fusion = f32[1024,512]{1,0:T(8,128)} fusion(f32[1024,512]{1,0:T(8,128)S(1)} %get-tuple-element.928, f32[1024,256]{1,0:T(8,128)S(1)} %fusion.59, f32[512,256]{1,0:T(8,128)S(1)} %fusion.58, f32[1024]{0:T(1024)S(1)} %bitcast.220), kind=kOutput, calls=%fused_computation.95 | convolution fusion | flops 1611661312 | bytes 5771264 | tf_op jit(solution)/shard_map/dot_general | solution.py:19
  (102 shorter events, 36.8 us)
Async XLA Ops:
  0.0 30.0 %copy-start.9 = (s32[32]{0:T(128)S(1)}, s32[32]{0:T(128)}, u32[]{:S(2)}) copy-start(s32[32]{0:T(128)} %param.8) | copy-start | bytes 388
  2.1 39.2 %copy-start = (f32[1024,512]{1,0:T(8,128)S(1)}, f32[1024,512]{1,0:T(8,128)}, u32[]{:S(2)}) copy-start(f32[1024,512]{1,0:T(8,128)} %param.7) | copy-start | bytes 6291460
  3.0 26.9 %all-to-all-start.2 = ((f32[32,8,640]{2,1,0:T(8,128)}), f32[32,8,640]{2,1,0:T(8,128)S(1)}, u32[]{:S(2)}, u32[]{:S(2)}) async-start(f32[32,8,640]{2,1,0:T(8,128)} %broadcast_in_dim.183), calls=%async_computation.2 | async-start | bytes 1310720 | tf_op jit(solution)/shard_map/all_to_all | solution.py:25
  29.9 11.4 %copy-start.1 = (f32[32,8,640]{2,1,0:T(8,128)}, f32[32,8,640]{2,1,0:T(8,128)S(1)}, u32[]{:S(2)}) copy-start(f32[32,8,640]{2,1,0:T(8,128)S(1)} %all-to-all-done.2) | copy-start | bytes 1966084
  44.4 2.3 copy-start.7
  55.7 20.8 %copy-start.8 = (s32[256]{0:T(256)S(1)}, s32[256]{0:T(256)}, u32[]{:S(2)}) copy-start(s32[256]{0:T(256)} %copy-done.7) | copy-start | bytes 3076 | tf_op jit(solution)/shard_map/while
  75.2 28.7 %copy-start.4 = (f32[32,256]{1,0:T(8,128)S(1)}, f32[32,256]{1,0:T(8,128)}, u32[]{:S(2)}) copy-start(f32[32,256]{1,0:T(8,128)} %get-tuple-element.872) | copy-start | bytes 98308 | tf_op jit(solution)/shard_map/while
  77.8 25.6 %all-to-all-start.1 = ((f32[16,4,8,128]{3,2,1,0:T(8,128)}), f32[16,4,8,128]{3,2,1,0:T(8,128)S(1)}, u32[]{:S(2)}, u32[]{:S(2)}) async-start(f32[16,4,8,128]{3,2,1,0:T(8,128)} %pad_maximum_fusion.10), calls=%async_computation.1 | async-start | bytes 524288 | tf_op jit(solution)/shard_map/while/body/all_to_all | solution.py:25
  104.4 0.6 copy-start.5
  105.0 6.3 %copy-start.10 = (s32[32]{0:T(128)S(1)}, s32[32]{0:T(128)}, u32[]{:S(2)}) copy-start(s32[32]{0:T(128)} %param.8) | copy-start | bytes 388
  105.0 7.6 %copy-start.6 = (f32[32,256]{1,0:T(8,128)S(1)}, f32[32,256]{1,0:T(8,128)}, u32[]{:S(2)}) copy-start(f32[32,256]{1,0:T(8,128)} %get-tuple-element.491) | copy-start | bytes 98308
  107.0 37.6 %all-to-all-start.3 = ((f32[32,40,256]{2,1,0:T(8,128)}), f32[32,40,256]{2,1,0:T(8,128)S(1)}, u32[]{:S(2)}, u32[]{:S(2)}) async-start(f32[32,40,256]{2,1,0:T(8,128)} %broadcast_in_dim.186), calls=%async_computation.3 | async-start | bytes 2621440 | tf_op jit(solution)/shard_map/all_to_all | solution.py:25
  112.6 29.2 %collective-permute-start = (f32[32,256]{1,0:T(8,128)S(1)}, f32[32,256]{1,0:T(8,128)S(1)}, u32[]{:S(2)}, u32[]{:S(2)}) collective-permute-start(f32[32,256]{1,0:T(8,128)S(1)} %copy-done.6), channel_id=1, source_target_pairs={{0,0},{1,1},{2,32},{3,33},{4,64},{5,65},{6,96},{7,97},{8,128},{9,1... | collective-permute-start | bytes 98312 | tf_op jit(solution)/shard_map/ppermute | solution.py:137
  145.4 95.8 %all-to-all-start.4 = ((f32[32,16,256]{2,1,0:T(8,128)}), f32[32,16,256]{2,1,0:T(8,128)}, u32[]{:S(2)}, u32[]{:S(2)}) async-start(f32[32,16,256]{2,1,0:T(8,128)} %bitcast.218), calls=%async_computation.4 | async-start | bytes 1048576 | tf_op jit(solution)/shard_map/all_to_all | solution.py:25
  163.7 0.7 copy-start.2
  238.3 0.7 copy-start.3

commit v2 on v1

v2 whole, which is shorter than its diff:
```python
import jax
import jax.numpy as jnp
from jax import lax
from jax.experimental import pallas as pl
from jax.experimental.pallas import tpu as pltpu
from jax.sharding import Mesh
from jax.sharding import PartitionSpec as P

TR = ("z", "k")
TC = ("x", "yh", "yl")
NEAR = ("z", "k", "yl")
ALL = ("z", "k", "x", "yh", "yl")
SLOTS = 32
PAIR_SLOTS = 48
LANES = 128
GROUPS = LANES // SLOTS
SETTLED = 1e-7

precise = lax.Precision.HIGHEST


def dot(former, latter, dims=((1,), (0,))):
    return lax.dot_general(
        former, latter, (dims, ((), ())), precision=precise, preferred_element_type=jnp.float32
    )


def iota(shape, dim):
    return lax.broadcasted_iota(jnp.int32, shape, dim)


def exchange(array, axes):
    return lax.all_to_all(array, axes, 0, 0, tiled=True)


def in_vmem(count):
    return [pl.BlockSpec(memory_space=pltpu.VMEM)] * count


def params():
    return pltpu.CompilerParams(vmem_limit_bytes=48 * 1024 * 1024)


def as_row(column):
    return jnp.broadcast_to(column, (column.shape[0], LANES)).T[:1]


def codes_kernel(everything, order_column, codes, rounds):
    nobs = everything.shape[0]
    tile = everything.shape[1] - LANES
    station = everything[:, tile : tile + 1].astype(jnp.int32)
    station_row = as_row(everything[:, tile : tile + 1]).astype(jnp.int32)
    blocks = order_column.shape[0]
    position = jnp.sum(
        jnp.where(order_column[...] == station_row, iota((blocks, nobs), 0), 0), axis=0, keepdims=True
    )
    position_column = jnp.broadcast_to(position, (LANES, nobs)).astype(jnp.float32).T[:, :1].astype(jnp.int32)
    before = iota((nobs, nobs), 0) < iota((nobs, nobs), 1)
    rank = jnp.sum(((station == station_row) & before).astype(jnp.int32), axis=0, keepdims=True)
    paired = (position_column >> 1) == (position >> 1)
    pair_rank = jnp.sum((paired & before).astype(jnp.int32), axis=0, keepdims=True)
    codes[0:1] = position
    codes[1:2] = rank
    codes[2:3] = pair_rank
    codes[3:8] = jnp.zeros((5, nobs), jnp.int32)
    rounds[0] = 1 + jnp.maximum(jnp.max(rank) // SLOTS, jnp.max(pair_rank) // PAIR_SLOTS)


def make_codes(everything, order):
    return pl.pallas_call(
        codes_kernel,
        out_shape=(
            jax.ShapeDtypeStruct((8, everything.shape[0]), jnp.int32),
            jax.ShapeDtypeStruct((1,), jnp.int32),
        ),
        in_specs=in_vmem(2),
        out_specs=(pl.BlockSpec(memory_space=pltpu.VMEM), pl.BlockSpec(memory_space=pltpu.SMEM)),
        compiler_params=params(),
    )(everything, order.reshape(-1, 1))


def slot_codes(codes, number):
    position = codes[0:1]
    slot = codes[1:2] - number * SLOTS
    code = jnp.where((slot >= 0) & (slot < SLOTS), position * SLOTS + slot, -1)
    pair_slot = codes[2:3] - number * PAIR_SLOTS
    pair_code = jnp.where(
        (pair_slot >= 0) & (pair_slot < PAIR_SLOTS), (position >> 1) * PAIR_SLOTS + pair_slot, -1
    )
    return position, code, pair_code


def terms_kernel(where, everything, codes, cov, out):
    row, col, number = where[0], where[1], where[2]
    rows, tile = cov.shape
    nobs = everything.shape[0]
    groups = out.shape[0]
    halves = tile // groups // 8
    values = everything[:, :tile]
    position, code, pair_code = slot_codes(codes, number)
    sub = iota((LANES, nobs), 0)
    pick = (code == col * SLOTS + sub % SLOTS).astype(jnp.float32)
    column_weights = dot(pick, values)
    row_terms = dot(cov[...], column_weights, ((1,), (1,)))
    pair_pick = (pair_code == row * PAIR_SLOTS + sub % PAIR_SLOTS) & (sub < 2 * PAIR_SLOTS)
    column_terms = jnp.zeros((LANES, tile), jnp.float32)
    gram_terms = jnp.zeros((nobs, LANES), jnp.float32)
    position_column = jnp.broadcast_to(position, (LANES, nobs)).astype(jnp.float32).T[:, :1]
    for t in range(2):
        place = 2 * row + t
        off_diagonal = jnp.where(place != col, 1.0, 0.0)
        chosen = (pair_pick & (position == place)).astype(jnp.float32) * off_diagonal
        column_terms += dot(dot(chosen, values), cov[t * tile : (t + 1) * tile])
        weighted = values * (position_column == place.astype(jnp.float32)).astype(jnp.float32)
        gram_terms += dot(weighted, row_terms[t * tile : (t + 1) * tile])
    lane = iota((groups, 8, LANES), 2)
    shaped = row_terms.reshape(2, groups, halves, 8, LANES)
    first = jnp.zeros((groups, 8, LANES), jnp.float32)
    for t in range(2):
        for m in range(halves):
            first = jnp.where(lane // SLOTS == t * halves + m, shaped[t, :, m], first)
    out[:, :8] = first
    shaped = column_terms.T.reshape(groups, halves, 8, LANES)
    second = gram_terms.reshape(groups, 8, LANES)
    for m in range(halves):
        second = jnp.where(lane // PAIR_SLOTS == m, shaped[:, m], second)
    out[:, 8:] = second


def make_terms(where, everything, codes, cov, groups):
    return pl.pallas_call(
        terms_kernel,
        out_shape=jax.ShapeDtypeStruct((groups, 16, LANES), jnp.float32),
        in_specs=[pl.BlockSpec(memory_space=pltpu.SMEM), *in_vmem(3)],
        out_specs=pl.BlockSpec(memory_space=pltpu.VMEM),
        compiler_params=params(),
    )(where, everything, codes, cov)


def place_kernel(where, codes, arrived, placed, second):
    nobs = codes.shape[1]
    groups = arrived.shape[0]
    code = slot_codes(codes, where[2])[1]
    lane = iota((8, LANES), 1)
    parts = GROUPS + 1
    lines = [[] for _ in range(parts)]
    for g in range(groups // GROUPS):
        for part in range(parts):
            line = None
            for q in range(GROUPS):
                at, source = (part, arrived[g * GROUPS + q, :8]) if part < GROUPS else (
                    GROUPS - 1,
                    arrived[g * GROUPS + q, 8:],
                )
                shift = (q - at) * SLOTS % LANES
                turned = pltpu.roll(source, shift, 1) if shift else source
                line = turned if line is None else jnp.where(lane // SLOTS == q, turned, line)
            lines[part].append(line)
    former = jnp.concatenate([jnp.concatenate(line, axis=1) for line in lines], axis=0)
    spots = (iota((groups * SLOTS, nobs), 0) == code).astype(jnp.float32)
    result = dot(former, spots)
    placed[...] = result[: 8 * GROUPS]
    gram = result[8 * GROUPS :]
    for r in range(second.shape[0]):
        for t in range(2):
            second[r, t] = arrived[2 * r + t, 8:]
        for part in range(nobs // LANES):
            second[r, 2 + part] = gram[:, part * LANES : (part + 1) * LANES]


def place_rows(where, codes, arrived, tr_size):
    nobs = codes.shape[1]
    return pl.pallas_call(
        place_kernel,
        out_shape=(
            jax.ShapeDtypeStruct((8 * GROUPS, nobs), jnp.float32),
            jax.ShapeDtypeStruct((tr_size, 2 + nobs // LANES, 8, LANES), jnp.float32),
        ),
        in_specs=[pl.BlockSpec(memory_space=pltpu.SMEM), *in_vmem(2)],
        out_specs=tuple(in_vmem(2)),
        compiler_params=params(),
    )(where, codes, arrived)


def gather_kernel(where, codes, placed, arrived, out):
    nobs = codes.shape[1]
    pair_code = slot_codes(codes, where[2])[2]
    lane = iota((8, LANES), 1)
    pairs = arrived.shape[0]
    halves = GROUPS // 2
    lines = []
    for t in range(2):
        for m in range(halves):
            inside = lane // PAIR_SLOTS == m
            lines.append(
                jnp.concatenate([jnp.where(inside, arrived[r, t], 0.0) for r in range(pairs)], axis=1)
            )
    former = jnp.concatenate(lines, axis=0)
    at = iota((pairs * LANES, nobs), 0)
    within = at % LANES
    spot = jnp.where(within < 2 * PAIR_SLOTS, at // LANES * PAIR_SLOTS + within % PAIR_SLOTS, -2)
    spots = (spot == pair_code).astype(jnp.float32)
    out[: 8 * GROUPS] = placed[...] + dot(former, spots)
    for part in range(nobs // LANES):
        total = arrived[0, 2 + part]
        for r in range(1, pairs):
            total = total + arrived[r, 2 + part]
        out[8 * GROUPS :, part * LANES : (part + 1) * LANES] = total


def gather_rows(where, codes, placed, arrived):
    nobs = codes.shape[1]
    return pl.pallas_call(
        gather_kernel,
        out_shape=jax.ShapeDtypeStruct((8 * GROUPS + 8, nobs), jnp.float32),
        in_specs=[pl.BlockSpec(memory_space=pltpu.SMEM), *in_vmem(3)],
        out_specs=pl.BlockSpec(memory_space=pltpu.VMEM),
        compiler_params=params(),
    )(where, codes, placed, arrived)


def inverse_kernel(everything, codes, arrived, out):
    nobs = codes.shape[1]
    tile = everything.shape[1] - LANES
    gram = arrived[:, 8 * GROUPS :].reshape(nobs, nobs)
    both = gram + gram.T
    position = codes[0:1]
    position_column = jnp.broadcast_to(position, (LANES, nobs)).astype(jnp.float32).T[:, :1].astype(jnp.int32)
    errors = everything[:, tile + 1 : tile + 2]
    unit = (iota((nobs, nobs), 0) == iota((nobs, nobs), 1)).astype(jnp.float32)
    innovation = jnp.where(position == position_column, 0.5 * both, both) + unit * errors
    low = jnp.min(errors, keepdims=True)
    sums = jnp.sum(jnp.abs(innovation), axis=1, keepdims=True)
    high = jnp.maximum(jnp.max(sums, keepdims=True), low)
    ratio = (high - low) / (high + low)
    base = 2.0 / (low + high)
    square = ratio * ratio
    scale = 2.0 / (2.0 - square)
    start = (scale * base) * (2.0 * unit - base * innovation)

    def unsettled(carry):
        count, left, _, _ = carry
        return (left > SETTLED) & (count < 64)

    def step(carry):
        count, _, spread, inverse = carry
        gap = spread * spread
        grow = 2.0 / (2.0 - gap)
        shrunk = gap * 0.5 * grow
        rest = 2.0 * unit - dot(innovation, inverse)
        return count + 1, jnp.max(shrunk), shrunk, grow * dot(inverse, rest)

    first = square * 0.5 * scale
    result = lax.while_loop(unsettled, step, (jnp.int32(0), jnp.max(first), first, start))
    out[...] = result[3]


def invert(everything, codes, arrived):
    nobs = codes.shape[1]
    return pl.pallas_call(
        inverse_kernel,
        out_shape=jax.ShapeDtypeStruct((nobs, nobs), jnp.float32),
        in_specs=in_vmem(3),
        out_specs=pl.BlockSpec(memory_space=pltpu.VMEM),
        compiler_params=params(),
        cost_estimate=pl.CostEstimate(
            flops=150 * nobs**3, bytes_accessed=8 * nobs * nobs, transcendentals=0
        ),
    )(everything, codes, arrived)


def update_kernel(keep, cov, arrived, col_cross, inverse, out):
    tile = cov.shape[1]
    share = 4 * GROUPS
    solved = dot(col_cross[...], inverse[...])
    for t in range(2):
        lines = arrived[:, t * share : (t + 1) * share].reshape(tile, -1)
        part = slice(t * tile, (t + 1) * tile)
        out[part] = (cov[part] - dot(lines, solved, ((1,), (1,)))) * keep[t]


def update(keep, cov, arrived, col_cross, inverse):
    return pl.pallas_call(
        update_kernel,
        out_shape=jax.ShapeDtypeStruct(cov.shape, jnp.float32),
        in_specs=[pl.BlockSpec(memory_space=pltpu.SMEM), *in_vmem(4)],
        out_specs=pl.BlockSpec(memory_space=pltpu.VMEM),
        compiler_params=params(),
    )(keep, cov, arrived, col_cross, inverse)


def body(cov, order, stations, obs_values, obs_error):
    rows, tile = cov.shape
    nobs_own = obs_values.shape[1]
    tr_size, tc_size = lax.axis_size(TR), lax.axis_size(TC)
    nobs = nobs_own * tc_size
    share = tile // tc_size
    row = lax.axis_index(TR)
    col = lax.axis_index(TC)

    tail = jnp.stack([stations[0].astype(jnp.float32), obs_error[0]], axis=1)
    packed = jnp.concatenate(
        [obs_values[0], jnp.pad(tail, ((0, 0), (0, LANES - tail.shape[1])))], axis=1
    )
    packed = jnp.broadcast_to(packed[None], (tc_size, *packed.shape))
    everything = exchange(packed, TC).reshape(nobs, tile + LANES)
    codes, rounds = make_codes(everything, order)

    def one_round(number):
        where = jnp.stack([row, col, jnp.int32(number)]).astype(jnp.int32)
        terms = exchange(make_terms(where, everything, codes, cov, tc_size), TC)
        placed, second = place_rows(where, codes, terms, tr_size)
        return gather_rows(where, codes, placed, exchange(second, TR))

    own = lax.fori_loop(1, rounds[0], lambda number, sofar: sofar + one_round(number), one_round(0))

    moves = [
        (r * tc_size + c, (c // 2) * tc_size + 2 * r + c % 2)
        for r in range(tr_size)
        for c in range(tc_size)
    ]
    moved = lax.ppermute(own[: 2 * share], ALL, moves)
    arrived = exchange(jnp.broadcast_to(own[None], (tc_size, *own.shape)), TC)
    near = jnp.broadcast_to(moved.reshape(1, 2, share, nobs), (tr_size, 2, share, nobs))
    col_cross = exchange(near.reshape(2 * tr_size, share, nobs), NEAR).reshape(tile, nobs)
    inverse = invert(everything, codes, arrived)
    places = 2 * row + jnp.arange(2, dtype=jnp.int32)
    row_order = lax.dynamic_slice_in_dim(order, 2 * row, 2)
    col_order = lax.dynamic_slice_in_dim(order, col, 1)
    keep = ((row_order > col_order) | (places == col)).astype(jnp.float32)
    return update(keep, cov, arrived, col_cross, inverse)


def solution(mesh):
    tr_size, tc_size = mesh.shape["tr"], mesh.shape["tc"]
    y_size = 8 if tc_size % 8 == 0 else tc_size
    split = Mesh(
        mesh.devices.reshape(tr_size // 2, 2, tc_size // y_size, y_size // 2, 2), ALL
    )
    return jax.shard_map(
        body,
        mesh=split,
        in_specs=(P(TR, TC), P(), P(None, TC), P(None, TC, None), P(None, TC)),
        out_specs=P(TR, TC),
        check_vma=False,
    )
```

time: 249 us -> 159 us (0.64)
  other arithmetic: 78.9 us -> 2.89 us
  Pallas kernels: 0 us -> 23.6 us
  matrix products: 20.8 us -> 0 us
  local copies, waits for them, and re-layouts: 24.2 us -> 4.27 us
  waiting for transfers between devices: 54.9 us -> 64.8 us
  between operations: 6.27 us -> 0.12 us
    another operation x10 -> x1, other arithmetic: 60.8 us -> 0.08 us  [one_round(): where = jnp.stack([row, col, jnp.int32(number)]).astype(jnp.int32)]
    pallas_call x0 -> x6, Pallas kernels: none -> 23.6 us  [the longest x1 7.26 us: invert(): pl.pallas_call(inverse_kernel, out_shape=jax.ShapeDtypeStruct((nobs, nobs...]
    dot_general x13 -> x0, matrix products: 14.9 us -> none  [dot(): lax.dot_general(former, latter, (dims, ((), ())), precision=precise, pref...]
    another operation x9 -> x0, local copies, waits for them, and re-layouts: 8.11 us -> none
    all_to_all x4, waiting for transfers between devices: 30.8 us -> 38.3 us  [exchange(): return lax.all_to_all(array, axes, 0, 0, tiled=True)]
    another operation x5 -> x0, matrix products: 5.94 us -> none  [the longest x2 3.43 us: body(): factor = jnp.linalg.cholesky(innovation)]
    reshape x8 -> x1, local copies, waits for them, and re-layouts: 5.6 us -> 0.74 us  [make_codes(): order.reshape(-1, 1)]
    add x4 -> x0, other arithmetic: 2.95 us -> none  [the longest x1 1.79 us: body(): innovation = jnp.where(same, 0.5 * both, both) + jnp.diag(errors)]
  transfers between devices with their start and end apart: 5 -> 5, of which waited for: 4 -> 5; matrix products, arithmetic and copies ran while one was open for 34% -> 1% of each run, Pallas kernels for 0% -> 5%
where the time goes in v2:
time: 159 us; the launch traced here: 158 us
  waiting for transfers between devices  64.8 us (41%)
  starting transfers between devices  44 us (28%)
  Pallas kernels  23.6 us (15%)
  blocking collectives  17.8 us (11%)
  local copies, waits for them, and re-layouts  4.27 us (3%)
  other arithmetic  2.89 us (2%)
    all_to_all x4, starting transfers between devices, exchange(): return lax.all_to_all(array, axes, 0, 0, tiled=True)  39.9 us
    all_to_all x4, waiting for transfers between devices, exchange(): return lax.all_to_all(array, axes, 0, 0, tiled=True)  38.3 us
    ppermute x1, waiting for transfers between devices, body(): moved = lax.ppermute(own[:2 * share], ALL, moves)  26.5 us
    all_to_all x1, blocking collectives, exchange(): return lax.all_to_all(array, axes, 0, 0, tiled=True)  17.8 us
    pallas_call x1, Pallas kernels, invert(): pl.pallas_call(inverse_kernel, out_shape=jax.ShapeDtypeStruct((nobs, nobs...  7.26 us
    pallas_call x1, Pallas kernels, make_terms(): pl.pallas_call(terms_kernel, out_shape=jax.ShapeDtypeStruct((groups, 16,...  5.85 us
    pallas_call x1, Pallas kernels, update(): pl.pallas_call(update_kernel, out_shape=jax.ShapeDtypeStruct(cov.shape, j...  5.31 us
    ppermute x1, starting transfers between devices, body(): moved = lax.ppermute(own[:2 * share], ALL, moves)  4.05 us
  transfers between devices with their start and end apart: 5, of which 5 were waited for; matrix products, arithmetic and copies ran while one was open for 1% of the time, Pallas kernels for 5%

profile of v2, /device:TPU:1, one launch (start us, length us, event | category | flops | bytes accessed | tf_op | source)
XLA Modules:
  0.0 158.4 jit_solution(7715184775562808701)
XLA Ops:
  0.0 0.0 copy-start
  0.0 0.8 convert_bitcast_fusion
  0.8 0.7 pad_maximum_fusion
  1.5 0.1 copy.8
  1.6 0.7 select_maximum_fusion
  2.3 0.9 broadcast_in_dim.8
  3.2 10.5 %all-to-all-start.2 = ((f32[32,8,640]{2,1,0:T(8,128)}), f32[32,8,640]{2,1,0:T(8,128)S(1)}, u32[]{:S(2)}, u32[]{:S(2)}) async-start(f32[32,8,640]{2,1,0:T(8,128)} %broadcast_in_dim.8), calls=%async_computation.2 | async-start | bytes 1310720 | tf_op jit(solution)/shard_map/all_to_all | solution.py:33
  13.7 0.7 copy.7.order_column
  14.4 0.1 pad_add_fusion.1.where
  14.5 15.6 %all-to-all-done.2 = f32[32,8,640]{2,1,0:T(8,128)S(1)} async-done(((f32[32,8,640]{2,1,0:T(8,128)}), f32[32,8,640]{2,1,0:T(8,128)S(1)}, u32[]{:S(2)}, u32[]{:S(2)}) %all-to-all-start.2) | async-done | bytes 655392 | tf_op jit(solution)/shard_map/all_to_all | solution.py:33
  30.1 1.1 shard_map.55
  31.1 0.0 copy-done
  31.1 5.8 %shard_map.56 = f32[32,16,128]{2,1,0:T(8,128)S(1)} custom-call(s32[3]{0:T(128)S(1)} %pad_add_fusion.1.where, f32[256,640]{1,0:T(8,128)S(1)} %bitcast.24, s32[8,256]{1,0:T(8,128)S(1)} %get-tuple-element.135.codes, f32[1024,512]{1,0:T(8,128)S(1)} %copy-done), custom_call_target="tpu_custom_call" | custom-call | tf_op jit(solution)/shard_map/pallas_call | solution.py:131
  37.0 17.8 %all_to_all.37.arrived = f32[32,16,128]{2,1,0:T(8,128)S(1)} all-to-all(f32[32,16,128]{2,1,0:T(8,128)S(1)} %shard_map.56), channel_id=1, replica_groups=mesh['z'=8,'k'=2,'x'=4,'yh'=4,'yl'=2] {'x','yh','yl'}, dimensions={0} | all-to-all | bytes 524288 | tf_op jit(solution)/shard_map/all_to_all | solution.py:33
  54.8 2.1 %shard_map.57 = (f32[32,256]{1,0:T(8,128)S(1)}, f32[16,4,8,128]{3,2,1,0:T(8,128)}) custom-call(s32[3]{0:T(128)S(1)} %pad_add_fusion.1.where, s32[8,256]{1,0:T(8,128)S(1)} %get-tuple-element.135.codes, f32[32,16,128]{2,1,0:T(8,128)S(1)} %all_to_all.37.arrived), custom_call_target="tpu_custom_call" | custom-call | tf_op jit(solution)/shard_map/pallas_call | solution.py:173
  56.9 13.9 %all-to-all-start.4 = ((f32[16,4,8,128]{3,2,1,0:T(8,128)}), f32[16,4,8,128]{3,2,1,0:T(8,128)S(1)}, u32[]{:S(2)}, u32[]{:S(2)}) async-start(f32[16,4,8,128]{3,2,1,0:T(8,128)} %get-tuple-element.56), calls=%async_computation.4 | async-start | bytes 524288 | tf_op jit(solution)/shard_map/all_to_all | solution.py:33
  70.9 11.7 %all-to-all-done.4.arrived = f32[16,4,8,128]{3,2,1,0:T(8,128)S(1)} async-done(((f32[16,4,8,128]{3,2,1,0:T(8,128)}), f32[16,4,8,128]{3,2,1,0:T(8,128)S(1)}, u32[]{:S(2)}, u32[]{:S(2)}) %all-to-all-start.4) | async-done | bytes 262176 | tf_op jit(solution)/shard_map/all_to_all | solution.py:33
  82.6 2.0 %shard_map.58 = f32[40,256]{1,0:T(8,128)S(1)} custom-call(s32[3]{0:T(128)S(1)} %pad_add_fusion.1.where, s32[8,256]{1,0:T(8,128)S(1)} %get-tuple-element.135.codes, f32[32,256]{1,0:T(8,128)S(1)} %get-tuple-element.55.placed, f32[16,4,8,128]{3,2,1,0:T(8,128)S(1)} %all-to-all-done.4.arrived), custom_call_target="tpu_custom_call" | custom-call | tf_op jit(solution)/shard_map/pallas_call | solution.py:213
  84.6 0.9 while.10
  85.5 1.1 broadcast_in_dim.9
  86.6 4.4 %all-to-all-start.5 = ((f32[32,40,256]{2,1,0:T(8,128)}), f32[32,40,256]{2,1,0:T(8,128)S(1)}, u32[]{:S(2)}, u32[]{:S(2)}) async-start(f32[32,40,256]{2,1,0:T(8,128)} %broadcast_in_dim.9), calls=%async_computation.5 | async-start | bytes 2621440 | tf_op jit(solution)/shard_map/all_to_all | solution.py:33
  91.1 4.1 %collective-permute-start = (f32[32,256]{1,0:T(8,128)S(1)}, f32[32,256]{1,0:T(8,128)S(1)}, u32[]{:S(2)}, u32[]{:S(2)}) collective-permute-start(f32[32,256]{1,0:T(8,128)S(1)} %slice.3), channel_id=1, source_target_pairs={{0,0},{1,1},{2,32},{3,33},{4,64},{5,65},{6,96},{7,97},{8,128},{9,1... | collective-permute-start | bytes 98312 | tf_op jit(solution)/shard_map/ppermute | solution.py:322
  95.1 26.5 %collective-permute-done = f32[32,256]{1,0:T(8,128)S(1)} collective-permute-done((f32[32,256]{1,0:T(8,128)S(1)}, f32[32,256]{1,0:T(8,128)S(1)}, u32[]{:S(2)}, u32[]{:S(2)}) %collective-permute-start) | collective-permute-done | bytes 32800 | tf_op jit(solution)/shard_map/ppermute | solution.py:322
  121.6 2.7 %all-to-all-done.5.arrived = f32[32,40,256]{2,1,0:T(8,128)S(1)} async-done(((f32[32,40,256]{2,1,0:T(8,128)}), f32[32,40,256]{2,1,0:T(8,128)S(1)}, u32[]{:S(2)}, u32[]{:S(2)}) %all-to-all-start.5) | async-done | bytes 1310752 | tf_op jit(solution)/shard_map/all_to_all | solution.py:33
  124.3 0.9 broadcast_in_dim.22
  125.2 11.1 %all-to-all-start.6 = ((f32[32,16,256]{2,1,0:T(8,128)}), f32[32,16,256]{2,1,0:T(8,128)S(1)}, u32[]{:S(2)}, u32[]{:S(2)}) async-start(f32[32,16,256]{2,1,0:T(8,128)} %bitcast.13), calls=%async_computation.6 | async-start | bytes 1048576 | tf_op jit(solution)/shard_map/all_to_all | solution.py:33
  136.3 0.0 copy-done.1
  136.3 0.6 dynamic_slice.7
  136.8 0.6 or_convert_fusion.keep
  137.4 7.3 %shard_map.59.inverse = f32[256,256]{1,0:T(8,128)S(1)} custom-call(f32[256,640]{1,0:T(8,128)S(1)} %get-tuple-element.162, s32[8,256]{1,0:T(8,128)S(1)} %get-tuple-element.165, f32[32,40,256]{2,1,0:T(8,128)S(1)} %all-to-all-done.5.arrived), custom_call_target="tpu_custom_call" | custom-call | flops 2516582400 | bytes 524288 | tf_op jit(solution)/shard_map/pallas_call | solution.py:260
  144.7 8.4 %all-to-all-done.6 = f32[32,16,256]{2,1,0:T(8,128)S(1)} async-done(((f32[32,16,256]{2,1,0:T(8,128)}), f32[32,16,256]{2,1,0:T(8,128)S(1)}, u32[]{:S(2)}, u32[]{:S(2)}) %all-to-all-start.6) | async-done | bytes 524320 | tf_op jit(solution)/shard_map/all_to_all | solution.py:33
  153.1 5.3 %shard_map.60 = f32[1024,512]{1,0:T(8,128)} custom-call(f32[2]{0:T(128)S(1)} %or_convert_fusion.keep, f32[1024,512]{1,0:T(8,128)} %cov.3, f32[32,40,256]{2,1,0:T(8,128)S(1)} %all-to-all-done.5.arrived, f32[512,256]{1,0:T(8,128)S(1)} %bitcast.22, f32[256,256]{1,0:T(8,128)S(1)} %shard_map.59.inverse), custom_call_target="tpu_custom_call" | custom-call | tf_op jit(solution)/shard_map/pallas_call | solution.py:283
  (2 shorter events, 0.0 us)
Async XLA Ops:
  0.0 31.1 %copy-start = (f32[1024,512]{1,0:T(8,128)S(1)}, f32[1024,512]{1,0:T(8,128)}, u32[]{:S(2)}) copy-start(f32[1024,512]{1,0:T(8,128)} %cov.3) | copy-start | bytes 6291460
  3.2 26.9 %all-to-all-start.2 = ((f32[32,8,640]{2,1,0:T(8,128)}), f32[32,8,640]{2,1,0:T(8,128)S(1)}, u32[]{:S(2)}, u32[]{:S(2)}) async-start(f32[32,8,640]{2,1,0:T(8,128)} %broadcast_in_dim.8), calls=%async_computation.2 | async-start | bytes 1310720 | tf_op jit(solution)/shard_map/all_to_all | solution.py:33
  56.9 25.6 %all-to-all-start.4 = ((f32[16,4,8,128]{3,2,1,0:T(8,128)}), f32[16,4,8,128]{3,2,1,0:T(8,128)S(1)}, u32[]{:S(2)}, u32[]{:S(2)}) async-start(f32[16,4,8,128]{3,2,1,0:T(8,128)} %get-tuple-element.56), calls=%async_computation.4 | async-start | bytes 524288 | tf_op jit(solution)/shard_map/all_to_all | solution.py:33
  86.6 49.6 %copy-start.1 = (s32[32]{0:T(128)S(1)}, s32[32]{0:T(128)}, u32[]{:S(2)}) copy-start(s32[32]{0:T(128)} %param.8) | copy-start | bytes 388
  86.6 37.7 %all-to-all-start.5 = ((f32[32,40,256]{2,1,0:T(8,128)}), f32[32,40,256]{2,1,0:T(8,128)S(1)}, u32[]{:S(2)}, u32[]{:S(2)}) async-start(f32[32,40,256]{2,1,0:T(8,128)} %broadcast_in_dim.9), calls=%async_computation.5 | async-start | bytes 2621440 | tf_op jit(solution)/shard_map/all_to_all | solution.py:33
  91.1 30.6 %collective-permute-start = (f32[32,256]{1,0:T(8,128)S(1)}, f32[32,256]{1,0:T(8,128)S(1)}, u32[]{:S(2)}, u32[]{:S(2)}) collective-permute-start(f32[32,256]{1,0:T(8,128)S(1)} %slice.3), channel_id=1, source_target_pairs={{0,0},{1,1},{2,32},{3,33},{4,64},{5,65},{6,96},{7,97},{8,128},{9,1... | collective-permute-start | bytes 98312 | tf_op jit(solution)/shard_map/ppermute | solution.py:322
  125.2 27.9 %all-to-all-start.6 = ((f32[32,16,256]{2,1,0:T(8,128)}), f32[32,16,256]{2,1,0:T(8,128)S(1)}, u32[]{:S(2)}, u32[]{:S(2)}) async-start(f32[32,16,256]{2,1,0:T(8,128)} %bitcast.13), calls=%async_computation.6 | async-start | bytes 1048576 | tf_op jit(solution)/shard_map/all_to_all | solution.py:33

commit v3 on v2

--- a/solution.py
+++ b/solution.py
@@ -8,6 +8,7 @@
 
 TR = ("z", "k")
 TC = ("x", "yh", "yl")
+Y = ("yh", "yl")
 NEAR = ("z", "k", "yl")
 ALL = ("z", "k", "x", "yh", "yl")
 SLOTS = 32
@@ -25,6 +26,32 @@
     )
 
 
+def halves_of(array):
+    upper = array.astype(jnp.bfloat16)
+    return upper, (array - upper.astype(jnp.float32)).astype(jnp.bfloat16)
+
+
+def short(former, latter, dims=((1,), (0,))):
+    return lax.dot_general(former, latter, (dims, ((), ())), preferred_element_type=jnp.float32)
+
+
+def split_dot(former, latter, dims=((1,), (0,))):
+    small = short(former[0], latter[1], dims) + short(former[1], latter[0], dims)
+    return short(former[0], latter[0], dims) + small
+
+
+def chosen_rows(pick, pair):
+    return tuple(short(pick, part).astype(jnp.bfloat16) for part in pair)
+
+
+def placing_dot(former, spots):
+    upper = former.astype(jnp.bfloat16)
+    rest = former - upper.astype(jnp.float32)
+    middle = rest.astype(jnp.bfloat16)
+    lower = (rest - middle.astype(jnp.float32)).astype(jnp.bfloat16)
+    return short(upper, spots) + (short(middle, spots) + short(lower, spots))
+
+
 def iota(shape, dim):
     return lax.broadcasted_iota(jnp.int32, shape, dim)
 
@@ -43,6 +70,28 @@
 
 def as_row(column):
     return jnp.broadcast_to(column, (column.shape[0], LANES)).T[:1]
+
+
+def pack_kernel(stations, errors, values, out):
+    own, tile = values.shape
+    diagonal = iota((own, own), 0) == iota((own, own), 1)
+    station = jnp.sum(jnp.where(diagonal, stations[...].astype(jnp.float32), 0.0), axis=1, keepdims=True)
+    error = jnp.sum(jnp.where(diagonal, errors[...], 0.0), axis=1, keepdims=True)
+    tail = jnp.where(iota((own, LANES), 1) == 0, station, error)
+    for place in range(out.shape[0]):
+        out[place, :, :tile] = values[...]
+        out[place, :, tile:] = tail
+
+
+def pack(stations, errors, values, copies):
+    own, tile = values.shape
+    return pl.pallas_call(
+        pack_kernel,
+        out_shape=jax.ShapeDtypeStruct((copies, own, tile + LANES), jnp.float32),
+        in_specs=in_vmem(3),
+        out_specs=pl.BlockSpec(memory_space=pltpu.VMEM),
+        compiler_params=params(),
+    )(stations, errors, values)
 
 
 def codes_kernel(everything, order_column, codes, rounds):
@@ -99,20 +148,27 @@
     values = everything[:, :tile]
     position, code, pair_code = slot_codes(codes, number)
     sub = iota((LANES, nobs), 0)
-    pick = (code == col * SLOTS + sub % SLOTS).astype(jnp.float32)
-    column_weights = dot(pick, values)
-    row_terms = dot(cov[...], column_weights, ((1,), (1,)))
+    pick = (code == col * SLOTS + sub % SLOTS).astype(jnp.bfloat16)
+    weights = halves_of(values)
+    covariance = halves_of(cov[...])
+    row_terms = split_dot(covariance, chosen_rows(pick, weights), ((1,), (1,)))
+    parts = halves_of(row_terms)
     pair_pick = (pair_code == row * PAIR_SLOTS + sub % PAIR_SLOTS) & (sub < 2 * PAIR_SLOTS)
     column_terms = jnp.zeros((LANES, tile), jnp.float32)
     gram_terms = jnp.zeros((nobs, LANES), jnp.float32)
     position_column = jnp.broadcast_to(position, (LANES, nobs)).astype(jnp.float32).T[:, :1]
     for t in range(2):
         place = 2 * row + t
+        lines = slice(t * tile, (t + 1) * tile)
         off_diagonal = jnp.where(place != col, 1.0, 0.0)
         chosen = (pair_pick & (position == place)).astype(jnp.float32) * off_diagonal
-        column_terms += dot(dot(chosen, values), cov[t * tile : (t + 1) * tile])
-        weighted = values * (position_column == place.astype(jnp.float32)).astype(jnp.float32)
-        gram_terms += dot(weighted, row_terms[t * tile : (t + 1) * tile])
+        column_terms += split_dot(
+            chosen_rows(chosen.astype(jnp.bfloat16), weights), tuple(part[lines] for part in covariance)
+        )
+        inside = (position_column == place.astype(jnp.float32)).astype(jnp.float32)
+        gram_terms += split_dot(
+            halves_of(values * inside), tuple(part[lines] for part in parts)
+        )
     lane = iota((groups, 8, LANES), 2)
     shaped = row_terms.reshape(2, groups, halves, 8, LANES)
     first = jnp.zeros((groups, 8, LANES), jnp.float32)
@@ -157,8 +213,8 @@
                 line = turned if line is None else jnp.where(lane // SLOTS == q, turned, line)
             lines[part].append(line)
     former = jnp.concatenate([jnp.concatenate(line, axis=1) for line in lines], axis=0)
-    spots = (iota((groups * SLOTS, nobs), 0) == code).astype(jnp.float32)
-    result = dot(former, spots)
+    spots = (iota((groups * SLOTS, nobs), 0) == code).astype(jnp.bfloat16)
+    result = placing_dot(former, spots)
     placed[...] = result[: 8 * GROUPS]
     gram = result[8 * GROUPS :]
     for r in range(second.shape[0]):
@@ -199,8 +255,8 @@
     at = iota((pairs * LANES, nobs), 0)
     within = at % LANES
     spot = jnp.where(within < 2 * PAIR_SLOTS, at // LANES * PAIR_SLOTS + within % PAIR_SLOTS, -2)
-    spots = (spot == pair_code).astype(jnp.float32)
-    out[: 8 * GROUPS] = placed[...] + dot(former, spots)
+    spots = (spot == pair_code).astype(jnp.bfloat16)
+    out[: 8 * GROUPS] = placed[...] + placing_dot(former, spots)
     for part in range(nobs // LANES):
         total = arrived[0, 2 + part]
         for r in range(1, pairs):
@@ -272,11 +328,11 @@
 def update_kernel(keep, cov, arrived, col_cross, inverse, out):
     tile = cov.shape[1]
     share = 4 * GROUPS
-    solved = dot(col_cross[...], inverse[...])
+    solved = halves_of(split_dot(halves_of(col_cross[...]), halves_of(inverse[...])))
     for t in range(2):
         lines = arrived[:, t * share : (t + 1) * share].reshape(tile, -1)
         part = slice(t * tile, (t + 1) * tile)
-        out[part] = (cov[part] - dot(lines, solved, ((1,), (1,)))) * keep[t]
+        out[part] = (cov[part] - split_dot(halves_of(lines), solved, ((1,), (1,)))) * keep[t]
 
 
 def update(keep, cov, arrived, col_cross, inverse):
@@ -298,11 +354,7 @@
     row = lax.axis_index(TR)
     col = lax.axis_index(TC)
 
-    tail = jnp.stack([stations[0].astype(jnp.float32), obs_error[0]], axis=1)
-    packed = jnp.concatenate(
-        [obs_values[0], jnp.pad(tail, ((0, 0), (0, LANES - tail.shape[1])))], axis=1
-    )
-    packed = jnp.broadcast_to(packed[None], (tc_size, *packed.shape))
+    packed = pack(stations, obs_error, obs_values[0], tc_size)
     everything = exchange(packed, TC).reshape(nobs, tile + LANES)
     codes, rounds = make_codes(everything, order)
 
@@ -320,7 +372,12 @@
         for c in range(tc_size)
     ]
     moved = lax.ppermute(own[: 2 * share], ALL, moves)
-    arrived = exchange(jnp.broadcast_to(own[None], (tc_size, *own.shape)), TC)
+    arrived = own
+    for axes in (Y, "x"):
+        count = lax.axis_size(axes)
+        arrived = exchange(jnp.broadcast_to(arrived[None], (count, *arrived.shape)), axes)
+    arrived = arrived.reshape(tc_size, *own.shape)
+    moved, arrived = lax.optimization_barrier((moved, arrived))
     near = jnp.broadcast_to(moved.reshape(1, 2, share, nobs), (tr_size, 2, share, nobs))
     col_cross = exchange(near.reshape(2 * tr_size, share, nobs), NEAR).reshape(tile, nobs)
     inverse = invert(everything, codes, arrived)

time: 159 us -> 149 us (0.937)
  blocking collectives: 17.8 us -> 34.6 us
  waiting for transfers between devices: 64.8 us -> 50.9 us
  starting transfers between devices: 44 us -> 35.3 us
  Pallas kernels: 23.6 us -> 20.4 us
  other arithmetic: 2.89 us -> 0.71 us
    ppermute x1, waiting for transfers between devices: 26.5 us -> 4.01 us  [body(): moved = lax.ppermute(own[:2 * share], ALL, moves)]
    all_to_all x1 -> x2, blocking collectives: 17.8 us -> 34.6 us  [exchange(): return lax.all_to_all(array, axes, 0, 0, tiled=True)]
    all_to_all x4, waiting for transfers between devices: 38.3 us -> 46.9 us  [exchange(): return lax.all_to_all(array, axes, 0, 0, tiled=True)]
    all_to_all x4, starting transfers between devices: 39.9 us -> 32.9 us  [exchange(): return lax.all_to_all(array, axes, 0, 0, tiled=True)]
    pallas_call x1, Pallas kernels: 5.85 us -> 3.68 us  [make_terms(): pl.pallas_call(terms_kernel, out_shape=jax.ShapeDtypeStruct((groups, 16,...]
    unnamed x5 -> x10, local copies, waits for them, and re-layouts: 0.09 us -> 2.03 us
    ppermute x1, starting transfers between devices: 4.05 us -> 2.41 us  [body(): moved = lax.ppermute(own[:2 * share], ALL, moves)]
where the time goes in v3:
time: 149 us; the launch traced here: 148 us
  waiting for transfers between devices  50.9 us (34%)
  starting transfers between devices  35.3 us (24%)
  blocking collectives  34.6 us (23%)
  Pallas kernels  20.4 us (14%)
  local copies, waits for them, and re-layouts  5.41 us (4%)
    all_to_all x4, waiting for transfers between devices, exchange(): return lax.all_to_all(array, axes, 0, 0, tiled=True)  46.9 us
    all_to_all x2, blocking collectives, exchange(): return lax.all_to_all(array, axes, 0, 0, tiled=True)  34.6 us
    all_to_all x4, starting transfers between devices, exchange(): return lax.all_to_all(array, axes, 0, 0, tiled=True)  32.9 us
    pallas_call x1, Pallas kernels, invert(): pl.pallas_call(inverse_kernel, out_shape=jax.ShapeDtypeStruct((nobs, nobs...  7.26 us
    pallas_call x1, Pallas kernels, update(): pl.pallas_call(update_kernel, out_shape=jax.ShapeDtypeStruct(cov.shape, j...  4.19 us
    ppermute x1, waiting for transfers between devices, body(): moved = lax.ppermute(own[:2 * share], ALL, moves)  4.01 us
    pallas_call x1, Pallas kernels, make_terms(): pl.pallas_call(terms_kernel, out_shape=jax.ShapeDtypeStruct((groups, 16,...  3.68 us
  transfers between devices with their start and end apart: 5, of which 5 were waited for; matrix products, arithmetic and copies ran while one was open for 1% of the time, Pallas kernels for 5%

profile of v3, /device:TPU:1, one launch (start us, length us, event | category | flops | bytes accessed | tf_op | source)
XLA Modules:
  0.0 148.0 jit_solution(963841599636471180)
XLA Ops:
  0.0 0.0 copy-start
  0.0 0.7 copy-done
  0.7 0.7 copy-done.1
  1.4 0.7 copy-done.2
  2.0 0.9 shard_map.55
  3.0 10.5 %all-to-all-start.2 = ((f32[32,8,640]{2,1,0:T(8,128)}), f32[32,8,640]{2,1,0:T(8,128)S(1)}, u32[]{:S(2)}, u32[]{:S(2)}) async-start(f32[32,8,640]{2,1,0:T(8,128)} %shard_map.55), calls=%async_computation.2 | async-start | bytes 1310720 | tf_op jit(solution)/shard_map/all_to_all | solution.py:60
  13.5 0.7 copy.6.order_column
  14.2 0.1 pad_add_fusion.1.where
  14.3 15.6 %all-to-all-done.2 = f32[32,8,640]{2,1,0:T(8,128)S(1)} async-done(((f32[32,8,640]{2,1,0:T(8,128)}), f32[32,8,640]{2,1,0:T(8,128)S(1)}, u32[]{:S(2)}, u32[]{:S(2)}) %all-to-all-start.2) | async-done | bytes 655392 | tf_op jit(solution)/shard_map/all_to_all | solution.py:60
  29.8 1.1 shard_map.56
  30.9 0.0 copy-done.3
  30.9 3.7 %shard_map.57 = f32[32,16,128]{2,1,0:T(8,128)S(1)} custom-call(s32[3]{0:T(128)S(1)} %pad_add_fusion.1.where, f32[256,640]{1,0:T(8,128)S(1)} %bitcast.25, s32[8,256]{1,0:T(8,128)S(1)} %get-tuple-element.139.codes, f32[1024,512]{1,0:T(8,128)S(1)} %copy-done.3), custom_call_target="tpu_custom_call" | custom-call | tf_op jit(solution)/shard_map/pallas_call | solution.py:187
  34.6 17.8 %all_to_all.42.arrived = f32[32,16,128]{2,1,0:T(8,128)S(1)} all-to-all(f32[32,16,128]{2,1,0:T(8,128)S(1)} %shard_map.57), channel_id=1, replica_groups=mesh['z'=8,'k'=2,'x'=4,'yh'=4,'yl'=2] {'x','yh','yl'}, dimensions={0} | all-to-all | bytes 524288 | tf_op jit(solution)/shard_map/all_to_all | solution.py:60
  52.5 1.7 %shard_map.58 = (f32[32,256]{1,0:T(8,128)S(1)}, f32[16,4,8,128]{3,2,1,0:T(8,128)}) custom-call(s32[3]{0:T(128)S(1)} %pad_add_fusion.1.where, s32[8,256]{1,0:T(8,128)S(1)} %get-tuple-element.139.codes, f32[32,16,128]{2,1,0:T(8,128)S(1)} %all_to_all.42.arrived), custom_call_target="tpu_custom_call" | custom-call | tf_op jit(solution)/shard_map/pallas_call | solution.py:229
  54.2 13.9 %all-to-all-start.4 = ((f32[16,4,8,128]{3,2,1,0:T(8,128)}), f32[16,4,8,128]{3,2,1,0:T(8,128)S(1)}, u32[]{:S(2)}, u32[]{:S(2)}) async-start(f32[16,4,8,128]{3,2,1,0:T(8,128)} %get-tuple-element.58), calls=%async_computation.4 | async-start | bytes 524288 | tf_op jit(solution)/shard_map/all_to_all | solution.py:60
  68.1 11.7 %all-to-all-done.4.arrived = f32[16,4,8,128]{3,2,1,0:T(8,128)S(1)} async-done(((f32[16,4,8,128]{3,2,1,0:T(8,128)}), f32[16,4,8,128]{3,2,1,0:T(8,128)S(1)}, u32[]{:S(2)}, u32[]{:S(2)}) %all-to-all-start.4) | async-done | bytes 262176 | tf_op jit(solution)/shard_map/all_to_all | solution.py:60
  79.8 1.5 %shard_map.59 = f32[40,256]{1,0:T(8,128)S(1)} custom-call(s32[3]{0:T(128)S(1)} %pad_add_fusion.1.where, s32[8,256]{1,0:T(8,128)S(1)} %get-tuple-element.139.codes, f32[32,256]{1,0:T(8,128)S(1)} %get-tuple-element.57.placed, f32[16,4,8,128]{3,2,1,0:T(8,128)S(1)} %all-to-all-done.4.arrived), custom_call_target="tpu_custom_call" | custom-call | tf_op jit(solution)/shard_map/pallas_call | solution.py:269
  81.4 0.6 while.10
  82.1 16.7 %all_to_all.43 = f32[8,40,256]{2,1,0:T(8,128)S(1)} all-to-all(f32[8,40,256]{2,1,0:T(8,128)S(1)} %broadcast_in_dim.8), channel_id=1, replica_groups=mesh['z'=8,'k'=2,'x'=4,'yh'=4,'yl'=2] {'yh','yl'}, dimensions={0} | all-to-all | bytes 655360 | tf_op jit(solution)/shard_map/all_to_all | solution.py:60
  98.8 1.2 broadcast_in_dim.9
  100.0 3.7 %all-to-all-start.6 = ((f32[4,8,40,256]{3,2,1,0:T(8,128)}), f32[4,8,40,256]{3,2,1,0:T(8,128)S(1)}, u32[]{:S(2)}, u32[]{:S(2)}) async-start(f32[4,8,40,256]{3,2,1,0:T(8,128)} %broadcast_in_dim.9), calls=%async_computation.6 | async-start | bytes 2621440 | tf_op jit(solution)/shard_map/all_to_all | solution.py:60
  103.7 2.4 %collective-permute-start = (f32[32,256]{1,0:T(8,128)S(1)}, f32[32,256]{1,0:T(8,128)S(1)}, u32[]{:S(2)}, u32[]{:S(2)}) collective-permute-start(f32[32,256]{1,0:T(8,128)S(1)} %slice.3), channel_id=1, source_target_pairs={{0,0},{1,1},{2,32},{3,33},{4,64},{5,65},{6,96},{7,97},{8,128},{9,1... | collective-permute-start | bytes 98312 | tf_op jit(solution)/shard_map/ppermute | solution.py:374
  106.1 4.0 %collective-permute-done = f32[32,256]{1,0:T(8,128)S(1)} collective-permute-done((f32[32,256]{1,0:T(8,128)S(1)}, f32[32,256]{1,0:T(8,128)S(1)}, u32[]{:S(2)}, u32[]{:S(2)}) %collective-permute-start) | collective-permute-done | bytes 32800 | tf_op jit(solution)/shard_map/ppermute | solution.py:374
  110.1 11.1 %all-to-all-done.6 = f32[4,8,40,256]{3,2,1,0:T(8,128)S(1)} async-done(((f32[4,8,40,256]{3,2,1,0:T(8,128)}), f32[4,8,40,256]{3,2,1,0:T(8,128)S(1)}, u32[]{:S(2)}, u32[]{:S(2)}) %all-to-all-start.6) | async-done | bytes 1310752 | tf_op jit(solution)/shard_map/all_to_all | solution.py:60
  121.2 0.9 broadcast_in_dim.22
  122.1 4.8 %all-to-all-start.7 = ((f32[32,16,256]{2,1,0:T(8,128)}), f32[32,16,256]{2,1,0:T(8,128)S(1)}, u32[]{:S(2)}, u32[]{:S(2)}) async-start(f32[32,16,256]{2,1,0:T(8,128)} %bitcast.12), calls=%async_computation.7 | async-start | bytes 1048576 | tf_op jit(solution)/shard_map/all_to_all | solution.py:60
  126.9 0.0 copy-done.4
  126.9 0.6 dynamic_slice.7
  127.5 0.6 or_convert_fusion.keep
  128.1 7.3 %shard_map.60.inverse = f32[256,256]{1,0:T(8,128)S(1)} custom-call(f32[256,640]{1,0:T(8,128)S(1)} %get-tuple-element.166, s32[8,256]{1,0:T(8,128)S(1)} %get-tuple-element.167, f32[32,40,256]{2,1,0:T(8,128)S(1)} %bitcast.20), custom_call_target="tpu_custom_call" | custom-call | flops 2516582400 | bytes 524288 | tf_op jit(solution)/shard_map/pallas_call | solution.py:316
  135.4 8.5 %all-to-all-done.7 = f32[32,16,256]{2,1,0:T(8,128)S(1)} async-done(((f32[32,16,256]{2,1,0:T(8,128)}), f32[32,16,256]{2,1,0:T(8,128)S(1)}, u32[]{:S(2)}, u32[]{:S(2)}) %all-to-all-start.7) | async-done | bytes 524320 | tf_op jit(solution)/shard_map/all_to_all | solution.py:60
  143.8 4.2 %shard_map.61 = f32[1024,512]{1,0:T(8,128)} custom-call(f32[2]{0:T(128)S(1)} %or_convert_fusion.keep, f32[1024,512]{1,0:T(8,128)} %cov.3, f32[32,40,256]{2,1,0:T(8,128)S(1)} %bitcast.21, f32[512,256]{1,0:T(8,128)S(1)} %bitcast.22, f32[256,256]{1,0:T(8,128)S(1)} %shard_map.60.inverse), custom_call_target="tpu_custom_call" | custom-call | tf_op jit(solution)/shard_map/pallas_call | solution.py:339
  (6 shorter events, 0.0 us)
Async XLA Ops:
  0.0 0.7 copy-start
  0.7 0.7 copy-start.1
  1.4 0.7 copy-start.2
  2.0 28.9 %copy-start.3 = (f32[1024,512]{1,0:T(8,128)S(1)}, f32[1024,512]{1,0:T(8,128)}, u32[]{:S(2)}) copy-start(f32[1024,512]{1,0:T(8,128)} %cov.3) | copy-start | bytes 6291460
  3.0 26.9 %all-to-all-start.2 = ((f32[32,8,640]{2,1,0:T(8,128)}), f32[32,8,640]{2,1,0:T(8,128)S(1)}, u32[]{:S(2)}, u32[]{:S(2)}) async-start(f32[32,8,640]{2,1,0:T(8,128)} %shard_map.55), calls=%async_computation.2 | async-start | bytes 1310720 | tf_op jit(solution)/shard_map/all_to_all | solution.py:60
  54.2 25.6 %all-to-all-start.4 = ((f32[16,4,8,128]{3,2,1,0:T(8,128)}), f32[16,4,8,128]{3,2,1,0:T(8,128)S(1)}, u32[]{:S(2)}, u32[]{:S(2)}) async-start(f32[16,4,8,128]{3,2,1,0:T(8,128)} %get-tuple-element.58), calls=%async_computation.4 | async-start | bytes 524288 | tf_op jit(solution)/shard_map/all_to_all | solution.py:60
  100.0 26.9 %copy-start.4 = (s32[32]{0:T(128)S(1)}, s32[32]{0:T(128)}, u32[]{:S(2)}) copy-start(s32[32]{0:T(128)} %param.8) | copy-start | bytes 388
  100.0 21.2 %all-to-all-start.6 = ((f32[4,8,40,256]{3,2,1,0:T(8,128)}), f32[4,8,40,256]{3,2,1,0:T(8,128)S(1)}, u32[]{:S(2)}, u32[]{:S(2)}) async-start(f32[4,8,40,256]{3,2,1,0:T(8,128)} %broadcast_in_dim.9), calls=%async_computation.6 | async-start | bytes 2621440 | tf_op jit(solution)/shard_map/all_to_all | solution.py:60
  103.7 6.4 %collective-permute-start = (f32[32,256]{1,0:T(8,128)S(1)}, f32[32,256]{1,0:T(8,128)S(1)}, u32[]{:S(2)}, u32[]{:S(2)}) collective-permute-start(f32[32,256]{1,0:T(8,128)S(1)} %slice.3), channel_id=1, source_target_pairs={{0,0},{1,1},{2,32},{3,33},{4,64},{5,65},{6,96},{7,97},{8,128},{9,1... | collective-permute-start | bytes 98312 | tf_op jit(solution)/shard_map/ppermute | solution.py:374
  122.1 21.8 %all-to-all-start.7 = ((f32[32,16,256]{2,1,0:T(8,128)}), f32[32,16,256]{2,1,0:T(8,128)S(1)}, u32[]{:S(2)}, u32[]{:S(2)}) async-start(f32[32,16,256]{2,1,0:T(8,128)} %bitcast.12), calls=%async_computation.7 | async-start | bytes 1048576 | tf_op jit(solution)/shard_map/all_to_all | solution.py:60

commit v4 on v3

--- a/solution.py
+++ b/solution.py
@@ -36,8 +36,11 @@
 
 
 def split_dot(former, latter, dims=((1,), (0,))):
-    small = short(former[0], latter[1], dims) + short(former[1], latter[0], dims)
-    return short(former[0], latter[0], dims) + small
+    return short(
+        jnp.concatenate([former[0], former[1], former[0]], axis=dims[0][0]),
+        jnp.concatenate([latter[0], latter[0], latter[1]], axis=dims[1][0]),
+        dims,
+    )
 
 
 def chosen_rows(pick, pair):
@@ -72,7 +75,17 @@
     return jnp.broadcast_to(column, (column.shape[0], LANES)).T[:1]
 
 
-def pack_kernel(stations, errors, values, out):
+def pack_kernel(stations_at, errors_at, values_at, out, stations, errors, values, arrived):
+    copies = [
+        pltpu.make_async_copy(source, held, arrived.at[number])
+        for number, (source, held) in enumerate(
+            ((stations_at, stations), (errors_at, errors), (values_at, values))
+        )
+    ]
+    for copy in copies:
+        copy.start()
+    for copy in copies:
+        copy.wait()
     own, tile = values.shape
     diagonal = iota((own, own), 0) == iota((own, own), 1)
     station = jnp.sum(jnp.where(diagonal, stations[...].astype(jnp.float32), 0.0), axis=1, keepdims=True)
@@ -88,8 +101,14 @@
     return pl.pallas_call(
         pack_kernel,
         out_shape=jax.ShapeDtypeStruct((copies, own, tile + LANES), jnp.float32),
-        in_specs=in_vmem(3),
+        in_specs=[pl.BlockSpec(memory_space=pltpu.HBM)] * 3,
         out_specs=pl.BlockSpec(memory_space=pltpu.VMEM),
+        scratch_shapes=[
+            pltpu.VMEM(stations.shape, jnp.int32),
+            pltpu.VMEM(errors.shape, jnp.float32),
+            pltpu.VMEM(values.shape, jnp.float32),
+            pltpu.SemaphoreType.DMA((3,)),
+        ],
         compiler_params=params(),
     )(stations, errors, values)
 
@@ -275,10 +294,19 @@
     )(where, codes, placed, arrived)
 
 
-def inverse_kernel(everything, codes, arrived, out):
+def source_of(place, away, count):
+    return lax.rem(place + count - away, count)
+
+
+def inverse_kernel(where, everything, codes, *refs):
+    pieces, (out, grid, rest) = refs[:-3], refs[-3:]
+    for away, piece in enumerate(pieces):
+        lines = piece[:, 8 * GROUPS :].reshape(-1, codes.shape[1])
+        start = source_of(where[3], away, len(pieces)) * lines.shape[0]
+        grid[pl.ds(pl.multiple_of(start, 8), lines.shape[0])] = lines
     nobs = codes.shape[1]
     tile = everything.shape[1] - LANES
-    gram = arrived[:, 8 * GROUPS :].reshape(nobs, nobs)
+    gram = grid[...]
     both = gram + gram.T
     position = codes[0:1]
     position_column = jnp.broadcast_to(position, (LANES, nobs)).astype(jnp.float32).T[:, :1].astype(jnp.int32)
@@ -292,57 +320,97 @@
     base = 2.0 / (low + high)
     square = ratio * ratio
     scale = 2.0 / (2.0 - square)
-    start = (scale * base) * (2.0 * unit - base * innovation)
+    out[...] = (scale * base) * (2.0 * unit - base * innovation)
+    cautious = jnp.max(high - 1000.0 * low) > 0.0
+    parts = halves_of(innovation)
 
     def unsettled(carry):
-        count, left, _, _ = carry
+        count, left, _ = carry
         return (left > SETTLED) & (count < 64)
 
     def step(carry):
-        count, _, spread, inverse = carry
+        count, left, spread = carry
         gap = spread * spread
         grow = 2.0 / (2.0 - gap)
         shrunk = gap * 0.5 * grow
-        rest = 2.0 * unit - dot(innovation, inverse)
-        return count + 1, jnp.max(shrunk), shrunk, grow * dot(inverse, rest)
+        exact = cautious | (left < 1e-3)
+
+        @pl.when(exact)
+        def _():
+            rest[...] = unit - dot(innovation, out[...])
+
+        @pl.when(jnp.logical_not(exact))
+        def _():
+            rest[...] = unit - split_dot(parts, halves_of(out[...]))
+
+        @pl.when(cautious)
+        def _():
+            out[...] = grow * (out[...] + dot(out[...], rest[...]))
+
+        @pl.when(jnp.logical_not(cautious))
+        def _():
+            out[...] = grow * (out[...] + split_dot(halves_of(out[...]), halves_of(rest[...])))
+
+        return count + 1, jnp.max(shrunk), shrunk
 
     first = square * 0.5 * scale
-    result = lax.while_loop(unsettled, step, (jnp.int32(0), jnp.max(first), first, start))
-    out[...] = result[3]
-
-
-def invert(everything, codes, arrived):
+    lax.while_loop(unsettled, step, (jnp.int32(0), jnp.max(first), first))
+
+
+def invert(where, everything, codes, pieces):
     nobs = codes.shape[1]
     return pl.pallas_call(
         inverse_kernel,
         out_shape=jax.ShapeDtypeStruct((nobs, nobs), jnp.float32),
-        in_specs=in_vmem(3),
+        in_specs=[pl.BlockSpec(memory_space=pltpu.SMEM), *in_vmem(2 + len(pieces))],
         out_specs=pl.BlockSpec(memory_space=pltpu.VMEM),
+        scratch_shapes=[pltpu.VMEM((nobs, nobs), jnp.float32)] * 2,
         compiler_params=params(),
         cost_estimate=pl.CostEstimate(
-            flops=150 * nobs**3, bytes_accessed=8 * nobs * nobs, transcendentals=0
+            flops=1500 * nobs**3, bytes_accessed=8 * nobs * nobs, transcendentals=0
         ),
-    )(everything, codes, arrived)
-
-
-def update_kernel(keep, cov, arrived, col_cross, inverse, out):
+    )(where, everything, codes, *pieces)
+
+
+def update_kernel(where, keep, cov, col_cross, inverse, *refs):
+    pieces, (out, held, left) = refs[:-3], refs[-3:]
     tile = cov.shape[1]
     share = 4 * GROUPS
-    solved = halves_of(split_dot(halves_of(col_cross[...]), halves_of(inverse[...])))
-    for t in range(2):
-        lines = arrived[:, t * share : (t + 1) * share].reshape(tile, -1)
-        part = slice(t * tile, (t + 1) * tile)
-        out[part] = (cov[part] - split_dot(halves_of(lines), solved, ((1,), (1,)))) * keep[t]
-
-
-def update(keep, cov, arrived, col_cross, inverse):
+    nobs = inverse.shape[0]
+    solved = split_dot(halves_of(inverse[...]), halves_of(col_cross[...]), ((1,), (1,)))
+    upper, lower = halves_of(solved)
+    latter = jnp.concatenate([upper, upper, lower], axis=0)
+    size = tile // len(pieces)
+    copies = []
+    for away, piece in enumerate(pieces):
+        source = source_of(where[3], away, len(pieces))
+        lines = [piece[:, t * share : (t + 1) * share].reshape(size, nobs) for t in range(2)]
+        upper, lower = halves_of(jnp.concatenate(lines, axis=0))
+        change = short(jnp.concatenate([upper, lower, upper], axis=1), latter)
+        for t in range(2):
+            part = pl.ds(pl.multiple_of(t * tile + source * size, 8), size)
+            number = len(copies)
+            held[number] = (cov[part] - change[t * size : (t + 1) * size]) * keep[t]
+            copies.append(pltpu.make_async_copy(held.at[number], out.at[part], left.at[number]))
+            copies[-1].start()
+    for copy in copies:
+        copy.wait()
+
+
+def update(where, keep, cov, col_cross, inverse, pieces):
+    tile = cov.shape[1]
+    count = 2 * len(pieces)
     return pl.pallas_call(
         update_kernel,
         out_shape=jax.ShapeDtypeStruct(cov.shape, jnp.float32),
-        in_specs=[pl.BlockSpec(memory_space=pltpu.SMEM), *in_vmem(4)],
-        out_specs=pl.BlockSpec(memory_space=pltpu.VMEM),
-        compiler_params=params(),
-    )(keep, cov, arrived, col_cross, inverse)
+        in_specs=[pl.BlockSpec(memory_space=pltpu.SMEM)] * 2 + in_vmem(3 + len(pieces)),
+        out_specs=pl.BlockSpec(memory_space=pl.ANY),
+        scratch_shapes=[
+            pltpu.VMEM((count, 2 * tile // count, tile), jnp.float32),
+            pltpu.SemaphoreType.DMA((count,)),
+        ],
+        compiler_params=params(),
+    )(where, keep, cov, col_cross, inverse, *pieces)
 
 
 def body(cov, order, stations, obs_values, obs_error):
@@ -358,8 +426,12 @@
     everything = exchange(packed, TC).reshape(nobs, tile + LANES)
     codes, rounds = make_codes(everything, order)
 
+    def place_of(number):
+        place = jnp.stack([row, col, jnp.int32(number), lax.axis_index("x")])
+        return place.astype(jnp.int32)
+
     def one_round(number):
-        where = jnp.stack([row, col, jnp.int32(number)]).astype(jnp.int32)
+        where = place_of(number)
         terms = exchange(make_terms(where, everything, codes, cov, tc_size), TC)
         placed, second = place_rows(where, codes, terms, tr_size)
         return gather_rows(where, codes, placed, exchange(second, TR))
@@ -372,20 +444,21 @@
         for c in range(tc_size)
     ]
     moved = lax.ppermute(own[: 2 * share], ALL, moves)
-    arrived = own
-    for axes in (Y, "x"):
-        count = lax.axis_size(axes)
-        arrived = exchange(jnp.broadcast_to(arrived[None], (count, *arrived.shape)), axes)
-    arrived = arrived.reshape(tc_size, *own.shape)
-    moved, arrived = lax.optimization_barrier((moved, arrived))
+    y_size, x_size = lax.axis_size(Y), lax.axis_size("x")
+    near_rows = exchange(jnp.broadcast_to(own[None], (y_size, *own.shape)), Y)
+    moved, near_rows = lax.optimization_barrier((moved, near_rows))
+    pieces = [near_rows] + [
+        lax.ppermute(near_rows, "x", [(x, (x + away) % x_size) for x in range(x_size)])
+        for away in range(1, x_size)
+    ]
     near = jnp.broadcast_to(moved.reshape(1, 2, share, nobs), (tr_size, 2, share, nobs))
     col_cross = exchange(near.reshape(2 * tr_size, share, nobs), NEAR).reshape(tile, nobs)
-    inverse = invert(everything, codes, arrived)
+    inverse = invert(place_of(0), everything, codes, pieces)
     places = 2 * row + jnp.arange(2, dtype=jnp.int32)
     row_order = lax.dynamic_slice_in_dim(order, 2 * row, 2)
     col_order = lax.dynamic_slice_in_dim(order, col, 1)
     keep = ((row_order > col_order) | (places == col)).astype(jnp.float32)
-    return update(keep, cov, arrived, col_cross, inverse)
+    return update(place_of(0), keep, cov, col_cross, inverse, pieces)
 
 
 def solution(mesh):

time: 149 us -> 140 us (0.940)
  blocking collectives: 34.6 us -> 17.9 us
  starting transfers between devices: 35.3 us -> 47.9 us
  Pallas kernels: 20.4 us -> 17.3 us
  waiting for transfers between devices: 50.9 us -> 49.1 us
    all_to_all x2 -> x1, blocking collectives: 34.6 us -> 17.9 us  [exchange(): return lax.all_to_all(array, axes, 0, 0, tiled=True)]
    all_to_all x4, waiting for transfers between devices: 46.9 us -> 38.9 us  [exchange(): return lax.all_to_all(array, axes, 0, 0, tiled=True)]
    ppermute x0 -> x3, starting transfers between devices: none -> 7.85 us  [body(): lax.ppermute(near_rows, 'x', [(x, (x + away) % x_size) for x in range(x_s...]
    ppermute x0 -> x3, waiting for transfers between devices: none -> 4.65 us  [body(): lax.ppermute(near_rows, 'x', [(x, (x + away) % x_size) for x in range(x_s...]
    all_to_all x4, starting transfers between devices: 32.9 us -> 36.1 us  [exchange(): return lax.all_to_all(array, axes, 0, 0, tiled=True)]
    pallas_call x1, Pallas kernels: 7.26 us -> 4.79 us  [invert(): pl.pallas_call(inverse_kernel, out_shape=jax.ShapeDtypeStruct((nobs, nobs...]
    ppermute x1, starting transfers between devices: 2.41 us -> 3.95 us  [body(): moved = lax.ppermute(own[:2 * share], ALL, moves)]
    ppermute x1, waiting for transfers between devices: 4.01 us -> 5.52 us  [body(): moved = lax.ppermute(own[:2 * share], ALL, moves)]
  transfers between devices with their start and end apart: 5 -> 8, of which waited for: 5 -> 6; matrix products, arithmetic and copies ran while one was open for 1% -> 2% of each run, Pallas kernels for 5% -> 3%
where the time goes in v4:
time: 140 us; the launch traced here: 139 us
  waiting for transfers between devices  49.1 us (35%)
  starting transfers between devices  47.9 us (34%)
  blocking collectives  17.9 us (13%)
  Pallas kernels  17.3 us (12%)
  local copies, waits for them, and re-layouts  4.97 us (4%)
    all_to_all x4, waiting for transfers between devices, exchange(): return lax.all_to_all(array, axes, 0, 0, tiled=True)  38.9 us
    all_to_all x4, starting transfers between devices, exchange(): return lax.all_to_all(array, axes, 0, 0, tiled=True)  36.1 us
    all_to_all x1, blocking collectives, exchange(): return lax.all_to_all(array, axes, 0, 0, tiled=True)  17.9 us
    ppermute x3, starting transfers between devices, body(): lax.ppermute(near_rows, 'x', [(x, (x + away) % x_size) for x in range(x_s...  7.85 us
    ppermute x1, waiting for transfers between devices, body(): moved = lax.ppermute(own[:2 * share], ALL, moves)  5.52 us
    pallas_call x1, Pallas kernels, invert(): pl.pallas_call(inverse_kernel, out_shape=jax.ShapeDtypeStruct((nobs, nobs...  4.79 us
    ppermute x3, waiting for transfers between devices, body(): lax.ppermute(near_rows, 'x', [(x, (x + away) % x_size) for x in range(x_s...  4.65 us
    ppermute x1, starting transfers between devices, body(): moved = lax.ppermute(own[:2 * share], ALL, moves)  3.95 us
  transfers between devices with their start and end apart: 8, of which 6 were waited for; matrix products, arithmetic and copies ran while one was open for 2% of the time, Pallas kernels for 3%

profile of v4, /device:TPU:1, one launch (start us, length us, event | category | flops | bytes accessed | tf_op | source)
XLA Modules:
  0.0 138.7 jit_solution(6043261393557472162)
XLA Ops:
  0.0 0.7 copy-done
  0.7 0.7 copy-done.1
  1.4 0.7 copy-done.2
  2.0 1.0 shard_map.55
  3.0 10.5 %all-to-all-start.2 = ((f32[32,8,640]{2,1,0:T(8,128)}), f32[32,8,640]{2,1,0:T(8,128)S(1)}, u32[]{:S(2)}, u32[]{:S(2)}) async-start(f32[32,8,640]{2,1,0:T(8,128)} %shard_map.55), calls=%async_computation.2 | async-start | bytes 1310720 | tf_op jit(solution)/shard_map/all_to_all | solution.py:63
  13.5 0.7 copy.6.order_column
  14.3 0.1 pad_add_fusion.1.where
  14.4 15.6 %all-to-all-done.2 = f32[32,8,640]{2,1,0:T(8,128)S(1)} async-done(((f32[32,8,640]{2,1,0:T(8,128)}), f32[32,8,640]{2,1,0:T(8,128)S(1)}, u32[]{:S(2)}, u32[]{:S(2)}) %all-to-all-start.2) | async-done | bytes 655392 | tf_op jit(solution)/shard_map/all_to_all | solution.py:63
  29.9 1.1 shard_map.56
  31.0 3.3 %shard_map.57 = f32[32,16,128]{2,1,0:T(8,128)S(1)} custom-call(s32[4]{0:T(128)S(1)} %pad_add_fusion.1.where, f32[256,640]{1,0:T(8,128)S(1)} %bitcast.26, s32[8,256]{1,0:T(8,128)S(1)} %get-tuple-element.139.codes, f32[1024,512]{1,0:T(8,128)S(1)} %copy-done.3), custom_call_target="tpu_custom_call" | custom-call | tf_op jit(solution)/shard_map/pallas_call | solution.py:206
  34.3 17.9 %all_to_all.37.arrived = f32[32,16,128]{2,1,0:T(8,128)S(1)} all-to-all(f32[32,16,128]{2,1,0:T(8,128)S(1)} %shard_map.57), channel_id=1, replica_groups=mesh['z'=8,'k'=2,'x'=4,'yh'=4,'yl'=2] {'x','yh','yl'}, dimensions={0} | all-to-all | bytes 524288 | tf_op jit(solution)/shard_map/all_to_all | solution.py:63
  52.2 1.7 %shard_map.58 = (f32[32,256]{1,0:T(8,128)S(1)}, f32[16,4,8,128]{3,2,1,0:T(8,128)}) custom-call(s32[4]{0:T(128)S(1)} %pad_add_fusion.1.where, s32[8,256]{1,0:T(8,128)S(1)} %get-tuple-element.139.codes, f32[32,16,128]{2,1,0:T(8,128)S(1)} %all_to_all.37.arrived), custom_call_target="tpu_custom_call" | custom-call | tf_op jit(solution)/shard_map/pallas_call | solution.py:248
  53.9 13.9 %all-to-all-start.4 = ((f32[16,4,8,128]{3,2,1,0:T(8,128)}), f32[16,4,8,128]{3,2,1,0:T(8,128)S(1)}, u32[]{:S(2)}, u32[]{:S(2)}) async-start(f32[16,4,8,128]{3,2,1,0:T(8,128)} %get-tuple-element.58), calls=%async_computation.4 | async-start | bytes 524288 | tf_op jit(solution)/shard_map/all_to_all | solution.py:63
  67.8 11.7 %all-to-all-done.4.arrived = f32[16,4,8,128]{3,2,1,0:T(8,128)S(1)} async-done(((f32[16,4,8,128]{3,2,1,0:T(8,128)}), f32[16,4,8,128]{3,2,1,0:T(8,128)S(1)}, u32[]{:S(2)}, u32[]{:S(2)}) %all-to-all-start.4) | async-done | bytes 262176 | tf_op jit(solution)/shard_map/all_to_all | solution.py:63
  79.6 1.5 %shard_map.59 = f32[40,256]{1,0:T(8,128)S(1)} custom-call(s32[4]{0:T(128)S(1)} %pad_add_fusion.1.where, s32[8,256]{1,0:T(8,128)S(1)} %get-tuple-element.139.codes, f32[32,256]{1,0:T(8,128)S(1)} %get-tuple-element.57.placed, f32[16,4,8,128]{3,2,1,0:T(8,128)S(1)} %all-to-all-done.4.arrived), custom_call_target="tpu_custom_call" | custom-call | tf_op jit(solution)/shard_map/pallas_call | solution.py:288
  81.1 0.6 while.10
  81.8 0.7 broadcast_in_dim.6
  82.5 3.4 %all-to-all-start.5 = ((f32[8,40,256]{2,1,0:T(8,128)}), f32[8,40,256]{2,1,0:T(8,128)S(1)}, u32[]{:S(2)}, u32[]{:S(2)}) async-start(f32[8,40,256]{2,1,0:T(8,128)} %broadcast_in_dim.6), calls=%async_computation.5 | async-start | bytes 655360 | tf_op jit(solution)/shard_map/all_to_all | solution.py:63
  86.0 3.9 %collective-permute-start = (f32[32,256]{1,0:T(8,128)S(1)}, f32[32,256]{1,0:T(8,128)S(1)}, u32[]{:S(2)}, u32[]{:S(2)}) collective-permute-start(f32[32,256]{1,0:T(8,128)S(1)} %slice.3), channel_id=1, source_target_pairs={{0,0},{1,1},{2,32},{3,33},{4,64},{5,65},{6,96},{7,97},{8,128},{9,1... | collective-permute-start | bytes 98312 | tf_op jit(solution)/shard_map/ppermute | solution.py:446
  89.9 5.5 %collective-permute-done = f32[32,256]{1,0:T(8,128)S(1)} collective-permute-done((f32[32,256]{1,0:T(8,128)S(1)}, f32[32,256]{1,0:T(8,128)S(1)}, u32[]{:S(2)}, u32[]{:S(2)}) %collective-permute-start) | collective-permute-done | bytes 32800 | tf_op jit(solution)/shard_map/ppermute | solution.py:446
  95.4 4.3 %all-to-all-done.5.refs_0_ = f32[8,40,256]{2,1,0:T(8,128)S(1)} async-done(((f32[8,40,256]{2,1,0:T(8,128)}), f32[8,40,256]{2,1,0:T(8,128)S(1)}, u32[]{:S(2)}, u32[]{:S(2)}) %all-to-all-start.5) | async-done | bytes 327712 | tf_op jit(solution)/shard_map/all_to_all | solution.py:63
  99.7 2.9 %collective-permute-start.3 = (f32[8,40,256]{2,1,0:T(8,128)S(1)}, f32[8,40,256]{2,1,0:T(8,128)S(1)}, u32[]{:S(2)}, u32[]{:S(2)}) collective-permute-start(f32[8,40,256]{2,1,0:T(8,128)S(1)} %all-to-all-done.5.refs_0_), channel_id=1, source_target_pairs={{0,24},{8,0},{16,8},{24,16},{1,25},{9,1},{17,9},{25,17},{2,26},{10... | collective-permute-start | bytes 983048 | tf_op jit(solution)/shard_map/ppermute | solution.py:451
  102.6 3.0 %collective-permute-start.2 = (f32[8,40,256]{2,1,0:T(8,128)S(1)}, f32[8,40,256]{2,1,0:T(8,128)S(1)}, u32[]{:S(2)}, u32[]{:S(2)}) collective-permute-start(f32[8,40,256]{2,1,0:T(8,128)S(1)} %all-to-all-done.5.refs_0_), channel_id=1, source_target_pairs={{0,16},{8,24},{16,0},{24,8},{1,17},{9,25},{17,1},{25,9},{2,18},{10... | collective-permute-start | bytes 983048 | tf_op jit(solution)/shard_map/ppermute | solution.py:451
  105.6 1.9 %collective-permute-start.1 = (f32[8,40,256]{2,1,0:T(8,128)S(1)}, f32[8,40,256]{2,1,0:T(8,128)S(1)}, u32[]{:S(2)}, u32[]{:S(2)}) collective-permute-start(f32[8,40,256]{2,1,0:T(8,128)S(1)} %all-to-all-done.5.refs_0_), channel_id=1, source_target_pairs={{0,8},{8,16},{16,24},{24,0},{1,9},{9,17},{17,25},{25,1},{2,10},{10... | collective-permute-start | bytes 983048 | tf_op jit(solution)/shard_map/ppermute | solution.py:451
  107.6 0.6 dynamic_slice.7
  108.2 0.7 or_convert_fusion.keep
  108.9 0.9 broadcast_in_dim.15
  109.8 8.2 %all-to-all-start.6 = ((f32[32,16,256]{2,1,0:T(8,128)}), f32[32,16,256]{2,1,0:T(8,128)S(1)}, u32[]{:S(2)}, u32[]{:S(2)}) async-start(f32[32,16,256]{2,1,0:T(8,128)} %bitcast.13), calls=%async_computation.6 | async-start | bytes 1048576 | tf_op jit(solution)/shard_map/all_to_all | solution.py:63
  118.0 4.6 %collective-permute-done.1.refs_1_ = f32[8,40,256]{2,1,0:T(8,128)S(1)} collective-permute-done((f32[8,40,256]{2,1,0:T(8,128)S(1)}, f32[8,40,256]{2,1,0:T(8,128)S(1)}, u32[]{:S(2)}, u32[]{:S(2)}) %collective-permute-start.1) | collective-permute-done | bytes 327712 | tf_op jit(solution)/shard_map/ppermute | solution.py:451
  122.6 4.8 %shard_map.60.inverse = f32[256,256]{1,0:T(8,128)S(1)} custom-call(s32[4]{0:T(128)S(1)} %pad_add_fusion.1.where, f32[256,640]{1,0:T(8,128)S(1)} %get-tuple-element.175, s32[8,256]{1,0:T(8,128)S(1)} %get-tuple-element.176, f32[8,40,256]{2,1,0:T(8,128)S(1)} %all-to-all-done.5.refs_0_, f32[8,40,256]{2,1,0:T(8,128)S(1)} %collective-permute-done.1.refs_1_, ...), custom_call_target="tpu_custom_call" | custom-call | flops 25165824000 | bytes 524288 | tf_op jit(solution)/shard_map/pallas_call | solution.py:362
  127.4 7.4 %all-to-all-done.6 = f32[32,16,256]{2,1,0:T(8,128)S(1)} async-done(((f32[32,16,256]{2,1,0:T(8,128)}), f32[32,16,256]{2,1,0:T(8,128)S(1)}, u32[]{:S(2)}, u32[]{:S(2)}) %all-to-all-start.6) | async-done | bytes 524320 | tf_op jit(solution)/shard_map/all_to_all | solution.py:63
  134.8 3.9 %shard_map.61 = f32[1024,512]{1,0:T(8,128)} custom-call(s32[4]{0:T(128)S(1)} %pad_add_fusion.1.where, f32[2]{0:T(128)S(1)} %or_convert_fusion.keep, f32[1024,512]{1,0:T(8,128)} %cov.3, f32[512,256]{1,0:T(8,128)S(1)} %bitcast.23, f32[256,256]{1,0:T(8,128)S(1)} %shard_map.60.inverse, f32[8,40,256]{2,1,0:T(8,128)S(1)} %all-to-all-done.5.refs_0_, ...), custom_call_target="tpu_custom_call" | custom-call | tf_op jit(solution)/shard_map/pallas_call | solution.py:403
  (10 shorter events, 0.0 us)
Async XLA Ops:
  0.0 0.7 copy-start
  0.7 0.7 copy-start.1
  1.4 0.7 copy-start.2
  2.0 29.0 %copy-start.3 = (f32[1024,512]{1,0:T(8,128)S(1)}, f32[1024,512]{1,0:T(8,128)}, u32[]{:S(2)}) copy-start(f32[1024,512]{1,0:T(8,128)} %cov.3) | copy-start | bytes 6291460
  3.0 26.9 %all-to-all-start.2 = ((f32[32,8,640]{2,1,0:T(8,128)}), f32[32,8,640]{2,1,0:T(8,128)S(1)}, u32[]{:S(2)}, u32[]{:S(2)}) async-start(f32[32,8,640]{2,1,0:T(8,128)} %shard_map.55), calls=%async_computation.2 | async-start | bytes 1310720 | tf_op jit(solution)/shard_map/all_to_all | solution.py:63
  53.9 25.6 %all-to-all-start.4 = ((f32[16,4,8,128]{3,2,1,0:T(8,128)}), f32[16,4,8,128]{3,2,1,0:T(8,128)S(1)}, u32[]{:S(2)}, u32[]{:S(2)}) async-start(f32[16,4,8,128]{3,2,1,0:T(8,128)} %get-tuple-element.58), calls=%async_computation.4 | async-start | bytes 524288 | tf_op jit(solution)/shard_map/all_to_all | solution.py:63
  81.1 26.5 %copy-start.4 = (s32[32]{0:T(128)S(1)}, s32[32]{0:T(128)}, u32[]{:S(2)}) copy-start(s32[32]{0:T(128)} %param.8) | copy-start | bytes 388
  82.5 17.2 %all-to-all-start.5 = ((f32[8,40,256]{2,1,0:T(8,128)}), f32[8,40,256]{2,1,0:T(8,128)S(1)}, u32[]{:S(2)}, u32[]{:S(2)}) async-start(f32[8,40,256]{2,1,0:T(8,128)} %broadcast_in_dim.6), calls=%async_computation.5 | async-start | bytes 655360 | tf_op jit(solution)/shard_map/all_to_all | solution.py:63
  86.0 9.5 %collective-permute-start = (f32[32,256]{1,0:T(8,128)S(1)}, f32[32,256]{1,0:T(8,128)S(1)}, u32[]{:S(2)}, u32[]{:S(2)}) collective-permute-start(f32[32,256]{1,0:T(8,128)S(1)} %slice.3), channel_id=1, source_target_pairs={{0,0},{1,1},{2,32},{3,33},{4,64},{5,65},{6,96},{7,97},{8,128},{9,1... | collective-permute-start | bytes 98312 | tf_op jit(solution)/shard_map/ppermute | solution.py:446
  99.7 18.3 %collective-permute-start.3 = (f32[8,40,256]{2,1,0:T(8,128)S(1)}, f32[8,40,256]{2,1,0:T(8,128)S(1)}, u32[]{:S(2)}, u32[]{:S(2)}) collective-permute-start(f32[8,40,256]{2,1,0:T(8,128)S(1)} %all-to-all-done.5.refs_0_), channel_id=1, source_target_pairs={{0,24},{8,0},{16,8},{24,16},{1,25},{9,1},{17,9},{25,17},{2,26},{10... | collective-permute-start | bytes 983048 | tf_op jit(solution)/shard_map/ppermute | solution.py:451
  102.6 15.4 %collective-permute-start.2 = (f32[8,40,256]{2,1,0:T(8,128)S(1)}, f32[8,40,256]{2,1,0:T(8,128)S(1)}, u32[]{:S(2)}, u32[]{:S(2)}) collective-permute-start(f32[8,40,256]{2,1,0:T(8,128)S(1)} %all-to-all-done.5.refs_0_), channel_id=1, source_target_pairs={{0,16},{8,24},{16,0},{24,8},{1,17},{9,25},{17,1},{25,9},{2,18},{10... | collective-permute-start | bytes 983048 | tf_op jit(solution)/shard_map/ppermute | solution.py:451
  105.6 17.0 %collective-permute-start.1 = (f32[8,40,256]{2,1,0:T(8,128)S(1)}, f32[8,40,256]{2,1,0:T(8,128)S(1)}, u32[]{:S(2)}, u32[]{:S(2)}) collective-permute-start(f32[8,40,256]{2,1,0:T(8,128)S(1)} %all-to-all-done.5.refs_0_), channel_id=1, source_target_pairs={{0,8},{8,16},{16,24},{24,0},{1,9},{9,17},{17,25},{25,1},{2,10},{10... | collective-permute-start | bytes 983048 | tf_op jit(solution)/shard_map/ppermute | solution.py:451
  109.8 25.1 %all-to-all-start.6 = ((f32[32,16,256]{2,1,0:T(8,128)}), f32[32,16,256]{2,1,0:T(8,128)S(1)}, u32[]{:S(2)}, u32[]{:S(2)}) async-start(f32[32,16,256]{2,1,0:T(8,128)} %bitcast.13), calls=%async_computation.6 | async-start | bytes 1048576 | tf_op jit(solution)/shard_map/all_to_all | solution.py:63

commit v5 on v4

--- a/solution.py
+++ b/solution.py
@@ -9,7 +9,6 @@
 TR = ("z", "k")
 TC = ("x", "yh", "yl")
 Y = ("yh", "yl")
-NEAR = ("z", "k", "yl")
 ALL = ("z", "k", "x", "yh", "yl")
 SLOTS = 32
 PAIR_SLOTS = 48
@@ -75,49 +74,50 @@
     return jnp.broadcast_to(column, (column.shape[0], LANES)).T[:1]
 
 
-def pack_kernel(stations_at, errors_at, values_at, out, stations, errors, values, arrived):
+def pack_kernel(core, stations_at, errors_at, values_at, out, stations, errors, values, arrived):
+    own, width = values.shape
+    cells = pl.ds(pl.multiple_of(core[0] * width, LANES), width)
     copies = [
         pltpu.make_async_copy(source, held, arrived.at[number])
         for number, (source, held) in enumerate(
-            ((stations_at, stations), (errors_at, errors), (values_at, values))
+            ((stations_at, stations), (errors_at, errors), (values_at.at[:, cells], values))
         )
     ]
     for copy in copies:
         copy.start()
     for copy in copies:
         copy.wait()
-    own, tile = values.shape
     diagonal = iota((own, own), 0) == iota((own, own), 1)
     station = jnp.sum(jnp.where(diagonal, stations[...].astype(jnp.float32), 0.0), axis=1, keepdims=True)
     error = jnp.sum(jnp.where(diagonal, errors[...], 0.0), axis=1, keepdims=True)
     tail = jnp.where(iota((own, LANES), 1) == 0, station, error)
     for place in range(out.shape[0]):
-        out[place, :, :tile] = values[...]
-        out[place, :, tile:] = tail
-
-
-def pack(stations, errors, values, copies):
+        out[place, :, :width] = values[...]
+        out[place, :, width:] = tail
+
+
+def pack(core, stations, errors, values, copies):
     own, tile = values.shape
     return pl.pallas_call(
         pack_kernel,
-        out_shape=jax.ShapeDtypeStruct((copies, own, tile + LANES), jnp.float32),
-        in_specs=[pl.BlockSpec(memory_space=pltpu.HBM)] * 3,
+        out_shape=jax.ShapeDtypeStruct((copies, own, tile // 2 + LANES), jnp.float32),
+        in_specs=[pl.BlockSpec(memory_space=pltpu.SMEM)] + [pl.BlockSpec(memory_space=pltpu.HBM)] * 3,
         out_specs=pl.BlockSpec(memory_space=pltpu.VMEM),
         scratch_shapes=[
             pltpu.VMEM(stations.shape, jnp.int32),
             pltpu.VMEM(errors.shape, jnp.float32),
-            pltpu.VMEM(values.shape, jnp.float32),
+            pltpu.VMEM((own, tile // 2), jnp.float32),
             pltpu.SemaphoreType.DMA((3,)),
         ],
-        compiler_params=params(),
-    )(stations, errors, values)
+        compiler_params=pltpu.CompilerParams(vmem_limit_bytes=62 * 1024 * 1024),
+    )(core, stations, errors, values)
 
 
 def codes_kernel(everything, order_column, codes, rounds):
-    nobs = everything.shape[0]
-    tile = everything.shape[1] - LANES
-    station = everything[:, tile : tile + 1].astype(jnp.int32)
-    station_row = as_row(everything[:, tile : tile + 1]).astype(jnp.int32)
+    nobs = everything.shape[1]
+    width = everything.shape[2] - LANES
+    station = everything[0, :, width : width + 1].astype(jnp.int32)
+    station_row = as_row(everything[0, :, width : width + 1]).astype(jnp.int32)
     blocks = order_column.shape[0]
     position = jnp.sum(
         jnp.where(order_column[...] == station_row, iota((blocks, nobs), 0), 0), axis=0, keepdims=True
@@ -138,7 +138,7 @@
     return pl.pallas_call(
         codes_kernel,
         out_shape=(
-            jax.ShapeDtypeStruct((8, everything.shape[0]), jnp.int32),
+            jax.ShapeDtypeStruct((8, everything.shape[1]), jnp.int32),
             jax.ShapeDtypeStruct((1,), jnp.int32),
         ),
         in_specs=in_vmem(2),
@@ -161,10 +161,9 @@
 def terms_kernel(where, everything, codes, cov, out):
     row, col, number = where[0], where[1], where[2]
     rows, tile = cov.shape
-    nobs = everything.shape[0]
+    nobs = everything.shape[1]
     groups = out.shape[0]
-    halves = tile // groups // 8
-    values = everything[:, :tile]
+    values = jnp.concatenate([everything[part, :, : tile // 2] for part in range(2)], axis=1)
     position, code, pair_code = slot_codes(codes, number)
     sub = iota((LANES, nobs), 0)
     pick = (code == col * SLOTS + sub % SLOTS).astype(jnp.bfloat16)
@@ -189,23 +188,27 @@
             halves_of(values * inside), tuple(part[lines] for part in parts)
         )
     lane = iota((groups, 8, LANES), 2)
-    shaped = row_terms.reshape(2, groups, halves, 8, LANES)
-    first = jnp.zeros((groups, 8, LANES), jnp.float32)
-    for t in range(2):
-        for m in range(halves):
-            first = jnp.where(lane // SLOTS == t * halves + m, shaped[t, :, m], first)
+    shaped = row_terms.reshape(groups, GROUPS, 8, LANES)
+    first = shaped[:, 0]
+    for m in range(1, GROUPS):
+        first = jnp.where(lane // SLOTS == m, shaped[:, m], first)
     out[:, :8] = first
-    shaped = column_terms.T.reshape(groups, halves, 8, LANES)
-    second = gram_terms.reshape(groups, 8, LANES)
-    for m in range(halves):
-        second = jnp.where(lane // PAIR_SLOTS == m, shaped[:, m], second)
-    out[:, 8:] = second
+    owners = groups // 2
+    shaped = column_terms.T.reshape(owners, 2, 2, 8, LANES)
+    lane = iota((owners, 8, LANES), 2)
+    gram = gram_terms.reshape(2, owners, 8, LANES)
+    for part in range(2):
+        second = jnp.where(lane // PAIR_SLOTS == 0, shaped[:, part, 0], shaped[:, part, 1])
+        for side in range(2):
+            out[side * owners : (side + 1) * owners, 8 + 8 * part : 16 + 8 * part] = (
+                jnp.where(lane < 2 * PAIR_SLOTS, second, gram[side]) if part == 0 else second
+            )
 
 
 def make_terms(where, everything, codes, cov, groups):
     return pl.pallas_call(
         terms_kernel,
-        out_shape=jax.ShapeDtypeStruct((groups, 16, LANES), jnp.float32),
+        out_shape=jax.ShapeDtypeStruct((groups, 24, LANES), jnp.float32),
         in_specs=[pl.BlockSpec(memory_space=pltpu.SMEM), *in_vmem(3)],
         out_specs=pl.BlockSpec(memory_space=pltpu.VMEM),
         compiler_params=params(),
@@ -225,7 +228,7 @@
             for q in range(GROUPS):
                 at, source = (part, arrived[g * GROUPS + q, :8]) if part < GROUPS else (
                     GROUPS - 1,
-                    arrived[g * GROUPS + q, 8:],
+                    arrived[g * GROUPS + q, 8:16],
                 )
                 shift = (q - at) * SLOTS % LANES
                 turned = pltpu.roll(source, shift, 1) if shift else source
@@ -236,9 +239,10 @@
     result = placing_dot(former, spots)
     placed[...] = result[: 8 * GROUPS]
     gram = result[8 * GROUPS :]
+    side = jnp.where(where[1] >= groups // 2, 1, 0)
     for r in range(second.shape[0]):
-        for t in range(2):
-            second[r, t] = arrived[2 * r + t, 8:]
+        for part in range(2):
+            second[r, part] = arrived[2 * r + side, 8 + 8 * part : 16 + 8 * part]
         for part in range(nobs // LANES):
             second[r, 2 + part] = gram[:, part * LANES : (part + 1) * LANES]
 
@@ -305,12 +309,12 @@
         start = source_of(where[3], away, len(pieces)) * lines.shape[0]
         grid[pl.ds(pl.multiple_of(start, 8), lines.shape[0])] = lines
     nobs = codes.shape[1]
-    tile = everything.shape[1] - LANES
+    width = everything.shape[2] - LANES
     gram = grid[...]
     both = gram + gram.T
     position = codes[0:1]
     position_column = jnp.broadcast_to(position, (LANES, nobs)).astype(jnp.float32).T[:, :1].astype(jnp.int32)
-    errors = everything[:, tile + 1 : tile + 2]
+    errors = everything[0, :, width + 1 : width + 2]
     unit = (iota((nobs, nobs), 0) == iota((nobs, nobs), 1)).astype(jnp.float32)
     innovation = jnp.where(position == position_column, 0.5 * both, both) + unit * errors
     low = jnp.min(errors, keepdims=True)
@@ -375,31 +379,29 @@
 def update_kernel(where, keep, cov, col_cross, inverse, *refs):
     pieces, (out, held, left) = refs[:-3], refs[-3:]
     tile = cov.shape[1]
-    share = 4 * GROUPS
     nobs = inverse.shape[0]
-    solved = split_dot(halves_of(inverse[...]), halves_of(col_cross[...]), ((1,), (1,)))
+    lines = jnp.swapaxes(col_cross[...], 0, 1).reshape(tile, nobs)
+    solved = split_dot(halves_of(inverse[...]), halves_of(lines), ((1,), (1,)))
     upper, lower = halves_of(solved)
     latter = jnp.concatenate([upper, upper, lower], axis=0)
-    size = tile // len(pieces)
+    size = 2 * tile // len(pieces)
     copies = []
     for away, piece in enumerate(pieces):
         source = source_of(where[3], away, len(pieces))
-        lines = [piece[:, t * share : (t + 1) * share].reshape(size, nobs) for t in range(2)]
-        upper, lower = halves_of(jnp.concatenate(lines, axis=0))
+        upper, lower = halves_of(piece[:, : 8 * GROUPS].reshape(size, nobs))
         change = short(jnp.concatenate([upper, lower, upper], axis=1), latter)
-        for t in range(2):
-            part = pl.ds(pl.multiple_of(t * tile + source * size, 8), size)
-            number = len(copies)
-            held[number] = (cov[part] - change[t * size : (t + 1) * size]) * keep[t]
-            copies.append(pltpu.make_async_copy(held.at[number], out.at[part], left.at[number]))
-            copies[-1].start()
+        part = pl.ds(pl.multiple_of(source * size, 8), size)
+        kept = keep[lax.div(source * size, tile)]
+        held[away] = (cov[part] - change) * kept
+        copies.append(pltpu.make_async_copy(held.at[away], out.at[part], left.at[away]))
+        copies[-1].start()
     for copy in copies:
         copy.wait()
 
 
 def update(where, keep, cov, col_cross, inverse, pieces):
     tile = cov.shape[1]
-    count = 2 * len(pieces)
+    count = len(pieces)
     return pl.pallas_call(
         update_kernel,
         out_shape=jax.ShapeDtypeStruct(cov.shape, jnp.float32),
@@ -418,12 +420,12 @@
     nobs_own = obs_values.shape[1]
     tr_size, tc_size = lax.axis_size(TR), lax.axis_size(TC)
     nobs = nobs_own * tc_size
-    share = tile // tc_size
     row = lax.axis_index(TR)
     col = lax.axis_index(TC)
 
-    packed = pack(stations, obs_error, obs_values[0], tc_size)
-    everything = exchange(packed, TC).reshape(nobs, tile + LANES)
+    core = lax.axis_index("k").astype(jnp.int32).reshape(1)
+    packed = pack(core, stations, obs_error, obs_values[0], tc_size)
+    everything = lax.all_gather(exchange(packed, TC), "k").reshape(2, nobs, tile // 2 + LANES)
     codes, rounds = make_codes(everything, order)
 
     def place_of(number):
@@ -439,11 +441,11 @@
     own = lax.fori_loop(1, rounds[0], lambda number, sofar: sofar + one_round(number), one_round(0))
 
     moves = [
-        (r * tc_size + c, (c // 2) * tc_size + 2 * r + c % 2)
+        (r * tc_size + c, c % (tc_size // 2) * tc_size + 2 * r + c // (tc_size // 2))
         for r in range(tr_size)
         for c in range(tc_size)
     ]
-    moved = lax.ppermute(own[: 2 * share], ALL, moves)
+    moved = lax.ppermute(own[: 8 * GROUPS], ALL, moves)
     y_size, x_size = lax.axis_size(Y), lax.axis_size("x")
     near_rows = exchange(jnp.broadcast_to(own[None], (y_size, *own.shape)), Y)
     moved, near_rows = lax.optimization_barrier((moved, near_rows))
@@ -451,9 +453,10 @@
         lax.ppermute(near_rows, "x", [(x, (x + away) % x_size) for x in range(x_size)])
         for away in range(1, x_size)
     ]
-    near = jnp.broadcast_to(moved.reshape(1, 2, share, nobs), (tr_size, 2, share, nobs))
-    col_cross = exchange(near.reshape(2 * tr_size, share, nobs), NEAR).reshape(tile, nobs)
+    col_cross = exchange(jnp.broadcast_to(moved[None], (tr_size // 2, *moved.shape)), "z")
     inverse = invert(place_of(0), everything, codes, pieces)
+    col_cross, inverse = lax.optimization_barrier((col_cross, inverse))
+    col_cross = lax.all_gather(col_cross, "k")
     places = 2 * row + jnp.arange(2, dtype=jnp.int32)
     row_order = lax.dynamic_slice_in_dim(order, 2 * row, 2)
     col_order = lax.dynamic_slice_in_dim(order, col, 1)

time: 140 us -> 133 us (0.950)
  waiting for transfers between devices: 49.1 us -> 40.9 us
  blocking collectives: 17.9 us -> 24.8 us
  starting transfers between devices: 47.9 us -> 44 us
  local copies, waits for them, and re-layouts: 4.97 us -> 2.81 us
    all_to_all x4, waiting for transfers between devices: 38.9 us -> 25.5 us  [exchange(): return lax.all_to_all(array, axes, 0, 0, tiled=True)]
    all_gather x0 -> x2, blocking collectives: none -> 8.34 us  [the longest x1 6.03 us: body(): lax.all_gather(exchange(packed, TC), 'k')]
    all_to_all x4, starting transfers between devices: 36.1 us -> 31.8 us  [exchange(): return lax.all_to_all(array, axes, 0, 0, tiled=True)]
    ppermute x3, waiting for transfers between devices: 4.65 us -> 8.78 us  [body(): lax.ppermute(near_rows, 'x', [(x, (x + away) % x_size) for x in range(x_s...]
    unnamed x10 -> x4, local copies, waits for them, and re-layouts: 2.04 us -> 0.01 us
    all_to_all x1, blocking collectives: 17.9 us -> 16.4 us  [exchange(): return lax.all_to_all(array, axes, 0, 0, tiled=True)]
  transfers between devices with their start and end apart: 8 -> 8, of which waited for: 6 -> 6; matrix products, arithmetic and copies ran while one was open for 2% -> 2% of each run, Pallas kernels for 3% -> 4%
where the time goes in v5:
time: 133 us; the launch traced here: 132 us
  starting transfers between devices  44 us (33%)
  waiting for transfers between devices  40.9 us (31%)
  blocking collectives  24.8 us (19%)
  Pallas kernels  18 us (14%)
  local copies, waits for them, and re-layouts  2.81 us (2%)
    all_to_all x4, starting transfers between devices, exchange(): return lax.all_to_all(array, axes, 0, 0, tiled=True)  31.8 us
    all_to_all x4, waiting for transfers between devices, exchange(): return lax.all_to_all(array, axes, 0, 0, tiled=True)  25.5 us
    all_to_all x1, blocking collectives, exchange(): return lax.all_to_all(array, axes, 0, 0, tiled=True)  16.4 us
    ppermute x3, waiting for transfers between devices, body(): lax.ppermute(near_rows, 'x', [(x, (x + away) % x_size) for x in range(x_s...  8.78 us
    ppermute x3, starting transfers between devices, body(): lax.ppermute(near_rows, 'x', [(x, (x + away) % x_size) for x in range(x_s...  7.84 us
    ppermute x1, waiting for transfers between devices, body(): moved = lax.ppermute(own[:8 * GROUPS], ALL, moves)  6.62 us
    all_gather x1, blocking collectives, body(): lax.all_gather(exchange(packed, TC), 'k')  6.03 us
    pallas_call x1, Pallas kernels, invert(): pl.pallas_call(inverse_kernel, out_shape=jax.ShapeDtypeStruct((nobs, nobs...  4.84 us
  transfers between devices with their start and end apart: 8, of which 6 were waited for; matrix products, arithmetic and copies ran while one was open for 2% of the time, Pallas kernels for 4%

profile of v5, /device:TPU:1, one launch (start us, length us, event | category | flops | bytes accessed | tf_op | source)
XLA Modules:
  0.0 132.0 jit_solution(7774274627983565338)
XLA Ops:
  0.0 1.6 %shard_map.55 = f32[32,8,384]{2,1,0:T(8,128)} custom-call(s32[1]{0:T(128)} %bitcast.8.core, s32[1,8]{1,0:T(1,128)} %stations_at.1, f32[1,8]{1,0:T(1,128)} %errors_at.1, f32[8,512]{1,0:T(8,128)} %bitcast.26), custom_call_target="tpu_custom_call" | custom-call | tf_op jit(solution)/shard_map/pallas_call | solution.py:101
  1.6 0.0 copy-start
  1.6 10.8 %all-to-all-start.2 = ((f32[32,8,384]{2,1,0:T(8,128)}), f32[32,8,384]{2,1,0:T(8,128)}, u32[]{:S(2)}, u32[]{:S(2)}) async-start(f32[32,8,384]{2,1,0:T(8,128)} %shard_map.55), calls=%async_computation.2 | async-start | bytes 786432 | tf_op jit(solution)/shard_map/all_to_all | solution.py:62
  12.4 0.7 copy.7.order_column
  13.1 0.1 pad_add_fusion.1.where
  13.2 10.8 %all-to-all-done.2 = f32[32,8,384]{2,1,0:T(8,128)} async-done(((f32[32,8,384]{2,1,0:T(8,128)}), f32[32,8,384]{2,1,0:T(8,128)}, u32[]{:S(2)}, u32[]{:S(2)}) %all-to-all-start.2) | async-done | bytes 393248 | tf_op jit(solution)/shard_map/all_to_all | solution.py:62
  24.0 6.0 %all-gather = f32[64,8,384]{2,1,0:T(8,128)S(1)} all-gather(f32[32,8,384]{2,1,0:T(8,128)} %all-to-all-done.2), channel_id=2, replica_groups=mesh['z'=8,'k'=2,'x'=4,'yh'=4,'yl'=2] {'k'}, dimensions={0}, use_global_device_ids=true | all-gather | bytes 1179648 | tf_op jit(solution)/shard_map/all_gather | solution.py:428
  30.0 1.1 shard_map.56
  31.1 3.3 %shard_map.57 = f32[32,24,128]{2,1,0:T(8,128)S(1)} custom-call(s32[4]{0:T(128)S(1)} %pad_add_fusion.1.where, f32[2,256,384]{2,1,0:T(8,128)S(1)} %bitcast.24, s32[8,256]{1,0:T(8,128)S(1)} %get-tuple-element.143.codes, f32[1024,512]{1,0:T(8,128)S(1)} %copy-done), custom_call_target="tpu_custom_call" | custom-call | tf_op jit(solution)/shard_map/pallas_call | solution.py:209
  34.5 16.4 %all_to_all.37.arrived = f32[32,24,128]{2,1,0:T(8,128)S(1)} all-to-all(f32[32,24,128]{2,1,0:T(8,128)S(1)} %shard_map.57), channel_id=1, replica_groups=mesh['z'=8,'k'=2,'x'=4,'yh'=4,'yl'=2] {'x','yh','yl'}, dimensions={0} | all-to-all | bytes 786432 | tf_op jit(solution)/shard_map/all_to_all | solution.py:62
  50.9 1.7 %shard_map.58 = (f32[32,256]{1,0:T(8,128)S(1)}, f32[16,4,8,128]{3,2,1,0:T(8,128)}) custom-call(s32[4]{0:T(128)S(1)} %pad_add_fusion.1.where, s32[8,256]{1,0:T(8,128)S(1)} %get-tuple-element.143.codes, f32[32,24,128]{2,1,0:T(8,128)S(1)} %all_to_all.37.arrived), custom_call_target="tpu_custom_call" | custom-call | tf_op jit(solution)/shard_map/pallas_call | solution.py:252
  52.6 13.6 %all-to-all-start.4 = ((f32[16,4,8,128]{3,2,1,0:T(8,128)}), f32[16,4,8,128]{3,2,1,0:T(8,128)S(1)}, u32[]{:S(2)}, u32[]{:S(2)}) async-start(f32[16,4,8,128]{3,2,1,0:T(8,128)} %get-tuple-element.60), calls=%async_computation.4 | async-start | bytes 524288 | tf_op jit(solution)/shard_map/all_to_all | solution.py:62
  66.3 11.7 %all-to-all-done.4.arrived = f32[16,4,8,128]{3,2,1,0:T(8,128)S(1)} async-done(((f32[16,4,8,128]{3,2,1,0:T(8,128)}), f32[16,4,8,128]{3,2,1,0:T(8,128)S(1)}, u32[]{:S(2)}, u32[]{:S(2)}) %all-to-all-start.4) | async-done | bytes 262176 | tf_op jit(solution)/shard_map/all_to_all | solution.py:62
  78.0 1.5 %shard_map.59 = f32[40,256]{1,0:T(8,128)S(1)} custom-call(s32[4]{0:T(128)S(1)} %pad_add_fusion.1.where, s32[8,256]{1,0:T(8,128)S(1)} %get-tuple-element.143.codes, f32[32,256]{1,0:T(8,128)S(1)} %get-tuple-element.59.placed, f32[16,4,8,128]{3,2,1,0:T(8,128)S(1)} %all-to-all-done.4.arrived), custom_call_target="tpu_custom_call" | custom-call | tf_op jit(solution)/shard_map/pallas_call | solution.py:292
  79.6 0.7 while.10
  80.3 0.7 broadcast_in_dim.4
  81.0 4.0 %all-to-all-start.5 = ((f32[8,40,256]{2,1,0:T(8,128)}), f32[8,40,256]{2,1,0:T(8,128)S(1)}, u32[]{:S(2)}, u32[]{:S(2)}) async-start(f32[8,40,256]{2,1,0:T(8,128)} %broadcast_in_dim.4), calls=%async_computation.5 | async-start | bytes 655360 | tf_op jit(solution)/shard_map/all_to_all | solution.py:62
  85.1 4.3 %collective-permute-start = (f32[32,256]{1,0:T(8,128)S(1)}, f32[32,256]{1,0:T(8,128)S(1)}, u32[]{:S(2)}, u32[]{:S(2)}) collective-permute-start(f32[32,256]{1,0:T(8,128)S(1)} %slice.3), channel_id=1, source_target_pairs={{0,0},{1,32},{2,64},{3,96},{4,128},{5,160},{6,192},{7,224},{8,256}... | collective-permute-start | bytes 98312 | tf_op jit(solution)/shard_map/ppermute | solution.py:448
  89.3 6.6 %collective-permute-done = f32[32,256]{1,0:T(8,128)S(1)} collective-permute-done((f32[32,256]{1,0:T(8,128)S(1)}, f32[32,256]{1,0:T(8,128)S(1)}, u32[]{:S(2)}, u32[]{:S(2)}) %collective-permute-start) | collective-permute-done | bytes 32800 | tf_op jit(solution)/shard_map/ppermute | solution.py:448
  96.0 2.9 %all-to-all-done.5.refs_0_ = f32[8,40,256]{2,1,0:T(8,128)S(1)} async-done(((f32[8,40,256]{2,1,0:T(8,128)}), f32[8,40,256]{2,1,0:T(8,128)S(1)}, u32[]{:S(2)}, u32[]{:S(2)}) %all-to-all-start.5) | async-done | bytes 327712 | tf_op jit(solution)/shard_map/all_to_all | solution.py:62
  98.9 2.1 %collective-permute-start.3 = (f32[8,40,256]{2,1,0:T(8,128)S(1)}, f32[8,40,256]{2,1,0:T(8,128)S(1)}, u32[]{:S(2)}, u32[]{:S(2)}) collective-permute-start(f32[8,40,256]{2,1,0:T(8,128)S(1)} %all-to-all-done.5.refs_0_), channel_id=1, source_target_pairs={{0,24},{8,0},{16,8},{24,16},{1,25},{9,1},{17,9},{25,17},{2,26},{10... | collective-permute-start | bytes 983048 | tf_op jit(solution)/shard_map/ppermute | solution.py:453
  101.0 3.9 %collective-permute-start.2 = (f32[8,40,256]{2,1,0:T(8,128)S(1)}, f32[8,40,256]{2,1,0:T(8,128)S(1)}, u32[]{:S(2)}, u32[]{:S(2)}) collective-permute-start(f32[8,40,256]{2,1,0:T(8,128)S(1)} %all-to-all-done.5.refs_0_), channel_id=1, source_target_pairs={{0,16},{8,24},{16,0},{24,8},{1,17},{9,25},{17,1},{25,9},{2,18},{10... | collective-permute-start | bytes 983048 | tf_op jit(solution)/shard_map/ppermute | solution.py:453
  104.8 1.9 %collective-permute-start.1 = (f32[8,40,256]{2,1,0:T(8,128)S(1)}, f32[8,40,256]{2,1,0:T(8,128)S(1)}, u32[]{:S(2)}, u32[]{:S(2)}) collective-permute-start(f32[8,40,256]{2,1,0:T(8,128)S(1)} %all-to-all-done.5.refs_0_), channel_id=1, source_target_pairs={{0,8},{8,16},{16,24},{24,0},{1,9},{9,17},{17,25},{25,1},{2,10},{10... | collective-permute-start | bytes 983048 | tf_op jit(solution)/shard_map/ppermute | solution.py:453
  106.8 0.6 dynamic_slice.7
  107.4 0.7 or_convert_fusion.keep
  108.1 0.7 broadcast_in_dim.5
  108.8 3.4 %all-to-all-start.6 = ((f32[8,32,256]{2,1,0:T(8,128)}), f32[8,32,256]{2,1,0:T(8,128)S(1)}, u32[]{:S(2)}, u32[]{:S(2)}) async-start(f32[8,32,256]{2,1,0:T(8,128)} %broadcast_in_dim.5), calls=%async_computation.6 | async-start | bytes 524288 | tf_op jit(solution)/shard_map/all_to_all | solution.py:62
  112.2 0.7 collective-permute-done.2.refs_2_
  113.0 8.1 %collective-permute-done.1.refs_1_ = f32[8,40,256]{2,1,0:T(8,128)S(1)} collective-permute-done((f32[8,40,256]{2,1,0:T(8,128)S(1)}, f32[8,40,256]{2,1,0:T(8,128)S(1)}, u32[]{:S(2)}, u32[]{:S(2)}) %collective-permute-start.1) | collective-permute-done | bytes 327712 | tf_op jit(solution)/shard_map/ppermute | solution.py:453
  121.0 4.8 %shard_map.60.inverse = f32[256,256]{1,0:T(8,128)S(1)} custom-call(s32[4]{0:T(128)S(1)} %pad_add_fusion.1.where, f32[2,256,384]{2,1,0:T(8,128)S(1)} %get-tuple-element.177, s32[8,256]{1,0:T(8,128)S(1)} %get-tuple-element.178, f32[8,40,256]{2,1,0:T(8,128)S(1)} %all-to-all-done.5.refs_0_, f32[8,40,256]{2,1,0:T(8,128)S(1)} %collective-permute-done.1.refs_1_, ...), custom_call_target="tpu_custom_call" | custom-call | flops 25165824000 | bytes 524288 | tf_op jit(solution)/shard_map/pallas_call | solution.py:366
  125.9 2.3 %all-gather.1 = f32[16,32,256]{2,1,0:T(8,128)S(1)} all-gather(f32[8,32,256]{2,1,0:T(8,128)S(1)} %all-to-all-done.6), channel_id=3, replica_groups=mesh['z'=8,'k'=2,'x'=4,'yh'=4,'yl'=2] {'k'}, dimensions={0}, use_global_device_ids=true | all-gather | bytes 786432 | tf_op jit(solution)/shard_map/all_gather | solution.py:459
  128.2 3.9 %shard_map.61 = f32[1024,512]{1,0:T(8,128)} custom-call(s32[4]{0:T(128)S(1)} %pad_add_fusion.1.where, f32[2]{0:T(128)S(1)} %or_convert_fusion.keep, f32[1024,512]{1,0:T(8,128)} %cov.3, f32[2,8,32,256]{3,2,1,0:T(8,128)S(1)} %bitcast.22, f32[256,256]{1,0:T(8,128)S(1)} %shard_map.60.inverse, f32[8,40,256]{2,1,0:T(8,128)S(1)} %all-to-all-done.5.refs_0_, ...), custom_call_target="tpu_custom_call" | custom-call | tf_op jit(solution)/shard_map/pallas_call | solution.py:405
  (6 shorter events, 0.0 us)
Async XLA Ops:
  1.6 29.5 %copy-start = (f32[1024,512]{1,0:T(8,128)S(1)}, f32[1024,512]{1,0:T(8,128)}, u32[]{:S(2)}) copy-start(f32[1024,512]{1,0:T(8,128)} %cov.3) | copy-start | bytes 6291460
  1.6 22.4 %all-to-all-start.2 = ((f32[32,8,384]{2,1,0:T(8,128)}), f32[32,8,384]{2,1,0:T(8,128)}, u32[]{:S(2)}, u32[]{:S(2)}) async-start(f32[32,8,384]{2,1,0:T(8,128)} %shard_map.55), calls=%async_computation.2 | async-start | bytes 786432 | tf_op jit(solution)/shard_map/all_to_all | solution.py:62
  52.6 25.3 %all-to-all-start.4 = ((f32[16,4,8,128]{3,2,1,0:T(8,128)}), f32[16,4,8,128]{3,2,1,0:T(8,128)S(1)}, u32[]{:S(2)}, u32[]{:S(2)}) async-start(f32[16,4,8,128]{3,2,1,0:T(8,128)} %get-tuple-element.60), calls=%async_computation.4 | async-start | bytes 524288 | tf_op jit(solution)/shard_map/all_to_all | solution.py:62
  79.5 27.2 %copy-start.1 = (s32[32]{0:T(128)S(1)}, s32[32]{0:T(128)}, u32[]{:S(2)}) copy-start(s32[32]{0:T(128)} %param.8) | copy-start | bytes 388
  81.0 17.9 %all-to-all-start.5 = ((f32[8,40,256]{2,1,0:T(8,128)}), f32[8,40,256]{2,1,0:T(8,128)S(1)}, u32[]{:S(2)}, u32[]{:S(2)}) async-start(f32[8,40,256]{2,1,0:T(8,128)} %broadcast_in_dim.4), calls=%async_computation.5 | async-start | bytes 655360 | tf_op jit(solution)/shard_map/all_to_all | solution.py:62
  85.1 10.9 %collective-permute-start = (f32[32,256]{1,0:T(8,128)S(1)}, f32[32,256]{1,0:T(8,128)S(1)}, u32[]{:S(2)}, u32[]{:S(2)}) collective-permute-start(f32[32,256]{1,0:T(8,128)S(1)} %slice.3), channel_id=1, source_target_pairs={{0,0},{1,32},{2,64},{3,96},{4,128},{5,160},{6,192},{7,224},{8,256}... | collective-permute-start | bytes 98312 | tf_op jit(solution)/shard_map/ppermute | solution.py:448
  98.9 13.3 %collective-permute-start.3 = (f32[8,40,256]{2,1,0:T(8,128)S(1)}, f32[8,40,256]{2,1,0:T(8,128)S(1)}, u32[]{:S(2)}, u32[]{:S(2)}) collective-permute-start(f32[8,40,256]{2,1,0:T(8,128)S(1)} %all-to-all-done.5.refs_0_), channel_id=1, source_target_pairs={{0,24},{8,0},{16,8},{24,16},{1,25},{9,1},{17,9},{25,17},{2,26},{10... | collective-permute-start | bytes 983048 | tf_op jit(solution)/shard_map/ppermute | solution.py:453
  101.0 12.0 %collective-permute-start.2 = (f32[8,40,256]{2,1,0:T(8,128)S(1)}, f32[8,40,256]{2,1,0:T(8,128)S(1)}, u32[]{:S(2)}, u32[]{:S(2)}) collective-permute-start(f32[8,40,256]{2,1,0:T(8,128)S(1)} %all-to-all-done.5.refs_0_), channel_id=1, source_target_pairs={{0,16},{8,24},{16,0},{24,8},{1,17},{9,25},{17,1},{25,9},{2,18},{10... | collective-permute-start | bytes 983048 | tf_op jit(solution)/shard_map/ppermute | solution.py:453
  104.8 16.2 %collective-permute-start.1 = (f32[8,40,256]{2,1,0:T(8,128)S(1)}, f32[8,40,256]{2,1,0:T(8,128)S(1)}, u32[]{:S(2)}, u32[]{:S(2)}) collective-permute-start(f32[8,40,256]{2,1,0:T(8,128)S(1)} %all-to-all-done.5.refs_0_), channel_id=1, source_target_pairs={{0,8},{8,16},{16,24},{24,0},{1,9},{9,17},{17,25},{25,1},{2,10},{10... | collective-permute-start | bytes 983048 | tf_op jit(solution)/shard_map/ppermute | solution.py:453
  108.8 17.1 %all-to-all-start.6 = ((f32[8,32,256]{2,1,0:T(8,128)}), f32[8,32,256]{2,1,0:T(8,128)S(1)}, u32[]{:S(2)}, u32[]{:S(2)}) async-start(f32[8,32,256]{2,1,0:T(8,128)} %broadcast_in_dim.5), calls=%async_computation.6 | async-start | bytes 524288 | tf_op jit(solution)/shard_map/all_to_all | solution.py:62

commit v6 on v5

--- a/solution.py
+++ b/solution.py
@@ -10,10 +10,11 @@
 TC = ("x", "yh", "yl")
 Y = ("yh", "yl")
 ALL = ("z", "k", "x", "yh", "yl")
-SLOTS = 32
-PAIR_SLOTS = 48
 LANES = 128
-GROUPS = LANES // SLOTS
+SPAN = 32
+GROUPS = LANES // SPAN
+SLOTS = 24
+PAIR_SLOTS = 32
 SETTLED = 1e-7
 
 precise = lax.Precision.HIGHEST
@@ -150,7 +151,7 @@
 def slot_codes(codes, number):
     position = codes[0:1]
     slot = codes[1:2] - number * SLOTS
-    code = jnp.where((slot >= 0) & (slot < SLOTS), position * SLOTS + slot, -1)
+    code = jnp.where((slot >= 0) & (slot < SLOTS), position * SPAN + slot, -1)
     pair_slot = codes[2:3] - number * PAIR_SLOTS
     pair_code = jnp.where(
         (pair_slot >= 0) & (pair_slot < PAIR_SLOTS), (position >> 1) * PAIR_SLOTS + pair_slot, -1
@@ -166,12 +167,12 @@
     values = jnp.concatenate([everything[part, :, : tile // 2] for part in range(2)], axis=1)
     position, code, pair_code = slot_codes(codes, number)
     sub = iota((LANES, nobs), 0)
-    pick = (code == col * SLOTS + sub % SLOTS).astype(jnp.bfloat16)
+    pick = (code == col * SPAN + sub % SLOTS).astype(jnp.bfloat16)
     weights = halves_of(values)
     covariance = halves_of(cov[...])
     row_terms = split_dot(covariance, chosen_rows(pick, weights), ((1,), (1,)))
     parts = halves_of(row_terms)
-    pair_pick = (pair_code == row * PAIR_SLOTS + sub % PAIR_SLOTS) & (sub < 2 * PAIR_SLOTS)
+    pair_pick = pair_code == row * PAIR_SLOTS + sub % PAIR_SLOTS
     column_terms = jnp.zeros((LANES, tile), jnp.float32)
     gram_terms = jnp.zeros((nobs, LANES), jnp.float32)
     position_column = jnp.broadcast_to(position, (LANES, nobs)).astype(jnp.float32).T[:, :1]
@@ -189,26 +190,24 @@
         )
     lane = iota((groups, 8, LANES), 2)
     shaped = row_terms.reshape(groups, GROUPS, 8, LANES)
-    first = shaped[:, 0]
-    for m in range(1, GROUPS):
+    first = gram_terms.reshape(groups, 8, LANES)
+    for m in range(GROUPS):
         first = jnp.where(lane // SLOTS == m, shaped[:, m], first)
     out[:, :8] = first
     owners = groups // 2
-    shaped = column_terms.T.reshape(owners, 2, 2, 8, LANES)
+    shaped = column_terms.T.reshape(owners, GROUPS, 8, LANES)
     lane = iota((owners, 8, LANES), 2)
-    gram = gram_terms.reshape(2, owners, 8, LANES)
-    for part in range(2):
-        second = jnp.where(lane // PAIR_SLOTS == 0, shaped[:, part, 0], shaped[:, part, 1])
-        for side in range(2):
-            out[side * owners : (side + 1) * owners, 8 + 8 * part : 16 + 8 * part] = (
-                jnp.where(lane < 2 * PAIR_SLOTS, second, gram[side]) if part == 0 else second
-            )
+    second = shaped[:, 0]
+    for m in range(1, GROUPS):
+        second = jnp.where(lane // PAIR_SLOTS == m, shaped[:, m], second)
+    for side in range(2):
+        out[side * owners : (side + 1) * owners, 8:] = second
 
 
 def make_terms(where, everything, codes, cov, groups):
     return pl.pallas_call(
         terms_kernel,
-        out_shape=jax.ShapeDtypeStruct((groups, 24, LANES), jnp.float32),
+        out_shape=jax.ShapeDtypeStruct((groups, 16, LANES), jnp.float32),
         in_specs=[pl.BlockSpec(memory_space=pltpu.SMEM), *in_vmem(3)],
         out_specs=pl.BlockSpec(memory_space=pltpu.VMEM),
         compiler_params=params(),
@@ -226,25 +225,21 @@
         for part in range(parts):
             line = None
             for q in range(GROUPS):
-                at, source = (part, arrived[g * GROUPS + q, :8]) if part < GROUPS else (
-                    GROUPS - 1,
-                    arrived[g * GROUPS + q, 8:16],
-                )
-                shift = (q - at) * SLOTS % LANES
+                source = arrived[g * GROUPS + q, :8]
+                shift = (q * SPAN - part * SLOTS) % LANES
                 turned = pltpu.roll(source, shift, 1) if shift else source
-                line = turned if line is None else jnp.where(lane // SLOTS == q, turned, line)
+                line = turned if line is None else jnp.where(lane // SPAN == q, turned, line)
             lines[part].append(line)
     former = jnp.concatenate([jnp.concatenate(line, axis=1) for line in lines], axis=0)
-    spots = (iota((groups * SLOTS, nobs), 0) == code).astype(jnp.bfloat16)
+    spots = (iota((groups * SPAN, nobs), 0) == code).astype(jnp.bfloat16)
     result = placing_dot(former, spots)
     placed[...] = result[: 8 * GROUPS]
     gram = result[8 * GROUPS :]
     side = jnp.where(where[1] >= groups // 2, 1, 0)
     for r in range(second.shape[0]):
-        for part in range(2):
-            second[r, part] = arrived[2 * r + side, 8 + 8 * part : 16 + 8 * part]
+        second[r, 0] = arrived[2 * r + side, 8:]
         for part in range(nobs // LANES):
-            second[r, 2 + part] = gram[:, part * LANES : (part + 1) * LANES]
+            second[r, 1 + part] = gram[:, part * LANES : (part + 1) * LANES]
 
 
 def place_rows(where, codes, arrived, tr_size):
@@ -253,7 +248,7 @@
         place_kernel,
         out_shape=(
             jax.ShapeDtypeStruct((8 * GROUPS, nobs), jnp.float32),
-            jax.ShapeDtypeStruct((tr_size, 2 + nobs // LANES, 8, LANES), jnp.float32),
+            jax.ShapeDtypeStruct((tr_size, 1 + nobs // LANES, 8, LANES), jnp.float32),
         ),
         in_specs=[pl.BlockSpec(memory_space=pltpu.SMEM), *in_vmem(2)],
         out_specs=tuple(in_vmem(2)),
@@ -266,24 +261,21 @@
     pair_code = slot_codes(codes, where[2])[2]
     lane = iota((8, LANES), 1)
     pairs = arrived.shape[0]
-    halves = GROUPS // 2
     lines = []
-    for t in range(2):
-        for m in range(halves):
-            inside = lane // PAIR_SLOTS == m
-            lines.append(
-                jnp.concatenate([jnp.where(inside, arrived[r, t], 0.0) for r in range(pairs)], axis=1)
-            )
+    for m in range(GROUPS):
+        inside = lane // PAIR_SLOTS == m
+        lines.append(
+            jnp.concatenate([jnp.where(inside, arrived[r, 0], 0.0) for r in range(pairs)], axis=1)
+        )
     former = jnp.concatenate(lines, axis=0)
     at = iota((pairs * LANES, nobs), 0)
-    within = at % LANES
-    spot = jnp.where(within < 2 * PAIR_SLOTS, at // LANES * PAIR_SLOTS + within % PAIR_SLOTS, -2)
+    spot = at // LANES * PAIR_SLOTS + at % PAIR_SLOTS
     spots = (spot == pair_code).astype(jnp.bfloat16)
     out[: 8 * GROUPS] = placed[...] + placing_dot(former, spots)
     for part in range(nobs // LANES):
-        total = arrived[0, 2 + part]
+        total = arrived[0, 1 + part]
         for r in range(1, pairs):
-            total = total + arrived[r, 2 + part]
+            total = total + arrived[r, 1 + part]
         out[8 * GROUPS :, part * LANES : (part + 1) * LANES] = total
 
 

time: 133 us -> 129 us (0.970)
  blocking collectives: 24.8 us -> 22.4 us
    all_to_all x1, blocking collectives: 16.4 us -> 14.3 us  [exchange(): return lax.all_to_all(array, axes, 0, 0, tiled=True)]
  transfers between devices with their start and end apart: 8 -> 8, of which waited for: 6 -> 5; matrix products, arithmetic and copies ran while one was open for 2% -> 2% of each run, Pallas kernels for 4% -> 4%
where the time goes in v6:
time: 129 us; the launch traced here: 128 us
  starting transfers between devices  43.4 us (34%)
  waiting for transfers between devices  39.7 us (31%)
  blocking collectives  22.4 us (17%)
  Pallas kernels  17.8 us (14%)
  local copies, waits for them, and re-layouts  2.82 us (2%)
    all_to_all x4, starting transfers between devices, exchange(): return lax.all_to_all(array, axes, 0, 0, tiled=True)  31.5 us
    all_to_all x4, waiting for transfers between devices, exchange(): return lax.all_to_all(array, axes, 0, 0, tiled=True)  24.3 us
    all_to_all x1, blocking collectives, exchange(): return lax.all_to_all(array, axes, 0, 0, tiled=True)  14.3 us
    ppermute x3, waiting for transfers between devices, body(): lax.ppermute(near_rows, 'x', [(x, (x + away) % x_size) for x in range(x_s...  8.8 us
    ppermute x3, starting transfers between devices, body(): lax.ppermute(near_rows, 'x', [(x, (x + away) % x_size) for x in range(x_s...  7.84 us
    ppermute x1, waiting for transfers between devices, body(): moved = lax.ppermute(own[:8 * GROUPS], ALL, moves)  6.52 us
    all_gather x1, blocking collectives, body(): lax.all_gather(exchange(packed, TC), 'k')  5.82 us
    pallas_call x1, Pallas kernels, invert(): pl.pallas_call(inverse_kernel, out_shape=jax.ShapeDtypeStruct((nobs, nobs...  4.84 us
  transfers between devices with their start and end apart: 8, of which 5 were waited for; matrix products, arithmetic and copies ran while one was open for 2% of the time, Pallas kernels for 4%

profile of v6, /device:TPU:1, one launch (start us, length us, event | category | flops | bytes accessed | tf_op | source)
XLA Modules:
  0.0 127.6 jit_solution(6140294946696079728)
XLA Ops:
  0.0 1.6 %shard_map.55 = f32[32,8,384]{2,1,0:T(8,128)} custom-call(s32[1]{0:T(128)} %bitcast.8.core, s32[1,8]{1,0:T(1,128)} %stations_at.1, f32[1,8]{1,0:T(1,128)} %errors_at.1, f32[8,512]{1,0:T(8,128)} %bitcast.26), custom_call_target="tpu_custom_call" | custom-call | tf_op jit(solution)/shard_map/pallas_call | solution.py:102
  1.6 0.0 copy-start
  1.6 10.6 %all-to-all-start.2 = ((f32[32,8,384]{2,1,0:T(8,128)}), f32[32,8,384]{2,1,0:T(8,128)S(1)}, u32[]{:S(2)}, u32[]{:S(2)}) async-start(f32[32,8,384]{2,1,0:T(8,128)} %shard_map.55), calls=%async_computation.2 | async-start | bytes 786432 | tf_op jit(solution)/shard_map/all_to_all | solution.py:63
  12.3 0.7 copy.7.order_column
  13.0 0.1 pad_add_fusion.1.where
  13.1 10.8 %all-to-all-done.2 = f32[32,8,384]{2,1,0:T(8,128)S(1)} async-done(((f32[32,8,384]{2,1,0:T(8,128)}), f32[32,8,384]{2,1,0:T(8,128)S(1)}, u32[]{:S(2)}, u32[]{:S(2)}) %all-to-all-start.2) | async-done | bytes 393248 | tf_op jit(solution)/shard_map/all_to_all | solution.py:63
  23.9 5.8 %all-gather = f32[64,8,384]{2,1,0:T(8,128)S(1)} all-gather(f32[32,8,384]{2,1,0:T(8,128)S(1)} %all-to-all-done.2), channel_id=2, replica_groups=mesh['z'=8,'k'=2,'x'=4,'yh'=4,'yl'=2] {'k'}, dimensions={0}, use_global_device_ids=true | all-gather | bytes 1179648 | tf_op jit(solution)/shard_map/all_gather | solution.py:420
  29.7 1.1 shard_map.56
  30.8 3.3 %shard_map.57 = f32[32,16,128]{2,1,0:T(8,128)S(1)} custom-call(s32[4]{0:T(128)S(1)} %pad_add_fusion.1.where, f32[2,256,384]{2,1,0:T(8,128)S(1)} %bitcast.24, s32[8,256]{1,0:T(8,128)S(1)} %get-tuple-element.143.codes, f32[1024,512]{1,0:T(8,128)S(1)} %copy-done), custom_call_target="tpu_custom_call" | custom-call | tf_op jit(solution)/shard_map/pallas_call | solution.py:208
  34.1 14.3 %all_to_all.37.arrived = f32[32,16,128]{2,1,0:T(8,128)S(1)} all-to-all(f32[32,16,128]{2,1,0:T(8,128)S(1)} %shard_map.57), channel_id=1, replica_groups=mesh['z'=8,'k'=2,'x'=4,'yh'=4,'yl'=2] {'x','yh','yl'}, dimensions={0} | all-to-all | bytes 524288 | tf_op jit(solution)/shard_map/all_to_all | solution.py:63
  48.5 1.7 %shard_map.58 = (f32[32,256]{1,0:T(8,128)S(1)}, f32[16,3,8,128]{3,2,1,0:T(8,128)}) custom-call(s32[4]{0:T(128)S(1)} %pad_add_fusion.1.where, s32[8,256]{1,0:T(8,128)S(1)} %get-tuple-element.143.codes, f32[32,16,128]{2,1,0:T(8,128)S(1)} %all_to_all.37.arrived), custom_call_target="tpu_custom_call" | custom-call | tf_op jit(solution)/shard_map/pallas_call | solution.py:247
  50.2 14.0 %all-to-all-start.4 = ((f32[16,3,8,128]{3,2,1,0:T(8,128)}), f32[16,3,8,128]{3,2,1,0:T(8,128)S(1)}, u32[]{:S(2)}, u32[]{:S(2)}) async-start(f32[16,3,8,128]{3,2,1,0:T(8,128)} %get-tuple-element.60), calls=%async_computation.4 | async-start | bytes 393216 | tf_op jit(solution)/shard_map/all_to_all | solution.py:63
  64.2 10.3 %all-to-all-done.4.arrived = f32[16,3,8,128]{3,2,1,0:T(8,128)S(1)} async-done(((f32[16,3,8,128]{3,2,1,0:T(8,128)}), f32[16,3,8,128]{3,2,1,0:T(8,128)S(1)}, u32[]{:S(2)}, u32[]{:S(2)}) %all-to-all-start.4) | async-done | bytes 196640 | tf_op jit(solution)/shard_map/all_to_all | solution.py:63
  74.6 1.4 %shard_map.59 = f32[40,256]{1,0:T(8,128)S(1)} custom-call(s32[4]{0:T(128)S(1)} %pad_add_fusion.1.where, s32[8,256]{1,0:T(8,128)S(1)} %get-tuple-element.143.codes, f32[32,256]{1,0:T(8,128)S(1)} %get-tuple-element.59.placed, f32[16,3,8,128]{3,2,1,0:T(8,128)S(1)} %all-to-all-done.4.arrived), custom_call_target="tpu_custom_call" | custom-call | tf_op jit(solution)/shard_map/pallas_call | solution.py:284
  75.9 0.0 copy-start.1
  75.9 0.6 while.10
  76.5 0.7 broadcast_in_dim.4
  77.3 3.4 %all-to-all-start.5 = ((f32[8,40,256]{2,1,0:T(8,128)}), f32[8,40,256]{2,1,0:T(8,128)S(1)}, u32[]{:S(2)}, u32[]{:S(2)}) async-start(f32[8,40,256]{2,1,0:T(8,128)} %broadcast_in_dim.4), calls=%async_computation.5 | async-start | bytes 655360 | tf_op jit(solution)/shard_map/all_to_all | solution.py:63
  80.7 4.0 %collective-permute-start = (f32[32,256]{1,0:T(8,128)S(1)}, f32[32,256]{1,0:T(8,128)S(1)}, u32[]{:S(2)}, u32[]{:S(2)}) collective-permute-start(f32[32,256]{1,0:T(8,128)S(1)} %slice.3), channel_id=1, source_target_pairs={{0,0},{1,32},{2,64},{3,96},{4,128},{5,160},{6,192},{7,224},{8,256}... | collective-permute-start | bytes 98312 | tf_op jit(solution)/shard_map/ppermute | solution.py:440
  84.8 6.5 %collective-permute-done = f32[32,256]{1,0:T(8,128)S(1)} collective-permute-done((f32[32,256]{1,0:T(8,128)S(1)}, f32[32,256]{1,0:T(8,128)S(1)}, u32[]{:S(2)}, u32[]{:S(2)}) %collective-permute-start) | collective-permute-done | bytes 32800 | tf_op jit(solution)/shard_map/ppermute | solution.py:440
  91.3 3.2 %all-to-all-done.5.refs_0_ = f32[8,40,256]{2,1,0:T(8,128)S(1)} async-done(((f32[8,40,256]{2,1,0:T(8,128)}), f32[8,40,256]{2,1,0:T(8,128)S(1)}, u32[]{:S(2)}, u32[]{:S(2)}) %all-to-all-start.5) | async-done | bytes 327712 | tf_op jit(solution)/shard_map/all_to_all | solution.py:63
  94.5 2.1 %collective-permute-start.3 = (f32[8,40,256]{2,1,0:T(8,128)S(1)}, f32[8,40,256]{2,1,0:T(8,128)S(1)}, u32[]{:S(2)}, u32[]{:S(2)}) collective-permute-start(f32[8,40,256]{2,1,0:T(8,128)S(1)} %all-to-all-done.5.refs_0_), channel_id=1, source_target_pairs={{0,24},{8,0},{16,8},{24,16},{1,25},{9,1},{17,9},{25,17},{2,26},{10... | collective-permute-start | bytes 983048 | tf_op jit(solution)/shard_map/ppermute | solution.py:445
  96.6 3.8 %collective-permute-start.2 = (f32[8,40,256]{2,1,0:T(8,128)S(1)}, f32[8,40,256]{2,1,0:T(8,128)S(1)}, u32[]{:S(2)}, u32[]{:S(2)}) collective-permute-start(f32[8,40,256]{2,1,0:T(8,128)S(1)} %all-to-all-done.5.refs_0_), channel_id=1, source_target_pairs={{0,16},{8,24},{16,0},{24,8},{1,17},{9,25},{17,1},{25,9},{2,18},{10... | collective-permute-start | bytes 983048 | tf_op jit(solution)/shard_map/ppermute | solution.py:445
  100.4 1.9 %collective-permute-start.1 = (f32[8,40,256]{2,1,0:T(8,128)S(1)}, f32[8,40,256]{2,1,0:T(8,128)S(1)}, u32[]{:S(2)}, u32[]{:S(2)}) collective-permute-start(f32[8,40,256]{2,1,0:T(8,128)S(1)} %all-to-all-done.5.refs_0_), channel_id=1, source_target_pairs={{0,8},{8,16},{16,24},{24,0},{1,9},{9,17},{17,25},{25,1},{2,10},{10... | collective-permute-start | bytes 983048 | tf_op jit(solution)/shard_map/ppermute | solution.py:445
  102.4 0.6 dynamic_slice.7
  102.9 0.7 or_convert_fusion.keep
  103.7 0.7 broadcast_in_dim.5
  104.4 3.4 %all-to-all-start.6 = ((f32[8,32,256]{2,1,0:T(8,128)}), f32[8,32,256]{2,1,0:T(8,128)S(1)}, u32[]{:S(2)}, u32[]{:S(2)}) async-start(f32[8,32,256]{2,1,0:T(8,128)} %broadcast_in_dim.5), calls=%async_computation.6 | async-start | bytes 524288 | tf_op jit(solution)/shard_map/all_to_all | solution.py:63
  107.8 8.8 %collective-permute-done.1.refs_1_ = f32[8,40,256]{2,1,0:T(8,128)S(1)} collective-permute-done((f32[8,40,256]{2,1,0:T(8,128)S(1)}, f32[8,40,256]{2,1,0:T(8,128)S(1)}, u32[]{:S(2)}, u32[]{:S(2)}) %collective-permute-start.1) | collective-permute-done | bytes 327712 | tf_op jit(solution)/shard_map/ppermute | solution.py:445
  116.6 4.8 %shard_map.60.inverse = f32[256,256]{1,0:T(8,128)S(1)} custom-call(s32[4]{0:T(128)S(1)} %pad_add_fusion.1.where, f32[2,256,384]{2,1,0:T(8,128)S(1)} %get-tuple-element.177, s32[8,256]{1,0:T(8,128)S(1)} %get-tuple-element.178, f32[8,40,256]{2,1,0:T(8,128)S(1)} %all-to-all-done.5.refs_0_, f32[8,40,256]{2,1,0:T(8,128)S(1)} %collective-permute-done.1.refs_1_, ...), custom_call_target="tpu_custom_call" | custom-call | flops 25165824000 | bytes 524288 | tf_op jit(solution)/shard_map/pallas_call | solution.py:358
  121.5 2.3 %all-gather.1 = f32[16,32,256]{2,1,0:T(8,128)S(1)} all-gather(f32[8,32,256]{2,1,0:T(8,128)S(1)} %all-to-all-done.6), channel_id=3, replica_groups=mesh['z'=8,'k'=2,'x'=4,'yh'=4,'yl'=2] {'k'}, dimensions={0}, use_global_device_ids=true | all-gather | bytes 786432 | tf_op jit(solution)/shard_map/all_gather | solution.py:451
  123.8 3.9 %shard_map.61 = f32[1024,512]{1,0:T(8,128)} custom-call(s32[4]{0:T(128)S(1)} %pad_add_fusion.1.where, f32[2]{0:T(128)S(1)} %or_convert_fusion.keep, f32[1024,512]{1,0:T(8,128)} %cov.3, f32[2,8,32,256]{3,2,1,0:T(8,128)S(1)} %bitcast.22, f32[256,256]{1,0:T(8,128)S(1)} %shard_map.60.inverse, f32[8,40,256]{2,1,0:T(8,128)S(1)} %all-to-all-done.5.refs_0_, ...), custom_call_target="tpu_custom_call" | custom-call | tf_op jit(solution)/shard_map/pallas_call | solution.py:397
  (6 shorter events, 0.0 us)
Async XLA Ops:
  1.6 29.2 %copy-start = (f32[1024,512]{1,0:T(8,128)S(1)}, f32[1024,512]{1,0:T(8,128)}, u32[]{:S(2)}) copy-start(f32[1024,512]{1,0:T(8,128)} %cov.3) | copy-start | bytes 6291460
  1.6 22.3 %all-to-all-start.2 = ((f32[32,8,384]{2,1,0:T(8,128)}), f32[32,8,384]{2,1,0:T(8,128)S(1)}, u32[]{:S(2)}, u32[]{:S(2)}) async-start(f32[32,8,384]{2,1,0:T(8,128)} %shard_map.55), calls=%async_computation.2 | async-start | bytes 786432 | tf_op jit(solution)/shard_map/all_to_all | solution.py:63
  50.2 24.4 %all-to-all-start.4 = ((f32[16,3,8,128]{3,2,1,0:T(8,128)}), f32[16,3,8,128]{3,2,1,0:T(8,128)S(1)}, u32[]{:S(2)}, u32[]{:S(2)}) async-start(f32[16,3,8,128]{3,2,1,0:T(8,128)} %get-tuple-element.60), calls=%async_computation.4 | async-start | bytes 393216 | tf_op jit(solution)/shard_map/all_to_all | solution.py:63
  75.9 26.4 %copy-start.1 = (s32[32]{0:T(128)S(1)}, s32[32]{0:T(128)}, u32[]{:S(2)}) copy-start(s32[32]{0:T(128)} %param.8) | copy-start | bytes 388
  77.3 17.2 %all-to-all-start.5 = ((f32[8,40,256]{2,1,0:T(8,128)}), f32[8,40,256]{2,1,0:T(8,128)S(1)}, u32[]{:S(2)}, u32[]{:S(2)}) async-start(f32[8,40,256]{2,1,0:T(8,128)} %broadcast_in_dim.4), calls=%async_computation.5 | async-start | bytes 655360 | tf_op jit(solution)/shard_map/all_to_all | solution.py:63
  80.7 10.6 %collective-permute-start = (f32[32,256]{1,0:T(8,128)S(1)}, f32[32,256]{1,0:T(8,128)S(1)}, u32[]{:S(2)}, u32[]{:S(2)}) collective-permute-start(f32[32,256]{1,0:T(8,128)S(1)} %slice.3), channel_id=1, source_target_pairs={{0,0},{1,32},{2,64},{3,96},{4,128},{5,160},{6,192},{7,224},{8,256}... | collective-permute-start | bytes 98312 | tf_op jit(solution)/shard_map/ppermute | solution.py:440
  94.5 13.3 %collective-permute-start.3 = (f32[8,40,256]{2,1,0:T(8,128)S(1)}, f32[8,40,256]{2,1,0:T(8,128)S(1)}, u32[]{:S(2)}, u32[]{:S(2)}) collective-permute-start(f32[8,40,256]{2,1,0:T(8,128)S(1)} %all-to-all-done.5.refs_0_), channel_id=1, source_target_pairs={{0,24},{8,0},{16,8},{24,16},{1,25},{9,1},{17,9},{25,17},{2,26},{10... | collective-permute-start | bytes 983048 | tf_op jit(solution)/shard_map/ppermute | solution.py:445
  96.6 11.3 %collective-permute-start.2 = (f32[8,40,256]{2,1,0:T(8,128)S(1)}, f32[8,40,256]{2,1,0:T(8,128)S(1)}, u32[]{:S(2)}, u32[]{:S(2)}) collective-permute-start(f32[8,40,256]{2,1,0:T(8,128)S(1)} %all-to-all-done.5.refs_0_), channel_id=1, source_target_pairs={{0,16},{8,24},{16,0},{24,8},{1,17},{9,25},{17,1},{25,9},{2,18},{10... | collective-permute-start | bytes 983048 | tf_op jit(solution)/shard_map/ppermute | solution.py:445
  100.4 16.2 %collective-permute-start.1 = (f32[8,40,256]{2,1,0:T(8,128)S(1)}, f32[8,40,256]{2,1,0:T(8,128)S(1)}, u32[]{:S(2)}, u32[]{:S(2)}) collective-permute-start(f32[8,40,256]{2,1,0:T(8,128)S(1)} %all-to-all-done.5.refs_0_), channel_id=1, source_target_pairs={{0,8},{8,16},{16,24},{24,0},{1,9},{9,17},{17,25},{25,1},{2,10},{10... | collective-permute-start | bytes 983048 | tf_op jit(solution)/shard_map/ppermute | solution.py:445
  104.4 17.1 %all-to-all-start.6 = ((f32[8,32,256]{2,1,0:T(8,128)}), f32[8,32,256]{2,1,0:T(8,128)S(1)}, u32[]{:S(2)}, u32[]{:S(2)}) async-start(f32[8,32,256]{2,1,0:T(8,128)} %broadcast_in_dim.5), calls=%async_computation.6 | async-start | bytes 524288 | tf_op jit(solution)/shard_map/all_to_all | solution.py:63

commit v7 on v6

--- a/solution.py
+++ b/solution.py
@@ -290,13 +290,17 @@
     )(where, codes, placed, arrived)
 
 
+def distances(count):
+    return sorted(range(count), key=lambda away: min(away, count - away))
+
+
 def source_of(place, away, count):
     return lax.rem(place + count - away, count)
 
 
 def inverse_kernel(where, everything, codes, *refs):
     pieces, (out, grid, rest) = refs[:-3], refs[-3:]
-    for away, piece in enumerate(pieces):
+    for away, piece in zip(distances(len(pieces)), pieces):
         lines = piece[:, 8 * GROUPS :].reshape(-1, codes.shape[1])
         start = source_of(where[3], away, len(pieces)) * lines.shape[0]
         grid[pl.ds(pl.multiple_of(start, 8), lines.shape[0])] = lines
@@ -368,7 +372,7 @@
     )(where, everything, codes, *pieces)
 
 
-def update_kernel(where, keep, cov, col_cross, inverse, *refs):
+def update_kernel(where, order, cov, col_cross, inverse, *refs):
     pieces, (out, held, left) = refs[:-3], refs[-3:]
     tile = cov.shape[1]
     nobs = inverse.shape[0]
@@ -378,12 +382,14 @@
     latter = jnp.concatenate([upper, upper, lower], axis=0)
     size = 2 * tile // len(pieces)
     copies = []
-    for away, piece in enumerate(pieces):
+    for away, piece in zip(distances(len(pieces)), pieces):
         source = source_of(where[3], away, len(pieces))
         upper, lower = halves_of(piece[:, : 8 * GROUPS].reshape(size, nobs))
         change = short(jnp.concatenate([upper, lower, upper], axis=1), latter)
         part = pl.ds(pl.multiple_of(source * size, 8), size)
-        kept = keep[lax.div(source * size, tile)]
+        place = 2 * where[0] + lax.div(source * size, tile)
+        live = (order[place] > order[where[1]]) | (place == where[1])
+        kept = jnp.where(live, 1.0, 0.0)
         held[away] = (cov[part] - change) * kept
         copies.append(pltpu.make_async_copy(held.at[away], out.at[part], left.at[away]))
         copies[-1].start()
@@ -391,7 +397,7 @@
         copy.wait()
 
 
-def update(where, keep, cov, col_cross, inverse, pieces):
+def update(where, order, cov, col_cross, inverse, pieces):
     tile = cov.shape[1]
     count = len(pieces)
     return pl.pallas_call(
@@ -404,7 +410,7 @@
             pltpu.SemaphoreType.DMA((count,)),
         ],
         compiler_params=params(),
-    )(where, keep, cov, col_cross, inverse, *pieces)
+    )(where, order, cov, col_cross, inverse, *pieces)
 
 
 def body(cov, order, stations, obs_values, obs_error):
@@ -443,17 +449,13 @@
     moved, near_rows = lax.optimization_barrier((moved, near_rows))
     pieces = [near_rows] + [
         lax.ppermute(near_rows, "x", [(x, (x + away) % x_size) for x in range(x_size)])
-        for away in range(1, x_size)
+        for away in distances(x_size)[1:]
     ]
     col_cross = exchange(jnp.broadcast_to(moved[None], (tr_size // 2, *moved.shape)), "z")
     inverse = invert(place_of(0), everything, codes, pieces)
     col_cross, inverse = lax.optimization_barrier((col_cross, inverse))
     col_cross = lax.all_gather(col_cross, "k")
-    places = 2 * row + jnp.arange(2, dtype=jnp.int32)
-    row_order = lax.dynamic_slice_in_dim(order, 2 * row, 2)
-    col_order = lax.dynamic_slice_in_dim(order, col, 1)
-    keep = ((row_order > col_order) | (places == col)).astype(jnp.float32)
-    return update(place_of(0), keep, cov, col_cross, inverse, pieces)
+    return update(place_of(0), order, cov, col_cross, inverse, pieces)
 
 
 def solution(mesh):

time: 129 us -> 128 us (level)
  waiting for transfers between devices: 39.7 us -> 36.9 us
  blocking collectives: 22.4 us -> 23.9 us
  starting transfers between devices: 43.4 us -> 44.8 us
    ppermute x3, waiting for transfers between devices: 8.8 us -> 6.03 us  [body(): lax.ppermute(near_rows, 'x', [(x, (x + away) % x_size) for x in range(x_s...]
    all_gather x1, blocking collectives: 2.3 us -> 3.76 us  [body(): col_cross = lax.all_gather(col_cross, 'k')]
  transfers between devices with their start and end apart: 8 -> 8, of which waited for: 5 -> 6; matrix products, arithmetic and copies ran while one was open for 2% -> 1% of each run, Pallas kernels for 4% -> 4%
where the time goes in v7:
time: 128 us; the launch traced here: 126 us
  starting transfers between devices  44.8 us (35%)
  waiting for transfers between devices  36.9 us (29%)
  blocking collectives  23.9 us (19%)
  Pallas kernels  17.6 us (14%)
  local copies, waits for them, and re-layouts  2.22 us (2%)
    all_to_all x4, starting transfers between devices, exchange(): return lax.all_to_all(array, axes, 0, 0, tiled=True)  32.3 us
    all_to_all x4, waiting for transfers between devices, exchange(): return lax.all_to_all(array, axes, 0, 0, tiled=True)  24.3 us
    all_to_all x1, blocking collectives, exchange(): return lax.all_to_all(array, axes, 0, 0, tiled=True)  14.3 us
    ppermute x3, starting transfers between devices, body(): lax.ppermute(near_rows, 'x', [(x, (x + away) % x_size) for x in range(x_s...  8.45 us
    ppermute x1, waiting for transfers between devices, body(): moved = lax.ppermute(own[:8 * GROUPS], ALL, moves)  6.52 us
    ppermute x3, waiting for transfers between devices, body(): lax.ppermute(near_rows, 'x', [(x, (x + away) % x_size) for x in range(x_s...  6.03 us
    all_gather x1, blocking collectives, body(): lax.all_gather(exchange(packed, TC), 'k')  5.82 us
    pallas_call x1, Pallas kernels, invert(): pl.pallas_call(inverse_kernel, out_shape=jax.ShapeDtypeStruct((nobs, nobs...  4.82 us
  transfers between devices with their start and end apart: 8, of which 6 were waited for; matrix products, arithmetic and copies ran while one was open for 1% of the time, Pallas kernels for 4%

profile of v7, /device:TPU:1, one launch (start us, length us, event | category | flops | bytes accessed | tf_op | source)
XLA Modules:
  0.0 126.2 jit_solution(14988236768703456409)
XLA Ops:
  0.0 1.6 %shard_map.55 = f32[32,8,384]{2,1,0:T(8,128)} custom-call(s32[1]{0:T(128)} %bitcast.7.core, s32[1,8]{1,0:T(1,128)} %stations_at.1, f32[1,8]{1,0:T(1,128)} %errors_at.1, f32[8,512]{1,0:T(8,128)} %bitcast.26), custom_call_target="tpu_custom_call" | custom-call | tf_op jit(solution)/shard_map/pallas_call | solution.py:102
  1.6 0.0 copy-start.1
  1.6 10.6 %all-to-all-start.2 = ((f32[32,8,384]{2,1,0:T(8,128)}), f32[32,8,384]{2,1,0:T(8,128)S(1)}, u32[]{:S(2)}, u32[]{:S(2)}) async-start(f32[32,8,384]{2,1,0:T(8,128)} %shard_map.55), calls=%async_computation.2 | async-start | bytes 786432 | tf_op jit(solution)/shard_map/all_to_all | solution.py:63
  12.3 0.7 copy.7.order_column
  13.0 0.1 pad_add_fusion.1.where
  13.1 10.8 %all-to-all-done.2 = f32[32,8,384]{2,1,0:T(8,128)S(1)} async-done(((f32[32,8,384]{2,1,0:T(8,128)}), f32[32,8,384]{2,1,0:T(8,128)S(1)}, u32[]{:S(2)}, u32[]{:S(2)}) %all-to-all-start.2) | async-done | bytes 393248 | tf_op jit(solution)/shard_map/all_to_all | solution.py:63
  23.9 5.8 %all-gather = f32[64,8,384]{2,1,0:T(8,128)S(1)} all-gather(f32[32,8,384]{2,1,0:T(8,128)S(1)} %all-to-all-done.2), channel_id=2, replica_groups=mesh['z'=8,'k'=2,'x'=4,'yh'=4,'yl'=2] {'k'}, dimensions={0}, use_global_device_ids=true | all-gather | bytes 1179648 | tf_op jit(solution)/shard_map/all_gather | solution.py:426
  29.7 1.1 shard_map.56
  30.8 3.3 %shard_map.57 = f32[32,16,128]{2,1,0:T(8,128)S(1)} custom-call(s32[4]{0:T(128)S(1)} %pad_add_fusion.1.where, f32[2,256,384]{2,1,0:T(8,128)S(1)} %bitcast.24, s32[8,256]{1,0:T(8,128)S(1)} %get-tuple-element.143.codes, f32[1024,512]{1,0:T(8,128)S(1)} %copy-done.1), custom_call_target="tpu_custom_call" | custom-call | tf_op jit(solution)/shard_map/pallas_call | solution.py:208
  34.1 14.3 %all_to_all.37.arrived = f32[32,16,128]{2,1,0:T(8,128)S(1)} all-to-all(f32[32,16,128]{2,1,0:T(8,128)S(1)} %shard_map.57), channel_id=1, replica_groups=mesh['z'=8,'k'=2,'x'=4,'yh'=4,'yl'=2] {'x','yh','yl'}, dimensions={0} | all-to-all | bytes 524288 | tf_op jit(solution)/shard_map/all_to_all | solution.py:63
  48.4 1.7 %shard_map.58 = (f32[32,256]{1,0:T(8,128)S(1)}, f32[16,3,8,128]{3,2,1,0:T(8,128)}) custom-call(s32[4]{0:T(128)S(1)} %pad_add_fusion.1.where, s32[8,256]{1,0:T(8,128)S(1)} %get-tuple-element.143.codes, f32[32,16,128]{2,1,0:T(8,128)S(1)} %all_to_all.37.arrived), custom_call_target="tpu_custom_call" | custom-call | tf_op jit(solution)/shard_map/pallas_call | solution.py:247
  50.2 14.0 %all-to-all-start.4 = ((f32[16,3,8,128]{3,2,1,0:T(8,128)}), f32[16,3,8,128]{3,2,1,0:T(8,128)S(1)}, u32[]{:S(2)}, u32[]{:S(2)}) async-start(f32[16,3,8,128]{3,2,1,0:T(8,128)} %get-tuple-element.60), calls=%async_computation.4 | async-start | bytes 393216 | tf_op jit(solution)/shard_map/all_to_all | solution.py:63
  64.2 10.3 %all-to-all-done.4.arrived = f32[16,3,8,128]{3,2,1,0:T(8,128)S(1)} async-done(((f32[16,3,8,128]{3,2,1,0:T(8,128)}), f32[16,3,8,128]{3,2,1,0:T(8,128)S(1)}, u32[]{:S(2)}, u32[]{:S(2)}) %all-to-all-start.4) | async-done | bytes 196640 | tf_op jit(solution)/shard_map/all_to_all | solution.py:63
  74.5 1.4 %shard_map.59 = f32[40,256]{1,0:T(8,128)S(1)} custom-call(s32[4]{0:T(128)S(1)} %pad_add_fusion.1.where, s32[8,256]{1,0:T(8,128)S(1)} %get-tuple-element.143.codes, f32[32,256]{1,0:T(8,128)S(1)} %get-tuple-element.59.placed, f32[16,3,8,128]{3,2,1,0:T(8,128)S(1)} %all-to-all-done.4.arrived), custom_call_target="tpu_custom_call" | custom-call | tf_op jit(solution)/shard_map/pallas_call | solution.py:284
  75.9 0.6 while.10
  76.5 0.7 broadcast_in_dim.4
  77.2 3.4 %all-to-all-start.5 = ((f32[8,40,256]{2,1,0:T(8,128)}), f32[8,40,256]{2,1,0:T(8,128)S(1)}, u32[]{:S(2)}, u32[]{:S(2)}) async-start(f32[8,40,256]{2,1,0:T(8,128)} %broadcast_in_dim.4), calls=%async_computation.5 | async-start | bytes 655360 | tf_op jit(solution)/shard_map/all_to_all | solution.py:63
  80.7 4.0 %collective-permute-start = (f32[32,256]{1,0:T(8,128)S(1)}, f32[32,256]{1,0:T(8,128)S(1)}, u32[]{:S(2)}, u32[]{:S(2)}) collective-permute-start(f32[32,256]{1,0:T(8,128)S(1)} %slice.3), channel_id=1, source_target_pairs={{0,0},{1,32},{2,64},{3,96},{4,128},{5,160},{6,192},{7,224},{8,256}... | collective-permute-start | bytes 98312 | tf_op jit(solution)/shard_map/ppermute | solution.py:446
  84.7 6.5 %collective-permute-done = f32[32,256]{1,0:T(8,128)S(1)} collective-permute-done((f32[32,256]{1,0:T(8,128)S(1)}, f32[32,256]{1,0:T(8,128)S(1)}, u32[]{:S(2)}, u32[]{:S(2)}) %collective-permute-start) | collective-permute-done | bytes 32800 | tf_op jit(solution)/shard_map/ppermute | solution.py:446
  91.2 3.2 %all-to-all-done.5.refs_0_ = f32[8,40,256]{2,1,0:T(8,128)S(1)} async-done(((f32[8,40,256]{2,1,0:T(8,128)}), f32[8,40,256]{2,1,0:T(8,128)S(1)}, u32[]{:S(2)}, u32[]{:S(2)}) %all-to-all-start.5) | async-done | bytes 327712 | tf_op jit(solution)/shard_map/all_to_all | solution.py:63
  94.4 2.4 %collective-permute-start.3 = (f32[8,40,256]{2,1,0:T(8,128)S(1)}, f32[8,40,256]{2,1,0:T(8,128)S(1)}, u32[]{:S(2)}, u32[]{:S(2)}) collective-permute-start(f32[8,40,256]{2,1,0:T(8,128)S(1)} %all-to-all-done.5.refs_0_), channel_id=1, source_target_pairs={{0,16},{8,24},{16,0},{24,8},{1,17},{9,25},{17,1},{25,9},{2,18},{10... | collective-permute-start | bytes 983048 | tf_op jit(solution)/shard_map/ppermute | solution.py:451
  96.8 4.2 %collective-permute-start.2 = (f32[8,40,256]{2,1,0:T(8,128)S(1)}, f32[8,40,256]{2,1,0:T(8,128)S(1)}, u32[]{:S(2)}, u32[]{:S(2)}) collective-permute-start(f32[8,40,256]{2,1,0:T(8,128)S(1)} %all-to-all-done.5.refs_0_), channel_id=1, source_target_pairs={{0,24},{8,0},{16,8},{24,16},{1,25},{9,1},{17,9},{25,17},{2,26},{10... | collective-permute-start | bytes 983048 | tf_op jit(solution)/shard_map/ppermute | solution.py:451
  101.0 1.9 %collective-permute-start.1 = (f32[8,40,256]{2,1,0:T(8,128)S(1)}, f32[8,40,256]{2,1,0:T(8,128)S(1)}, u32[]{:S(2)}, u32[]{:S(2)}) collective-permute-start(f32[8,40,256]{2,1,0:T(8,128)S(1)} %all-to-all-done.5.refs_0_), channel_id=1, source_target_pairs={{0,8},{8,16},{16,24},{24,0},{1,9},{9,17},{17,25},{25,1},{2,10},{10... | collective-permute-start | bytes 983048 | tf_op jit(solution)/shard_map/ppermute | solution.py:451
  102.9 0.7 broadcast_in_dim.5
  103.6 4.2 %all-to-all-start.6 = ((f32[8,32,256]{2,1,0:T(8,128)}), f32[8,32,256]{2,1,0:T(8,128)S(1)}, u32[]{:S(2)}, u32[]{:S(2)}) async-start(f32[8,32,256]{2,1,0:T(8,128)} %broadcast_in_dim.5), calls=%async_computation.6 | async-start | bytes 524288 | tf_op jit(solution)/shard_map/all_to_all | solution.py:63
  107.8 0.0 collective-permute-done.3.refs_3_
  107.8 3.4 %collective-permute-done.2.refs_2_ = f32[8,40,256]{2,1,0:T(8,128)S(1)} collective-permute-done((f32[8,40,256]{2,1,0:T(8,128)S(1)}, f32[8,40,256]{2,1,0:T(8,128)S(1)}, u32[]{:S(2)}, u32[]{:S(2)}) %collective-permute-start.2) | collective-permute-done | bytes 327712 | tf_op jit(solution)/shard_map/ppermute | solution.py:451
  111.2 2.6 %collective-permute-done.1.refs_1_ = f32[8,40,256]{2,1,0:T(8,128)S(1)} collective-permute-done((f32[8,40,256]{2,1,0:T(8,128)S(1)}, f32[8,40,256]{2,1,0:T(8,128)S(1)}, u32[]{:S(2)}, u32[]{:S(2)}) %collective-permute-start.1) | collective-permute-done | bytes 327712 | tf_op jit(solution)/shard_map/ppermute | solution.py:451
  113.8 4.8 %shard_map.60.inverse = f32[256,256]{1,0:T(8,128)S(1)} custom-call(s32[4]{0:T(128)S(1)} %pad_add_fusion.1.where, f32[2,256,384]{2,1,0:T(8,128)S(1)} %get-tuple-element.177, s32[8,256]{1,0:T(8,128)S(1)} %get-tuple-element.178, f32[8,40,256]{2,1,0:T(8,128)S(1)} %all-to-all-done.5.refs_0_, f32[8,40,256]{2,1,0:T(8,128)S(1)} %collective-permute-done.1.refs_1_, ...), custom_call_target="tpu_custom_call" | custom-call | flops 25165824000 | bytes 524288 | tf_op jit(solution)/shard_map/pallas_call | solution.py:362
  118.6 0.0 all-to-all-done.6
  118.7 3.8 %all-gather.1 = f32[16,32,256]{2,1,0:T(8,128)S(1)} all-gather(f32[8,32,256]{2,1,0:T(8,128)S(1)} %all-to-all-done.6), channel_id=3, replica_groups=mesh['z'=8,'k'=2,'x'=4,'yh'=4,'yl'=2] {'k'}, dimensions={0}, use_global_device_ids=true | all-gather | bytes 786432 | tf_op jit(solution)/shard_map/all_gather | solution.py:457
  122.4 3.8 %shard_map.61 = f32[1024,512]{1,0:T(8,128)} custom-call(s32[4]{0:T(128)S(1)} %pad_add_fusion.1.where, s32[32]{0:T(128)S(1)} %copy-done, f32[1024,512]{1,0:T(8,128)} %cov.3, f32[2,8,32,256]{3,2,1,0:T(8,128)S(1)} %bitcast.21, f32[256,256]{1,0:T(8,128)S(1)} %shard_map.60.inverse, f32[8,40,256]{2,1,0:T(8,128)S(1)} %all-to-all-done.5.refs_0_, ...), custom_call_target="tpu_custom_call" | custom-call | tf_op jit(solution)/shard_map/pallas_call | solution.py:403
  (4 shorter events, 0.0 us)
Async XLA Ops:
  1.6 29.2 %copy-start.1 = (f32[1024,512]{1,0:T(8,128)S(1)}, f32[1024,512]{1,0:T(8,128)}, u32[]{:S(2)}) copy-start(f32[1024,512]{1,0:T(8,128)} %cov.3) | copy-start | bytes 6291460
  1.6 22.3 %all-to-all-start.2 = ((f32[32,8,384]{2,1,0:T(8,128)}), f32[32,8,384]{2,1,0:T(8,128)S(1)}, u32[]{:S(2)}, u32[]{:S(2)}) async-start(f32[32,8,384]{2,1,0:T(8,128)} %shard_map.55), calls=%async_computation.2 | async-start | bytes 786432 | tf_op jit(solution)/shard_map/all_to_all | solution.py:63
  50.2 24.4 %all-to-all-start.4 = ((f32[16,3,8,128]{3,2,1,0:T(8,128)}), f32[16,3,8,128]{3,2,1,0:T(8,128)S(1)}, u32[]{:S(2)}, u32[]{:S(2)}) async-start(f32[16,3,8,128]{3,2,1,0:T(8,128)} %get-tuple-element.60), calls=%async_computation.4 | async-start | bytes 393216 | tf_op jit(solution)/shard_map/all_to_all | solution.py:63
  77.2 17.2 %all-to-all-start.5 = ((f32[8,40,256]{2,1,0:T(8,128)}), f32[8,40,256]{2,1,0:T(8,128)S(1)}, u32[]{:S(2)}, u32[]{:S(2)}) async-start(f32[8,40,256]{2,1,0:T(8,128)} %broadcast_in_dim.4), calls=%async_computation.5 | async-start | bytes 655360 | tf_op jit(solution)/shard_map/all_to_all | solution.py:63
  80.7 10.6 %collective-permute-start = (f32[32,256]{1,0:T(8,128)S(1)}, f32[32,256]{1,0:T(8,128)S(1)}, u32[]{:S(2)}, u32[]{:S(2)}) collective-permute-start(f32[32,256]{1,0:T(8,128)S(1)} %slice.3), channel_id=1, source_target_pairs={{0,0},{1,32},{2,64},{3,96},{4,128},{5,160},{6,192},{7,224},{8,256}... | collective-permute-start | bytes 98312 | tf_op jit(solution)/shard_map/ppermute | solution.py:446
  94.4 13.4 %collective-permute-start.3 = (f32[8,40,256]{2,1,0:T(8,128)S(1)}, f32[8,40,256]{2,1,0:T(8,128)S(1)}, u32[]{:S(2)}, u32[]{:S(2)}) collective-permute-start(f32[8,40,256]{2,1,0:T(8,128)S(1)} %all-to-all-done.5.refs_0_), channel_id=1, source_target_pairs={{0,16},{8,24},{16,0},{24,8},{1,17},{9,25},{17,1},{25,9},{2,18},{10... | collective-permute-start | bytes 983048 | tf_op jit(solution)/shard_map/ppermute | solution.py:451
  96.8 14.4 %collective-permute-start.2 = (f32[8,40,256]{2,1,0:T(8,128)S(1)}, f32[8,40,256]{2,1,0:T(8,128)S(1)}, u32[]{:S(2)}, u32[]{:S(2)}) collective-permute-start(f32[8,40,256]{2,1,0:T(8,128)S(1)} %all-to-all-done.5.refs_0_), channel_id=1, source_target_pairs={{0,24},{8,0},{16,8},{24,16},{1,25},{9,1},{17,9},{25,17},{2,26},{10... | collective-permute-start | bytes 983048 | tf_op jit(solution)/shard_map/ppermute | solution.py:451
  101.0 12.9 %collective-permute-start.1 = (f32[8,40,256]{2,1,0:T(8,128)S(1)}, f32[8,40,256]{2,1,0:T(8,128)S(1)}, u32[]{:S(2)}, u32[]{:S(2)}) collective-permute-start(f32[8,40,256]{2,1,0:T(8,128)S(1)} %all-to-all-done.5.refs_0_), channel_id=1, source_target_pairs={{0,8},{8,16},{16,24},{24,0},{1,9},{9,17},{17,25},{25,1},{2,10},{10... | collective-permute-start | bytes 983048 | tf_op jit(solution)/shard_map/ppermute | solution.py:451
  103.6 15.0 %all-to-all-start.6 = ((f32[8,32,256]{2,1,0:T(8,128)}), f32[8,32,256]{2,1,0:T(8,128)S(1)}, u32[]{:S(2)}, u32[]{:S(2)}) async-start(f32[8,32,256]{2,1,0:T(8,128)} %broadcast_in_dim.5), calls=%async_computation.6 | async-start | bytes 524288 | tf_op jit(solution)/shard_map/all_to_all | solution.py:63
  107.8 14.6 %copy-start = (s32[32]{0:T(128)S(1)}, s32[32]{0:T(128)}, u32[]{:S(2)}) copy-start(s32[32]{0:T(128)} %order.1) | copy-start | bytes 388

commit v8 on v7

--- a/solution.py
+++ b/solution.py
@@ -271,19 +271,22 @@
     at = iota((pairs * LANES, nobs), 0)
     spot = at // LANES * PAIR_SLOTS + at % PAIR_SLOTS
     spots = (spot == pair_code).astype(jnp.bfloat16)
-    out[: 8 * GROUPS] = placed[...] + placing_dot(former, spots)
+    rows = placed[...] + placing_dot(former, spots)
+    for copy in range(out.shape[0]):
+        out[copy, : 8 * GROUPS] = rows
     for part in range(nobs // LANES):
         total = arrived[0, 1 + part]
         for r in range(1, pairs):
             total = total + arrived[r, 1 + part]
-        out[8 * GROUPS :, part * LANES : (part + 1) * LANES] = total
-
-
-def gather_rows(where, codes, placed, arrived):
+        for copy in range(out.shape[0]):
+            out[copy, 8 * GROUPS :, part * LANES : (part + 1) * LANES] = total
+
+
+def gather_rows(where, codes, placed, arrived, copies):
     nobs = codes.shape[1]
     return pl.pallas_call(
         gather_kernel,
-        out_shape=jax.ShapeDtypeStruct((8 * GROUPS + 8, nobs), jnp.float32),
+        out_shape=jax.ShapeDtypeStruct((copies, 8 * GROUPS + 8, nobs), jnp.float32),
         in_specs=[pl.BlockSpec(memory_space=pltpu.SMEM), *in_vmem(3)],
         out_specs=pl.BlockSpec(memory_space=pltpu.VMEM),
         compiler_params=params(),
@@ -418,6 +421,7 @@
     nobs_own = obs_values.shape[1]
     tr_size, tc_size = lax.axis_size(TR), lax.axis_size(TC)
     nobs = nobs_own * tc_size
+    y_size, x_size = lax.axis_size(Y), lax.axis_size("x")
     row = lax.axis_index(TR)
     col = lax.axis_index(TC)
 
@@ -434,7 +438,7 @@
         where = place_of(number)
         terms = exchange(make_terms(where, everything, codes, cov, tc_size), TC)
         placed, second = place_rows(where, codes, terms, tr_size)
-        return gather_rows(where, codes, placed, exchange(second, TR))
+        return gather_rows(where, codes, placed, exchange(second, TR), y_size)
 
     own = lax.fori_loop(1, rounds[0], lambda number, sofar: sofar + one_round(number), one_round(0))
 
@@ -443,9 +447,8 @@
         for r in range(tr_size)
         for c in range(tc_size)
     ]
-    moved = lax.ppermute(own[: 8 * GROUPS], ALL, moves)
-    y_size, x_size = lax.axis_size(Y), lax.axis_size("x")
-    near_rows = exchange(jnp.broadcast_to(own[None], (y_size, *own.shape)), Y)
+    moved = lax.ppermute(own[0, : 8 * GROUPS], ALL, moves)
+    near_rows = exchange(own, Y)
     moved, near_rows = lax.optimization_barrier((moved, near_rows))
     pieces = [near_rows] + [
         lax.ppermute(near_rows, "x", [(x, (x + away) % x_size) for x in range(x_size)])

time: 128 us -> 128 us (level)
  transfers between devices with their start and end apart: 8 -> 8, of which waited for: 6 -> 6; matrix products, arithmetic and copies ran while one was open for 1% -> 2% of each run, Pallas kernels for 4% -> 4%
where the time goes in v8:
time: 128 us; the launch traced here: 126 us
  starting transfers between devices  44.9 us (35%)
  waiting for transfers between devices  36 us (28%)
  blocking collectives  24 us (19%)
  Pallas kernels  18.4 us (14%)
  local copies, waits for them, and re-layouts  2.24 us (2%)
    all_to_all x4, starting transfers between devices, exchange(): return lax.all_to_all(array, axes, 0, 0, tiled=True)  32.4 us
    all_to_all x4, waiting for transfers between devices, exchange(): return lax.all_to_all(array, axes, 0, 0, tiled=True)  24.3 us
    all_to_all x1, blocking collectives, exchange(): return lax.all_to_all(array, axes, 0, 0, tiled=True)  14.3 us
    ppermute x3, starting transfers between devices, body(): lax.ppermute(near_rows, 'x', [(x, (x + away) % x_size) for x in range(x_s...  8.45 us
    ppermute x3, waiting for transfers between devices, body(): lax.ppermute(near_rows, 'x', [(x, (x + away) % x_size) for x in range(x_s...  5.91 us
    all_gather x1, blocking collectives, body(): lax.all_gather(exchange(packed, TC), 'k')  5.82 us
    ppermute x1, waiting for transfers between devices, body(): moved = lax.ppermute(own[0, :8 * GROUPS], ALL, moves)  5.73 us
    pallas_call x1, Pallas kernels, invert(): pl.pallas_call(inverse_kernel, out_shape=jax.ShapeDtypeStruct((nobs, nobs...  4.83 us
  transfers between devices with their start and end apart: 8, of which 6 were waited for; matrix products, arithmetic and copies ran while one was open for 2% of the time, Pallas kernels for 4%

profile of v8, /device:TPU:1, one launch (start us, length us, event | category | flops | bytes accessed | tf_op | source)
XLA Modules:
  0.0 126.3 jit_solution(14560753953409567437)
XLA Ops:
  0.0 1.6 %shard_map.55 = f32[32,8,384]{2,1,0:T(8,128)} custom-call(s32[1]{0:T(128)} %bitcast.7.core, s32[1,8]{1,0:T(1,128)} %stations_at.1, f32[1,8]{1,0:T(1,128)} %errors_at.1, f32[8,512]{1,0:T(8,128)} %bitcast.28), custom_call_target="tpu_custom_call" | custom-call | tf_op jit(solution)/shard_map/pallas_call | solution.py:102
  1.6 0.0 copy-start.1
  1.6 10.6 %all-to-all-start.2 = ((f32[32,8,384]{2,1,0:T(8,128)}), f32[32,8,384]{2,1,0:T(8,128)S(1)}, u32[]{:S(2)}, u32[]{:S(2)}) async-start(f32[32,8,384]{2,1,0:T(8,128)} %shard_map.55), calls=%async_computation.2 | async-start | bytes 786432 | tf_op jit(solution)/shard_map/all_to_all | solution.py:63
  12.3 0.7 copy.7.order_column
  13.0 0.1 pad_add_fusion.1.where
  13.1 10.8 %all-to-all-done.2 = f32[32,8,384]{2,1,0:T(8,128)S(1)} async-done(((f32[32,8,384]{2,1,0:T(8,128)}), f32[32,8,384]{2,1,0:T(8,128)S(1)}, u32[]{:S(2)}, u32[]{:S(2)}) %all-to-all-start.2) | async-done | bytes 393248 | tf_op jit(solution)/shard_map/all_to_all | solution.py:63
  23.9 5.8 %all-gather = f32[64,8,384]{2,1,0:T(8,128)S(1)} all-gather(f32[32,8,384]{2,1,0:T(8,128)S(1)} %all-to-all-done.2), channel_id=2, replica_groups=mesh['z'=8,'k'=2,'x'=4,'yh'=4,'yl'=2] {'k'}, dimensions={0}, use_global_device_ids=true | all-gather | bytes 1179648 | tf_op jit(solution)/shard_map/all_gather | solution.py:430
  29.7 1.1 shard_map.56
  30.8 3.3 %shard_map.57 = f32[32,16,128]{2,1,0:T(8,128)S(1)} custom-call(s32[4]{0:T(128)S(1)} %pad_add_fusion.1.where, f32[2,256,384]{2,1,0:T(8,128)S(1)} %bitcast.26, s32[8,256]{1,0:T(8,128)S(1)} %get-tuple-element.143.codes, f32[1024,512]{1,0:T(8,128)S(1)} %copy-done.1), custom_call_target="tpu_custom_call" | custom-call | tf_op jit(solution)/shard_map/pallas_call | solution.py:208
  34.1 14.3 %all_to_all.37.arrived = f32[32,16,128]{2,1,0:T(8,128)S(1)} all-to-all(f32[32,16,128]{2,1,0:T(8,128)S(1)} %shard_map.57), channel_id=1, replica_groups=mesh['z'=8,'k'=2,'x'=4,'yh'=4,'yl'=2] {'x','yh','yl'}, dimensions={0} | all-to-all | bytes 524288 | tf_op jit(solution)/shard_map/all_to_all | solution.py:63
  48.4 1.7 %shard_map.58 = (f32[32,256]{1,0:T(8,128)S(1)}, f32[16,3,8,128]{3,2,1,0:T(8,128)}) custom-call(s32[4]{0:T(128)S(1)} %pad_add_fusion.1.where, s32[8,256]{1,0:T(8,128)S(1)} %get-tuple-element.143.codes, f32[32,16,128]{2,1,0:T(8,128)S(1)} %all_to_all.37.arrived), custom_call_target="tpu_custom_call" | custom-call | tf_op jit(solution)/shard_map/pallas_call | solution.py:247
  50.2 14.0 %all-to-all-start.4 = ((f32[16,3,8,128]{3,2,1,0:T(8,128)}), f32[16,3,8,128]{3,2,1,0:T(8,128)S(1)}, u32[]{:S(2)}, u32[]{:S(2)}) async-start(f32[16,3,8,128]{3,2,1,0:T(8,128)} %get-tuple-element.60), calls=%async_computation.4 | async-start | bytes 393216 | tf_op jit(solution)/shard_map/all_to_all | solution.py:63
  64.2 10.3 %all-to-all-done.4.arrived = f32[16,3,8,128]{3,2,1,0:T(8,128)S(1)} async-done(((f32[16,3,8,128]{3,2,1,0:T(8,128)}), f32[16,3,8,128]{3,2,1,0:T(8,128)S(1)}, u32[]{:S(2)}, u32[]{:S(2)}) %all-to-all-start.4) | async-done | bytes 196640 | tf_op jit(solution)/shard_map/all_to_all | solution.py:63
  74.5 2.1 %shard_map.59 = f32[8,40,256]{2,1,0:T(8,128)} custom-call(s32[4]{0:T(128)S(1)} %pad_add_fusion.1.where, s32[8,256]{1,0:T(8,128)S(1)} %get-tuple-element.143.codes, f32[32,256]{1,0:T(8,128)S(1)} %get-tuple-element.59.placed, f32[16,3,8,128]{3,2,1,0:T(8,128)S(1)} %all-to-all-done.4.arrived), custom_call_target="tpu_custom_call" | custom-call | tf_op jit(solution)/shard_map/pallas_call | solution.py:287
  76.6 0.6 while.10
  77.2 3.4 %all-to-all-start.5 = ((f32[8,40,256]{2,1,0:T(8,128)}), f32[8,40,256]{2,1,0:T(8,128)S(1)}, u32[]{:S(2)}, u32[]{:S(2)}) async-start(f32[8,40,256]{2,1,0:T(8,128)} %get-tuple-element.62), calls=%async_computation.5 | async-start | bytes 655360 | tf_op jit(solution)/shard_map/all_to_all | solution.py:63
  80.6 0.8 slice_bitcast_fusion
  81.4 4.1 %collective-permute-start = (f32[32,256]{1,0:T(8,128)S(1)}, f32[32,256]{1,0:T(8,128)S(1)}, u32[]{:S(2)}, u32[]{:S(2)}) collective-permute-start(f32[32,256]{1,0:T(8,128)S(1)} %slice_bitcast_fusion), channel_id=1, source_target_pairs={{0,0},{1,32},{2,64},{3,96},{4,128},{5,160},{6,192},{7,224},{8,256}... | collective-permute-start | bytes 98312 | tf_op jit(solution)/shard_map/ppermute | solution.py:450
  85.5 5.7 %collective-permute-done = f32[32,256]{1,0:T(8,128)S(1)} collective-permute-done((f32[32,256]{1,0:T(8,128)S(1)}, f32[32,256]{1,0:T(8,128)S(1)}, u32[]{:S(2)}, u32[]{:S(2)}) %collective-permute-start) | collective-permute-done | bytes 32800 | tf_op jit(solution)/shard_map/ppermute | solution.py:450
  91.2 3.2 %all-to-all-done.5.refs_0_ = f32[8,40,256]{2,1,0:T(8,128)S(1)} async-done(((f32[8,40,256]{2,1,0:T(8,128)}), f32[8,40,256]{2,1,0:T(8,128)S(1)}, u32[]{:S(2)}, u32[]{:S(2)}) %all-to-all-start.5) | async-done | bytes 327712 | tf_op jit(solution)/shard_map/all_to_all | solution.py:63
  94.4 2.7 %collective-permute-start.3 = (f32[8,40,256]{2,1,0:T(8,128)S(1)}, f32[8,40,256]{2,1,0:T(8,128)S(1)}, u32[]{:S(2)}, u32[]{:S(2)}) collective-permute-start(f32[8,40,256]{2,1,0:T(8,128)S(1)} %all-to-all-done.5.refs_0_), channel_id=1, source_target_pairs={{0,16},{8,24},{16,0},{24,8},{1,17},{9,25},{17,1},{25,9},{2,18},{10... | collective-permute-start | bytes 983048 | tf_op jit(solution)/shard_map/ppermute | solution.py:454
  97.1 3.8 %collective-permute-start.2 = (f32[8,40,256]{2,1,0:T(8,128)S(1)}, f32[8,40,256]{2,1,0:T(8,128)S(1)}, u32[]{:S(2)}, u32[]{:S(2)}) collective-permute-start(f32[8,40,256]{2,1,0:T(8,128)S(1)} %all-to-all-done.5.refs_0_), channel_id=1, source_target_pairs={{0,24},{8,0},{16,8},{24,16},{1,25},{9,1},{17,9},{25,17},{2,26},{10... | collective-permute-start | bytes 983048 | tf_op jit(solution)/shard_map/ppermute | solution.py:454
  101.0 1.9 %collective-permute-start.1 = (f32[8,40,256]{2,1,0:T(8,128)S(1)}, f32[8,40,256]{2,1,0:T(8,128)S(1)}, u32[]{:S(2)}, u32[]{:S(2)}) collective-permute-start(f32[8,40,256]{2,1,0:T(8,128)S(1)} %all-to-all-done.5.refs_0_), channel_id=1, source_target_pairs={{0,8},{8,16},{16,24},{24,0},{1,9},{9,17},{17,25},{25,1},{2,10},{10... | collective-permute-start | bytes 983048 | tf_op jit(solution)/shard_map/ppermute | solution.py:454
  102.9 0.7 broadcast_in_dim.2
  103.6 4.3 %all-to-all-start.6 = ((f32[8,32,256]{2,1,0:T(8,128)}), f32[8,32,256]{2,1,0:T(8,128)S(1)}, u32[]{:S(2)}, u32[]{:S(2)}) async-start(f32[8,32,256]{2,1,0:T(8,128)} %broadcast_in_dim.2), calls=%async_computation.6 | async-start | bytes 524288 | tf_op jit(solution)/shard_map/all_to_all | solution.py:63
  107.9 0.0 collective-permute-done.3.refs_3_
  107.9 4.3 %collective-permute-done.2.refs_2_ = f32[8,40,256]{2,1,0:T(8,128)S(1)} collective-permute-done((f32[8,40,256]{2,1,0:T(8,128)S(1)}, f32[8,40,256]{2,1,0:T(8,128)S(1)}, u32[]{:S(2)}, u32[]{:S(2)}) %collective-permute-start.2) | collective-permute-done | bytes 327712 | tf_op jit(solution)/shard_map/ppermute | solution.py:454
  112.2 1.6 %collective-permute-done.1.refs_1_ = f32[8,40,256]{2,1,0:T(8,128)S(1)} collective-permute-done((f32[8,40,256]{2,1,0:T(8,128)S(1)}, f32[8,40,256]{2,1,0:T(8,128)S(1)}, u32[]{:S(2)}, u32[]{:S(2)}) %collective-permute-start.1) | collective-permute-done | bytes 327712 | tf_op jit(solution)/shard_map/ppermute | solution.py:454
  113.8 4.8 %shard_map.60.inverse = f32[256,256]{1,0:T(8,128)S(1)} custom-call(s32[4]{0:T(128)S(1)} %pad_add_fusion.1.where, f32[2,256,384]{2,1,0:T(8,128)S(1)} %get-tuple-element.177, s32[8,256]{1,0:T(8,128)S(1)} %get-tuple-element.178, f32[8,40,256]{2,1,0:T(8,128)S(1)} %all-to-all-done.5.refs_0_, f32[8,40,256]{2,1,0:T(8,128)S(1)} %collective-permute-done.1.refs_1_, ...), custom_call_target="tpu_custom_call" | custom-call | flops 25165824000 | bytes 524288 | tf_op jit(solution)/shard_map/pallas_call | solution.py:365
  118.7 0.0 all-to-all-done.6
  118.7 3.9 %all-gather.1 = f32[16,32,256]{2,1,0:T(8,128)S(1)} all-gather(f32[8,32,256]{2,1,0:T(8,128)S(1)} %all-to-all-done.6), channel_id=3, replica_groups=mesh['z'=8,'k'=2,'x'=4,'yh'=4,'yl'=2] {'k'}, dimensions={0}, use_global_device_ids=true | all-gather | bytes 786432 | tf_op jit(solution)/shard_map/all_gather | solution.py:460
  122.5 3.8 %shard_map.61 = f32[1024,512]{1,0:T(8,128)} custom-call(s32[4]{0:T(128)S(1)} %pad_add_fusion.1.where, s32[32]{0:T(128)S(1)} %copy-done, f32[1024,512]{1,0:T(8,128)} %cov.3, f32[2,8,32,256]{3,2,1,0:T(8,128)S(1)} %bitcast.23, f32[256,256]{1,0:T(8,128)S(1)} %shard_map.60.inverse, f32[8,40,256]{2,1,0:T(8,128)S(1)} %all-to-all-done.5.refs_0_, ...), custom_call_target="tpu_custom_call" | custom-call | tf_op jit(solution)/shard_map/pallas_call | solution.py:406
  (3 shorter events, 0.0 us)
Async XLA Ops:
  1.6 29.2 %copy-start.1 = (f32[1024,512]{1,0:T(8,128)S(1)}, f32[1024,512]{1,0:T(8,128)}, u32[]{:S(2)}) copy-start(f32[1024,512]{1,0:T(8,128)} %cov.3) | copy-start | bytes 6291460
  1.6 22.3 %all-to-all-start.2 = ((f32[32,8,384]{2,1,0:T(8,128)}), f32[32,8,384]{2,1,0:T(8,128)S(1)}, u32[]{:S(2)}, u32[]{:S(2)}) async-start(f32[32,8,384]{2,1,0:T(8,128)} %shard_map.55), calls=%async_computation.2 | async-start | bytes 786432 | tf_op jit(solution)/shard_map/all_to_all | solution.py:63
  50.2 24.4 %all-to-all-start.4 = ((f32[16,3,8,128]{3,2,1,0:T(8,128)}), f32[16,3,8,128]{3,2,1,0:T(8,128)S(1)}, u32[]{:S(2)}, u32[]{:S(2)}) async-start(f32[16,3,8,128]{3,2,1,0:T(8,128)} %get-tuple-element.60), calls=%async_computation.4 | async-start | bytes 393216 | tf_op jit(solution)/shard_map/all_to_all | solution.py:63
  77.2 17.2 %all-to-all-start.5 = ((f32[8,40,256]{2,1,0:T(8,128)}), f32[8,40,256]{2,1,0:T(8,128)S(1)}, u32[]{:S(2)}, u32[]{:S(2)}) async-start(f32[8,40,256]{2,1,0:T(8,128)} %get-tuple-element.62), calls=%async_computation.5 | async-start | bytes 655360 | tf_op jit(solution)/shard_map/all_to_all | solution.py:63
  81.4 9.8 %collective-permute-start = (f32[32,256]{1,0:T(8,128)S(1)}, f32[32,256]{1,0:T(8,128)S(1)}, u32[]{:S(2)}, u32[]{:S(2)}) collective-permute-start(f32[32,256]{1,0:T(8,128)S(1)} %slice_bitcast_fusion), channel_id=1, source_target_pairs={{0,0},{1,32},{2,64},{3,96},{4,128},{5,160},{6,192},{7,224},{8,256}... | collective-permute-start | bytes 98312 | tf_op jit(solution)/shard_map/ppermute | solution.py:450
  94.4 13.5 %collective-permute-start.3 = (f32[8,40,256]{2,1,0:T(8,128)S(1)}, f32[8,40,256]{2,1,0:T(8,128)S(1)}, u32[]{:S(2)}, u32[]{:S(2)}) collective-permute-start(f32[8,40,256]{2,1,0:T(8,128)S(1)} %all-to-all-done.5.refs_0_), channel_id=1, source_target_pairs={{0,16},{8,24},{16,0},{24,8},{1,17},{9,25},{17,1},{25,9},{2,18},{10... | collective-permute-start | bytes 983048 | tf_op jit(solution)/shard_map/ppermute | solution.py:454
  97.1 15.1 %collective-permute-start.2 = (f32[8,40,256]{2,1,0:T(8,128)S(1)}, f32[8,40,256]{2,1,0:T(8,128)S(1)}, u32[]{:S(2)}, u32[]{:S(2)}) collective-permute-start(f32[8,40,256]{2,1,0:T(8,128)S(1)} %all-to-all-done.5.refs_0_), channel_id=1, source_target_pairs={{0,24},{8,0},{16,8},{24,16},{1,25},{9,1},{17,9},{25,17},{2,26},{10... | collective-permute-start | bytes 983048 | tf_op jit(solution)/shard_map/ppermute | solution.py:454
  101.0 12.9 %collective-permute-start.1 = (f32[8,40,256]{2,1,0:T(8,128)S(1)}, f32[8,40,256]{2,1,0:T(8,128)S(1)}, u32[]{:S(2)}, u32[]{:S(2)}) collective-permute-start(f32[8,40,256]{2,1,0:T(8,128)S(1)} %all-to-all-done.5.refs_0_), channel_id=1, source_target_pairs={{0,8},{8,16},{16,24},{24,0},{1,9},{9,17},{17,25},{25,1},{2,10},{10... | collective-permute-start | bytes 983048 | tf_op jit(solution)/shard_map/ppermute | solution.py:454
  103.6 15.0 %all-to-all-start.6 = ((f32[8,32,256]{2,1,0:T(8,128)}), f32[8,32,256]{2,1,0:T(8,128)S(1)}, u32[]{:S(2)}, u32[]{:S(2)}) async-start(f32[8,32,256]{2,1,0:T(8,128)} %broadcast_in_dim.2), calls=%async_computation.6 | async-start | bytes 524288 | tf_op jit(solution)/shard_map/all_to_all | solution.py:63
  107.9 14.6 %copy-start = (s32[32]{0:T(128)S(1)}, s32[32]{0:T(128)}, u32[]{:S(2)}) copy-start(s32[32]{0:T(128)} %order.1) | copy-start | bytes 388
